TPU v7x, 32 devices: a whole 2x2x4 slice. The times are simulated.
32 devices in a mesh: az: 16 (over z, x, core), rad: 2 (over y).
Axes of the slice: x: 2, y: 2, z: 4, core: 2. Of those that a mesh axis runs over, the one named last changes fastest.
Arguments:
- pressure: float32 [2, 256, 192, 128], P(None, 'az', 'rad'), may hold values from -6 to 6
- source: float32 [2, 256, 192, 128], P(None, 'az', 'rad'), may hold values from -6 to 6
- diagonal: float32 [2, 256, 192, 128], P(None, 'az', 'rad'), may hold values from 0.5 to 8
- rot_offset: int32 [1], replicated, may hold values from 0 to 255
Outputs:
- corrected: float32 [2, 256, 192, 128], P(None, 'az', 'rad')
All inputs are finite; a program needn't handle non-finite values.
Results may differ from a plain program's by a relative error of at most 0.00002.
Values sent between devices are 32-bit elements; how exact they have to be, the bound alone decides.
No kernel may reach another device: no remote copies, remote signals or barrier semaphores. Data moves between devices by JAX's collectives and lax.ppermute only.
A program may use at most 64 MiB of HBM per device.

v0:
```python
import jax
import jax.numpy as jnp
from jax import lax
from jax.sharding import PartitionSpec as P

STEPS = 2
SWEEPS = 4


OMEGA = 0.8


def swapped(array, axis, bit):
    return lax.ppermute(array, axis, [(i, i ^ 1 << bit) for i in range(lax.axis_size(axis))])


def with_halo(array, sides, width):
    for axis, dim in sides:
        size, length = (lax.axis_size(axis), array.shape[dim])
        up = [(i, (i + 1) % size) for i in range(size)]
        down = [(j, i) for i, j in up]
        last = lax.slice_in_dim(array, length - width, length, axis=dim)
        first = lax.slice_in_dim(array, 0, width, axis=dim)
        before = lax.ppermute(last, axis, up)
        after = lax.ppermute(first, axis, down)
        array = jnp.concatenate([before, array, after], axis=dim)
    return array


def relax_once(
    padded, ghost_cycle, source, diagonal, margin, radial_index, radial_count, radial_cells
):
    low_row = margin - 1
    high_row = margin + radial_cells
    low_value = jnp.stack([padded[0, :, margin, :], ghost_cycle])
    high_value = jnp.stack([ghost_cycle, padded[1, :, high_row - 1, :]])
    low_value = jnp.where(radial_index == 0, low_value, padded[:, :, low_row, :])
    high_value = jnp.where(radial_index == radial_count - 1, high_value, padded[:, :, high_row, :])
    padded = padded.at[:, :, low_row, :].set(low_value).at[:, :, high_row, :].set(high_value)
    center_cells = padded[:, 1:-1, 1:-1, :]
    radial = padded[:, 1:-1, 2:, :] + padded[:, 1:-1, :-2, :]
    beside_all = padded[:, 2:, 1:-1, :] + padded[:, :-2, 1:-1, :]
    axial_pad = jnp.pad(center_cells, ((0, 0), (0, 0), (0, 0), (1, 1)))
    axial_sum = axial_pad[..., 2:] + axial_pad[..., :-2]
    center = 6.0 + diagonal
    misfit = source - (center * center_cells - (radial + beside_all + axial_sum))
    return center_cells + OMEGA * misfit / center


def per_device(pressure, source, diagonal, rot_offset):
    sector_cells = pressure.shape[1]
    radial_cells = pressure.shape[2]
    cycle_length = sector_cells * lax.axis_size("az")
    radial_count = lax.axis_size("rad")
    radial_index = lax.axis_index("rad")
    sector_start = lax.axis_index("az") * sector_cells
    for time_step in range(STEPS):
        offset = rot_offset[0] * (time_step + 1) % cycle_length
        edge_cycle = jnp.where(
            radial_index == 0, pressure[1, :, 0, :], pressure[0, :, radial_cells - 1, :]
        )
        facing = swapped(edge_cycle, "rad", 0)
        amount = jnp.where(radial_index == 0, offset, (cycle_length - offset) % cycle_length)
        whole_cycle = lax.all_gather(facing, "az", axis=0, tiled=True)
        doubled = jnp.concatenate([whole_cycle, whole_cycle[:sector_cells]], axis=0)
        slice_start = (sector_start - amount) % cycle_length
        aligned = lax.dynamic_slice_in_dim(doubled, slice_start, sector_cells, 0)
        ghost_cycle = jnp.pad(aligned, ((1, 1), (0, 0)))
        for sweep_number in range(SWEEPS):
            padded = with_halo(pressure, (("az", 1), ("rad", 2)), 1)
            pressure = relax_once(
                padded, ghost_cycle, source, diagonal, 1, radial_index, radial_count, radial_cells
            )
    return pressure


def solution(mesh):
    placed = (
        P(None, "az", "rad", None),
        P(None, "az", "rad", None),
        P(None, "az", "rad", None),
        P(),
    )
    return jax.shard_map(
        per_device,
        mesh=mesh,
        in_specs=placed,
        out_specs=P(None, "az", "rad", None),
        check_vma=False,
    )
```

profile of v0, /device:TPU:0, one launch (start us, length us, event | category | flops | bytes accessed | tf_op | source)
XLA Modules:
  0.0 167.9 jit_solution(420480368676721883)
XLA Ops:
  0.0 2.3 %copy.36 = f32[2,16,96,128]{3,1,2,0:T(8,128)S(1)} copy(f32[2,16,96,128]{3,2,1,0:T(8,128)} %param.36) | data formatting | bytes 3145728 | tf_op args[0]
  2.3 3.0 %collective-permute-start.4 = (f32[16,128]{1,0:T(8,128)S(1)}, f32[16,128]{1,0:T(8,128)S(1)}, u32[]{:S(2)}, u32[]{:S(2)}) collective-permute-start(f32[16,128]{1,0:T(8,128)S(1)} %fusion.99), channel_id=1, source_target_pairs={{0,1},{1,0},{2,3},{3,2},{4,5},{5,4},{6,7},{7,6},{8,9},{9,8},{10,11... | collective-permute-start | bytes 24584 | tf_op jit(solution)/shard_map/ppermute | solution.py:14
  6.4 4.4 %collective-permute-start.1 = (f32[2,1,96,128]{3,1,2,0:T(1,128)S(1)}, f32[2,1,96,128]{3,1,2,0:T(1,128)S(1)}, u32[]{:S(2)}, u32[]{:S(2)}) collective-permute-start(f32[2,1,96,128]{3,1,2,0:T(1,128)S(1)} %bitcast.15), channel_id=1, source_target_pairs={{2,0},{4,2},{6,4},{8,6},{10,8},{12,10},{14,12},{16,14},{18,16},{20... | collective-permute-start | bytes 294920 | tf_op jit(solution)/shard_map/ppermute | solution.py:25
  11.5 19.3 %all_gather.6 = f32[256,128]{1,0:T(8,128)S(1)} all-gather(f32[16,128]{1,0:T(8,128)S(1)} %collective-permute-done.4), channel_id=1, replica_groups=mesh['az'=16,'rad'=2] {'az'}, dimensions={0}, use_global_device_ids=true | all-gather | bytes 139264 | tf_op jit(solution)/shard_map/all_gather | solution.py:64
  37.6 3.0 %fusion.6 = f32[2,16,96,128]{3,1,2,0:T(8,128)S(1)} fusion(f32[2,16,96,128]{3,1,2,0:T(8,128)S(1)} %slice.843, f32[2,18,98,128]{3,1,2,0:T(8,128)S(1)} %fusion.81, f32[2,16,96,128]{3,2,1,0:T(8,128)S(1)} %copy-done, f32[2,16,96,128]{3,2,1,0:T(8,128)S(1)} %copy-done.1), kind=kLoop, calls=%fused_computation.30 | loop fusion | flops 4718592 | bytes 12582912 | tf_op jit(solution)/shard_map/add | solution.py:47
  42.9 4.6 %collective-permute-done.5 = f32[2,1,96,128]{3,1,2,0:T(1,128)S(1)} collective-permute-done((f32[2,1,96,128]{3,1,2,0:T(1,128)S(1)}, f32[2,1,96,128]{3,1,2,0:T(1,128)S(1)}, u32[]{:S(2)}, u32[]{:S(2)}) %collective-permute-start.5) | collective-permute-done | bytes 98336 | tf_op jit(solution)/shard_map/ppermute | solution.py:24
  49.6 1.8 %collective-permute-done.7 = f32[2,18,1,128]{3,1,2,0:T(8,128)S(1)} collective-permute-done((f32[2,18,1,128]{3,1,2,0:T(8,128)S(1)}, f32[2,18,1,128]{3,1,2,0:T(8,128)S(1)}, u32[]{:S(2)}, u32[]{:S(2)}) %collective-permute-start.7) | collective-permute-done | bytes 18464 | tf_op jit(solution)/shard_map/ppermute | solution.py:24
  53.5 3.0 %fusion.13 = f32[2,16,96,128]{3,1,2,0:T(8,128)S(1)} fusion(f32[2,16,96,128]{3,1,2,0:T(8,128)S(1)} %slice.850, f32[2,18,98,128]{3,1,2,0:T(8,128)S(1)} %fusion.83, f32[2,16,96,128]{3,2,1,0:T(8,128)S(1)} %copy-done, f32[2,16,96,128]{3,2,1,0:T(8,128)S(1)} %copy-done.1), kind=kLoop, calls=%fused_computation.37 | loop fusion | flops 4718592 | bytes 12582912 | tf_op jit(solution)/shard_map/add | solution.py:47
  58.9 4.8 %collective-permute-done.9 = f32[2,1,96,128]{3,1,2,0:T(1,128)S(1)} collective-permute-done((f32[2,1,96,128]{3,1,2,0:T(1,128)S(1)}, f32[2,1,96,128]{3,1,2,0:T(1,128)S(1)}, u32[]{:S(2)}, u32[]{:S(2)}) %collective-permute-start.9) | collective-permute-done | bytes 98336 | tf_op jit(solution)/shard_map/ppermute | solution.py:24
  68.6 3.0 %fusion.20 = f32[2,16,96,128]{3,1,2,0:T(8,128)S(1)} fusion(f32[2,16,96,128]{3,1,2,0:T(8,128)S(1)} %slice.857, f32[2,18,98,128]{3,1,2,0:T(8,128)S(1)} %fusion.85, f32[2,16,96,128]{3,2,1,0:T(8,128)S(1)} %copy-done, f32[2,16,96,128]{3,2,1,0:T(8,128)S(1)} %copy-done.1), kind=kLoop, calls=%fused_computation.44 | loop fusion | flops 4718592 | bytes 12582912 | tf_op jit(solution)/shard_map/add | solution.py:47
  74.0 4.6 %collective-permute-done.13 = f32[2,1,96,128]{3,1,2,0:T(1,128)S(1)} collective-permute-done((f32[2,1,96,128]{3,1,2,0:T(1,128)S(1)}, f32[2,1,96,128]{3,1,2,0:T(1,128)S(1)}, u32[]{:S(2)}, u32[]{:S(2)}) %collective-permute-start.13) | collective-permute-done | bytes 98336 | tf_op jit(solution)/shard_map/ppermute | solution.py:24
  81.3 2.0 %collective-permute-done.15 = f32[2,18,1,128]{3,1,2,0:T(8,128)S(1)} collective-permute-done((f32[2,18,1,128]{3,1,2,0:T(8,128)}, f32[2,18,1,128]{3,1,2,0:T(8,128)S(1)}, u32[]{:S(2)}, u32[]{:S(2)}) %collective-permute-start.15) | collective-permute-done | bytes 18464 | tf_op jit(solution)/shard_map/ppermute | solution.py:24
  84.8 1.8 %pad_maximum_fusion.3 = f32[2,18,98,128]{3,1,2,0:T(8,128)S(1)} fusion(f32[2,18,1,128]{3,1,2,0:T(8,128)S(1)} %collective-permute-done.16, f32[2,1,96,128]{3,1,2,0:T(1,128)S(1)} %collective-permute-done.14, f32[2,16,96,128]{3,1,2,0:T(8,128)} %copy-done.2, f32[2,1,96,128]{3,1,2,0:T(1,128)S(1)} %collective-permute-done.13, ...), kind=kLoop, calls=%fused_computation.19 | loop fusion | flops 1806336 | bytes 3612672 | tf_op jit(solution)/shard_map/concatenate | solution.py:26
  86.8 3.0 %fusion.27 = f32[2,16,96,128]{3,1,2,0:T(8,128)S(1)} fusion(f32[2,16,96,128]{3,1,2,0:T(8,128)S(1)} %slice.864, f32[2,18,98,128]{3,1,2,0:T(8,128)S(1)} %fusion.87, f32[2,16,96,128]{3,2,1,0:T(8,128)S(1)} %copy-done, f32[2,16,96,128]{3,2,1,0:T(8,128)S(1)} %copy-done.1), kind=kLoop, calls=%fused_computation.51 | loop fusion | flops 4718592 | bytes 12582912 | tf_op jit(solution)/shard_map/add | solution.py:47
  91.1 2.4 %collective-permute-done.21 = f32[16,128]{1,0:T(8,128)S(1)} collective-permute-done((f32[16,128]{1,0:T(8,128)S(1)}, f32[16,128]{1,0:T(8,128)S(1)}, u32[]{:S(2)}, u32[]{:S(2)}) %collective-permute-start.21) | collective-permute-done | bytes 8224 | tf_op jit(solution)/shard_map/ppermute | solution.py:14
  93.5 17.5 %all_gather.7 = f32[256,128]{1,0:T(8,128)S(1)} all-gather(f32[16,128]{1,0:T(8,128)S(1)} %collective-permute-done.21), channel_id=1, replica_groups=mesh['az'=16,'rad'=2] {'az'}, dimensions={0}, use_global_device_ids=true | all-gather | bytes 139264 | tf_op jit(solution)/shard_map/all_gather | solution.py:64
  116.0 3.0 %fusion.34 = f32[2,16,96,128]{3,1,2,0:T(8,128)S(1)} fusion(f32[2,16,96,128]{3,1,2,0:T(8,128)S(1)} %slice.874, f32[2,18,98,128]{3,1,2,0:T(8,128)S(1)} %fusion.65, f32[2,16,96,128]{3,2,1,0:T(8,128)S(1)} %copy-done, f32[2,16,96,128]{3,2,1,0:T(8,128)S(1)} %copy-done.1), kind=kLoop, calls=%fused_computation.58 | loop fusion | flops 4718592 | bytes 12582912 | tf_op jit(solution)/shard_map/add | solution.py:47
  119.7 2.2 %collective-permute-done.23 = f32[2,1,96,128]{3,1,2,0:T(1,128)S(1)} collective-permute-done((f32[2,1,96,128]{3,1,2,0:T(1,128)S(1)}, f32[2,1,96,128]{3,1,2,0:T(1,128)S(1)}, u32[]{:S(2)}, u32[]{:S(2)}) %collective-permute-start.23) | collective-permute-done | bytes 98336 | tf_op jit(solution)/shard_map/ppermute | solution.py:25
  121.9 4.5 %collective-permute-done.22 = f32[2,1,96,128]{3,1,2,0:T(1,128)S(1)} collective-permute-done((f32[2,1,96,128]{3,1,2,0:T(1,128)S(1)}, f32[2,1,96,128]{3,1,2,0:T(1,128)S(1)}, u32[]{:S(2)}, u32[]{:S(2)}) %collective-permute-start.22) | collective-permute-done | bytes 98336 | tf_op jit(solution)/shard_map/ppermute | solution.py:24
  132.4 3.0 %fusion.41 = f32[2,16,96,128]{3,1,2,0:T(8,128)S(1)} fusion(f32[2,16,96,128]{3,1,2,0:T(8,128)S(1)} %slice.881, f32[2,18,98,128]{3,1,2,0:T(8,128)S(1)} %fusion.67, f32[2,16,96,128]{3,2,1,0:T(8,128)S(1)} %copy-done, f32[2,16,96,128]{3,2,1,0:T(8,128)S(1)} %copy-done.1), kind=kLoop, calls=%fused_computation.65 | loop fusion | flops 4718592 | bytes 12582912 | tf_op jit(solution)/shard_map/add | solution.py:47
  137.8 4.6 %collective-permute-done.26 = f32[2,1,96,128]{3,1,2,0:T(1,128)S(1)} collective-permute-done((f32[2,1,96,128]{3,1,2,0:T(1,128)S(1)}, f32[2,1,96,128]{3,1,2,0:T(1,128)S(1)}, u32[]{:S(2)}, u32[]{:S(2)}) %collective-permute-start.26) | collective-permute-done | bytes 98336 | tf_op jit(solution)/shard_map/ppermute | solution.py:24
  147.4 3.0 %fusion.48 = f32[2,16,96,128]{3,1,2,0:T(8,128)S(1)} fusion(f32[2,16,96,128]{3,1,2,0:T(8,128)S(1)} %slice.888, f32[2,18,98,128]{3,1,2,0:T(8,128)S(1)} %fusion.69, f32[2,16,96,128]{3,2,1,0:T(8,128)S(1)} %copy-done, f32[2,16,96,128]{3,2,1,0:T(8,128)S(1)} %copy-done.1), kind=kLoop, calls=%fused_computation.72 | loop fusion | flops 4718592 | bytes 12582912 | tf_op jit(solution)/shard_map/add | solution.py:47
  152.8 4.6 %collective-permute-done.30 = f32[2,1,96,128]{3,1,2,0:T(1,128)S(1)} collective-permute-done((f32[2,1,96,128]{3,1,2,0:T(1,128)S(1)}, f32[2,1,96,128]{3,1,2,0:T(1,128)S(1)}, u32[]{:S(2)}, u32[]{:S(2)}) %collective-permute-start.30) | collective-permute-done | bytes 98336 | tf_op jit(solution)/shard_map/ppermute | solution.py:24
  163.3 3.0 %fusion.55 = f32[2,16,96,128]{3,1,2,0:T(8,128)S(1)} fusion(f32[2,16,96,128]{3,1,2,0:T(8,128)S(1)} %slice.895, f32[2,18,98,128]{3,1,2,0:T(8,128)S(1)} %fusion.71, f32[2,16,96,128]{3,2,1,0:T(8,128)S(1)} %copy-done, f32[2,16,96,128]{3,2,1,0:T(8,128)S(1)} %copy-done.1), kind=kLoop, calls=%fused_computation.79 | loop fusion | flops 4718592 | bytes 12582912 | tf_op jit(solution)/shard_map/add | solution.py:47
  (118 shorter events, 58.6 us)
Async XLA Ops:
  2.3 9.2 %collective-permute-start.4 = (f32[16,128]{1,0:T(8,128)S(1)}, f32[16,128]{1,0:T(8,128)S(1)}, u32[]{:S(2)}, u32[]{:S(2)}) collective-permute-start(f32[16,128]{1,0:T(8,128)S(1)} %fusion.99), channel_id=1, source_target_pairs={{0,1},{1,0},{2,3},{3,2},{4,5},{5,4},{6,7},{7,6},{8,9},{9,8},{10,11... | collective-permute-start | bytes 24584 | tf_op jit(solution)/shard_map/ppermute | solution.py:14
  6.3 24.5 %collective-permute-start = (f32[2,1,96,128]{3,1,2,0:T(1,128)S(1)}, f32[2,1,96,128]{3,1,2,0:T(1,128)S(1)}, u32[]{:S(2)}, u32[]{:S(2)}) collective-permute-start(f32[2,1,96,128]{3,1,2,0:T(1,128)S(1)} %bitcast.16), channel_id=1, source_target_pairs={{0,2},{2,4},{4,6},{6,8},{8,10},{10,12},{12,14},{14,16},{16,18},{18... | collective-permute-start | bytes 294920 | tf_op jit(solution)/shard_map/ppermute | solution.py:24
  6.4 24.5 %collective-permute-start.1 = (f32[2,1,96,128]{3,1,2,0:T(1,128)S(1)}, f32[2,1,96,128]{3,1,2,0:T(1,128)S(1)}, u32[]{:S(2)}, u32[]{:S(2)}) collective-permute-start(f32[2,1,96,128]{3,1,2,0:T(1,128)S(1)} %bitcast.15), channel_id=1, source_target_pairs={{2,0},{4,2},{6,4},{8,6},{10,8},{12,10},{14,12},{16,14},{18,16},{20... | collective-permute-start | bytes 294920 | tf_op jit(solution)/shard_map/ppermute | solution.py:25
  30.9 3.9 %collective-permute-start.2 = (f32[2,18,1,128]{3,1,2,0:T(8,128)S(1)}, f32[2,18,1,128]{3,1,2,0:T(8,128)S(1)}, u32[]{:S(2)}, u32[]{:S(2)}) collective-permute-start(f32[2,18,1,128]{3,1,2,0:T(8,128)S(1)} %get-tuple-element.253), channel_id=1, source_target_pairs={{0,1},{1,0},{2,3},{3,2},{4,5},{5,4},{6,7},{7,6},{8,9},{9,8},{10,11... | collective-permute-start | bytes 55304 | tf_op jit(solution)/shard_map/ppermute | solution.py:24
  31.5 3.8 %collective-permute-start.3 = (f32[2,18,1,128]{3,1,2,0:T(8,128)S(1)}, f32[2,18,1,128]{3,1,2,0:T(8,128)S(1)}, u32[]{:S(2)}, u32[]{:S(2)}) collective-permute-start(f32[2,18,1,128]{3,1,2,0:T(8,128)S(1)} %get-tuple-element.289), channel_id=1, source_target_pairs={{1,0},{0,1},{3,2},{2,3},{5,4},{4,5},{7,6},{6,7},{9,8},{8,9},{11,10... | collective-permute-start | bytes 55304 | tf_op jit(solution)/shard_map/ppermute | solution.py:25
  40.7 6.8 %collective-permute-start.5 = (f32[2,1,96,128]{3,1,2,0:T(1,128)S(1)}, f32[2,1,96,128]{3,1,2,0:T(1,128)S(1)}, u32[]{:S(2)}, u32[]{:S(2)}) collective-permute-start(f32[2,1,96,128]{3,1,2,0:T(1,128)S(1)} %get-tuple-element.306), channel_id=1, source_target_pairs={{0,2},{2,4},{4,6},{6,8},{8,10},{10,12},{12,14},{14,16},{16,18},{18... | collective-permute-start | bytes 294920 | tf_op jit(solution)/shard_map/ppermute | solution.py:24
  47.5 3.9 %collective-permute-start.7 = (f32[2,18,1,128]{3,1,2,0:T(8,128)S(1)}, f32[2,18,1,128]{3,1,2,0:T(8,128)S(1)}, u32[]{:S(2)}, u32[]{:S(2)}) collective-permute-start(f32[2,18,1,128]{3,1,2,0:T(8,128)S(1)} %get-tuple-element.245), channel_id=1, source_target_pairs={{0,1},{1,0},{2,3},{3,2},{4,5},{5,4},{6,7},{7,6},{8,9},{9,8},{10,11... | collective-permute-start | bytes 55304 | tf_op jit(solution)/shard_map/ppermute | solution.py:24
  49.1 3.8 %collective-permute-start.8 = (f32[2,18,1,128]{3,1,2,0:T(8,128)S(1)}, f32[2,18,1,128]{3,1,2,0:T(8,128)S(1)}, u32[]{:S(2)}, u32[]{:S(2)}) collective-permute-start(f32[2,18,1,128]{3,1,2,0:T(8,128)S(1)} %get-tuple-element.285), channel_id=1, source_target_pairs={{1,0},{0,1},{3,2},{2,3},{5,4},{4,5},{7,6},{6,7},{9,8},{8,9},{11,10... | collective-permute-start | bytes 55304 | tf_op jit(solution)/shard_map/ppermute | solution.py:25
  56.7 7.0 %collective-permute-start.9 = (f32[2,1,96,128]{3,1,2,0:T(1,128)S(1)}, f32[2,1,96,128]{3,1,2,0:T(1,128)S(1)}, u32[]{:S(2)}, u32[]{:S(2)}) collective-permute-start(f32[2,1,96,128]{3,1,2,0:T(1,128)S(1)} %get-tuple-element.304), channel_id=1, source_target_pairs={{0,2},{2,4},{4,6},{6,8},{8,10},{10,12},{12,14},{14,16},{16,18},{18... | collective-permute-start | bytes 294920 | tf_op jit(solution)/shard_map/ppermute | solution.py:24
  63.7 3.9 %collective-permute-start.11 = (f32[2,18,1,128]{3,1,2,0:T(8,128)S(1)}, f32[2,18,1,128]{3,1,2,0:T(8,128)S(1)}, u32[]{:S(2)}, u32[]{:S(2)}) collective-permute-start(f32[2,18,1,128]{3,1,2,0:T(8,128)S(1)} %get-tuple-element.237), channel_id=1, source_target_pairs={{0,1},{1,0},{2,3},{3,2},{4,5},{5,4},{6,7},{7,6},{8,9},{9,8},{10,11... | collective-permute-start | bytes 55304 | tf_op jit(solution)/shard_map/ppermute | solution.py:24
  71.8 6.8 %collective-permute-start.13 = (f32[2,1,96,128]{3,1,2,0:T(1,128)S(1)}, f32[2,1,96,128]{3,1,2,0:T(1,128)S(1)}, u32[]{:S(2)}, u32[]{:S(2)}) collective-permute-start(f32[2,1,96,128]{3,1,2,0:T(1,128)S(1)} %get-tuple-element.302), channel_id=1, source_target_pairs={{0,2},{2,4},{4,6},{6,8},{8,10},{10,12},{12,14},{14,16},{16,18},{18... | collective-permute-start | bytes 294920 | tf_op jit(solution)/shard_map/ppermute | solution.py:24
  79.3 4.0 %collective-permute-start.15 = (f32[2,18,1,128]{3,1,2,0:T(8,128)}, f32[2,18,1,128]{3,1,2,0:T(8,128)S(1)}, u32[]{:S(2)}, u32[]{:S(2)}) collective-permute-start(f32[2,18,1,128]{3,1,2,0:T(8,128)} %get-tuple-element.229), channel_id=1, source_target_pairs={{0,1},{1,0},{2,3},{3,2},{4,5},{5,4},{6,7},{7,6},{8,9},{9,8},{10,11... | collective-permute-start | bytes 55304 | tf_op jit(solution)/shard_map/ppermute | solution.py:24
  80.8 4.0 %collective-permute-start.16 = (f32[2,18,1,128]{3,1,2,0:T(8,128)}, f32[2,18,1,128]{3,1,2,0:T(8,128)S(1)}, u32[]{:S(2)}, u32[]{:S(2)}) collective-permute-start(f32[2,18,1,128]{3,1,2,0:T(8,128)} %get-tuple-element.277), channel_id=1, source_target_pairs={{1,0},{0,1},{3,2},{2,3},{5,4},{4,5},{7,6},{6,7},{9,8},{8,9},{11,10... | collective-permute-start | bytes 55304 | tf_op jit(solution)/shard_map/ppermute | solution.py:25
  90.5 20.5 %collective-permute-start.18 = (f32[2,1,96,128]{3,1,2,0:T(1,128)S(1)}, f32[2,1,96,128]{3,1,2,0:T(1,128)S(1)}, u32[]{:S(2)}, u32[]{:S(2)}) collective-permute-start(f32[2,1,96,128]{3,1,2,0:T(1,128)S(1)} %get-tuple-element.299), channel_id=1, source_target_pairs={{2,0},{4,2},{6,4},{8,6},{10,8},{12,10},{14,12},{16,14},{18,16},{20... | collective-permute-start | bytes 294920 | tf_op jit(solution)/shard_map/ppermute | solution.py:25
  90.6 20.4 %collective-permute-start.17 = (f32[2,1,96,128]{3,1,2,0:T(1,128)S(1)}, f32[2,1,96,128]{3,1,2,0:T(1,128)S(1)}, u32[]{:S(2)}, u32[]{:S(2)}) collective-permute-start(f32[2,1,96,128]{3,1,2,0:T(1,128)S(1)} %get-tuple-element.300), channel_id=1, source_target_pairs={{0,2},{2,4},{4,6},{6,8},{8,10},{10,12},{12,14},{14,16},{16,18},{18... | collective-permute-start | bytes 294920 | tf_op jit(solution)/shard_map/ppermute | solution.py:24
  111.1 3.9 %collective-permute-start.19 = (f32[2,18,1,128]{3,1,2,0:T(8,128)S(1)}, f32[2,18,1,128]{3,1,2,0:T(8,128)S(1)}, u32[]{:S(2)}, u32[]{:S(2)}) collective-permute-start(f32[2,18,1,128]{3,1,2,0:T(8,128)S(1)} %get-tuple-element.221), channel_id=1, source_target_pairs={{0,1},{1,0},{2,3},{3,2},{4,5},{5,4},{6,7},{7,6},{8,9},{9,8},{10,11... | collective-permute-start | bytes 55304 | tf_op jit(solution)/shard_map/ppermute | solution.py:24
  119.7 6.7 %collective-permute-start.22 = (f32[2,1,96,128]{3,1,2,0:T(1,128)S(1)}, f32[2,1,96,128]{3,1,2,0:T(1,128)S(1)}, u32[]{:S(2)}, u32[]{:S(2)}) collective-permute-start(f32[2,1,96,128]{3,1,2,0:T(1,128)S(1)} %get-tuple-element.298), channel_id=1, source_target_pairs={{0,2},{2,4},{4,6},{6,8},{8,10},{10,12},{12,14},{14,16},{16,18},{18... | collective-permute-start | bytes 294920 | tf_op jit(solution)/shard_map/ppermute | solution.py:24
  126.5 3.9 %collective-permute-start.24 = (f32[2,18,1,128]{3,1,2,0:T(8,128)S(1)}, f32[2,18,1,128]{3,1,2,0:T(8,128)S(1)}, u32[]{:S(2)}, u32[]{:S(2)}) collective-permute-start(f32[2,18,1,128]{3,1,2,0:T(8,128)S(1)} %get-tuple-element.213), channel_id=1, source_target_pairs={{0,1},{1,0},{2,3},{3,2},{4,5},{5,4},{6,7},{7,6},{8,9},{9,8},{10,11... | collective-permute-start | bytes 55304 | tf_op jit(solution)/shard_map/ppermute | solution.py:24
  135.6 6.8 %collective-permute-start.26 = (f32[2,1,96,128]{3,1,2,0:T(1,128)S(1)}, f32[2,1,96,128]{3,1,2,0:T(1,128)S(1)}, u32[]{:S(2)}, u32[]{:S(2)}) collective-permute-start(f32[2,1,96,128]{3,1,2,0:T(1,128)S(1)} %get-tuple-element.296), channel_id=1, source_target_pairs={{0,2},{2,4},{4,6},{6,8},{8,10},{10,12},{12,14},{14,16},{16,18},{18... | collective-permute-start | bytes 294920 | tf_op jit(solution)/shard_map/ppermute | solution.py:24
  142.4 3.9 %collective-permute-start.28 = (f32[2,18,1,128]{3,1,2,0:T(8,128)S(1)}, f32[2,18,1,128]{3,1,2,0:T(8,128)S(1)}, u32[]{:S(2)}, u32[]{:S(2)}) collective-permute-start(f32[2,18,1,128]{3,1,2,0:T(8,128)S(1)} %get-tuple-element.205), channel_id=1, source_target_pairs={{0,1},{1,0},{2,3},{3,2},{4,5},{5,4},{6,7},{7,6},{8,9},{9,8},{10,11... | collective-permute-start | bytes 55304 | tf_op jit(solution)/shard_map/ppermute | solution.py:24
  143.0 3.8 %collective-permute-start.29 = (f32[2,18,1,128]{3,1,2,0:T(8,128)S(1)}, f32[2,18,1,128]{3,1,2,0:T(8,128)S(1)}, u32[]{:S(2)}, u32[]{:S(2)}) collective-permute-start(f32[2,18,1,128]{3,1,2,0:T(8,128)S(1)} %get-tuple-element.265), channel_id=1, source_target_pairs={{1,0},{0,1},{3,2},{2,3},{5,4},{4,5},{7,6},{6,7},{9,8},{8,9},{11,10... | collective-permute-start | bytes 55304 | tf_op jit(solution)/shard_map/ppermute | solution.py:25
  150.6 6.8 %collective-permute-start.30 = (f32[2,1,96,128]{3,1,2,0:T(1,128)S(1)}, f32[2,1,96,128]{3,1,2,0:T(1,128)S(1)}, u32[]{:S(2)}, u32[]{:S(2)}) collective-permute-start(f32[2,1,96,128]{3,1,2,0:T(1,128)S(1)} %get-tuple-element.294), channel_id=1, source_target_pairs={{0,2},{2,4},{4,6},{6,8},{8,10},{10,12},{12,14},{14,16},{16,18},{18... | collective-permute-start | bytes 294920 | tf_op jit(solution)/shard_map/ppermute | solution.py:24
  157.4 3.9 %collective-permute-start.32 = (f32[2,18,1,128]{3,1,2,0:T(8,128)S(1)}, f32[2,18,1,128]{3,1,2,0:T(8,128)S(1)}, u32[]{:S(2)}, u32[]{:S(2)}) collective-permute-start(f32[2,18,1,128]{3,1,2,0:T(8,128)S(1)} %get-tuple-element.197), channel_id=1, source_target_pairs={{0,1},{1,0},{2,3},{3,2},{4,5},{5,4},{6,7},{7,6},{8,9},{9,8},{10,11... | collective-permute-start | bytes 55304 | tf_op jit(solution)/shard_map/ppermute | solution.py:24
  158.9 3.8 %collective-permute-start.33 = (f32[2,18,1,128]{3,1,2,0:T(8,128)S(1)}, f32[2,18,1,128]{3,1,2,0:T(8,128)S(1)}, u32[]{:S(2)}, u32[]{:S(2)}) collective-permute-start(f32[2,18,1,128]{3,1,2,0:T(8,128)S(1)} %get-tuple-element.261), channel_id=1, source_target_pairs={{1,0},{0,1},{3,2},{2,3},{5,4},{4,5},{7,6},{6,7},{9,8},{8,9},{11,10... | collective-permute-start | bytes 55304 | tf_op jit(solution)/shard_map/ppermute | solution.py:25
  (13 other events, 39.7 us)
where the time goes:
time: 168 us
  waiting for transfers between devices  63.5 us (38%)
  blocking collectives  36.7 us (22%)
  other arithmetic  28.9 us (17%)
  starting transfers between devices  28.7 us (17%)
  local copies, waits for them, and re-layouts  8.85 us (5%)
    ppermute x16, waiting for transfers between devices, with_halo(): before = lax.ppermute(last, axis, up)  42.2 us
    all_gather x2, blocking collectives, per_device(): whole_cycle = lax.all_gather(facing, 'az', axis=0, tiled=True)  36.7 us
    add x8, other arithmetic, relax_once(): return center_cells + OMEGA * misfit / center  23.7 us
    ppermute x16, waiting for transfers between devices, with_halo(): after = lax.ppermute(first, axis, down)  18.8 us
    ppermute x16, starting transfers between devices, with_halo(): after = lax.ppermute(first, axis, down)  13.5 us
    ppermute x16, starting transfers between devices, with_halo(): before = lax.ppermute(last, axis, up)  11.6 us
    concatenate x8, other arithmetic, with_halo(): array = jnp.concatenate([before, array, after], axis=dim)  4.29 us
    unnamed x7, local copies, waits for them, and re-layouts  4.03 us
  transfers between devices with their start and end apart: 34, of which 29 were waited for; matrix products, arithmetic and copies ran while one was open for 1% of the time, Pallas kernels for 0%

commit v1 on v0

v1 whole, which is shorter than its diff:
```python
import functools

import jax
import jax.numpy as jnp
from jax import lax
from jax.experimental import pallas as pl
from jax.experimental.pallas import tpu as pltpu
from jax.sharding import PartitionSpec as P

STEPS = 2
SWEEPS = 4
OMEGA = 0.8
TILE = 8
HALO = SWEEPS


def sweep_column(before, here, after, weight, shift, low_phys, high_phys, low_value, high_value):
    rows, lanes = here.shape
    row = lax.broadcasted_iota(jnp.int32, here.shape, 0)
    lane = lax.broadcasted_iota(jnp.int32, here.shape, 1)
    low_fix = jnp.logical_and(row == TILE - 1, low_phys)
    high_fix = jnp.logical_and(row == rows - TILE, high_phys)
    edged = jnp.where(low_fix, low_value, jnp.where(high_fix, high_value, here))
    radial = pltpu.roll(edged, 1, 0) + pltpu.roll(edged, rows - 1, 0)
    axial = jnp.where(lane == 0, 0.0, pltpu.roll(here, 1, 1)) + jnp.where(
        lane == lanes - 1, 0.0, pltpu.roll(here, lanes - 1, 1)
    )
    nbr = (before + after) + (radial + axial)
    return (1.0 - OMEGA) * here + shift + weight * nbr


def run_sweeps(rad_ref, ghost_ref, field, weight, shift, out_ref):
    _, columns, rows, _ = field.shape
    at_low = rad_ref[0] == 0
    at_high = jnp.logical_not(at_low)
    for sweep in range(1, SWEEPS + 1):
        for annulus in range(2):

            def body(j, before, annulus=annulus, sweep=sweep):
                here = field[annulus, j]
                after = field[annulus, j + 1]
                ghost = ghost_ref[pl.ds(j, 1), :]
                low_value = here[TILE : TILE + 1] if annulus == 0 else ghost
                high_value = ghost if annulus == 0 else here[rows - TILE - 1 : rows - TILE]
                new = sweep_column(
                    before,
                    here,
                    after,
                    weight[annulus, j],
                    shift[annulus, j],
                    at_low,
                    at_high,
                    low_value,
                    high_value,
                )
                if sweep == SWEEPS:
                    out_ref[annulus, j - HALO] = new[TILE : rows - TILE]
                else:
                    field[annulus, j] = new
                return here

            lax.fori_loop(sweep, columns - sweep, body, field[annulus, sweep - 1])


def place(target, own, left, right, cut, cut_left, cut_right, width):
    _, columns, rows, _ = target.shape
    inner = pl.ds(TILE, rows - 2 * TILE)
    for first, block, cut_block in (
        (HALO - width, left, cut_left),
        (HALO, own, cut),
        (columns - HALO, right, cut_right),
    ):
        span = pl.ds(first, block.shape[1])
        target[:, span, inner, :] = block
        target[:, span, pl.ds(0, TILE), :] = cut_block
        target[:, span, pl.ds(rows - TILE, TILE), :] = cut_block


def first_kernel(
    rad_ref,
    ghost_ref,
    p_ref,
    s_ref,
    d_ref,
    left_ref,
    right_ref,
    cut_ref,
    cut_left_ref,
    cut_right_ref,
    out_ref,
    weight,
    shift,
    field,
):
    h, n = HALO, HALO - 1
    place(
        field,
        p_ref[...],
        left_ref[:, :h],
        right_ref[:, :h],
        cut_ref[0],
        cut_left_ref[:, :h],
        cut_right_ref[:, :h],
        h,
    )
    for target, source, at, k in ((shift, s_ref, h, 1), (weight, d_ref, h + n, 2)):
        place(
            target,
            source[...],
            left_ref[:, at : at + n],
            right_ref[:, at : at + n],
            cut_ref[k],
            cut_left_ref[:, at : at + n],
            cut_right_ref[:, at : at + n],
            n,
        )

    def body(j, carry):
        for annulus in range(2):
            w = OMEGA / (6.0 + weight[annulus, j])
            weight[annulus, j] = w
            shift[annulus, j] = w * shift[annulus, j]
        return carry

    lax.fori_loop(1, field.shape[1] - 1, body, 0)
    run_sweeps(rad_ref, ghost_ref, field, weight, shift, out_ref)


def later_kernel(
    rad_ref,
    ghost_ref,
    p_ref,
    weight,
    shift,
    left_ref,
    right_ref,
    cut_ref,
    cut_left_ref,
    cut_right_ref,
    out_ref,
    field,
):
    place(
        field,
        p_ref[...],
        left_ref[...],
        right_ref[...],
        cut_ref[...],
        cut_left_ref[...],
        cut_right_ref[...],
        HALO,
    )
    run_sweeps(rad_ref, ghost_ref, field, weight, shift, out_ref)


def ring(size, step):
    return [(i, (i + step) % size) for i in range(size)]


def diagonal_pairs(size, step):
    return [(2 * i + r, 2 * ((i + step) % size) + 1 - r) for i in range(size) for r in range(2)]


def facing_pairs(size, turn, k):
    pairs = []
    for i in range(size):
        pairs.append((2 * ((i - turn + k) % size) + 1, 2 * i))
        pairs.append((2 * ((i + turn + k) % size), 2 * i + 1))
    return pairs


def far_pairs(size, turn):
    return [(2 * i + r, 2 * ((i + (2 * r - 1) * turn) % size) + r) for i in range(size) for r in range(2)]


def ghost_window(edge, offset, radial_index):
    size = lax.axis_size("az")
    cells = edge.shape[0]
    turn = (offset + cells // 2) // cells
    rest = offset - turn * cells
    turn = turn % size
    near = min(size, 16)

    def far(t):
        return lambda e: lax.ppermute(e, ("az", "rad"), far_pairs(size, t * near))

    def branch(t):
        return lambda e: tuple(
            lax.ppermute(e, ("az", "rad"), facing_pairs(size, t, k)) for k in (-1, 0, 1)
        )

    if size > near:
        edge = lax.switch(turn // near, [far(t) for t in range(-(-size // near))], edge)
    blocks = lax.switch(turn % near, [branch(t) for t in range(near)], edge)
    start = cells - HALO + jnp.where(radial_index == 0, -rest, rest)
    return lax.dynamic_slice_in_dim(
        jnp.concatenate(blocks, axis=0), start, cells + 2 * HALO, 0
    )


def per_device(pressure, source, diagonal, rot_offset):
    _, cells, radial_cells, lanes = pressure.shape
    size = lax.axis_size("az")
    radial_index = lax.axis_index("rad")
    rad = radial_index.astype(jnp.int32).reshape(1)
    h, n = HALO, HALO - 1
    rows = radial_cells + 2 * TILE
    extended = jax.ShapeDtypeStruct((2, cells + 2 * h, rows, lanes), jnp.float32)
    own = jax.ShapeDtypeStruct(pressure.shape, jnp.float32)
    vmem = pl.BlockSpec(memory_space=pltpu.VMEM)
    smem = pl.BlockSpec(memory_space=pltpu.SMEM)
    params = pltpu.CompilerParams(vmem_limit_bytes=40 << 20)

    def cut_tile(x):
        return jnp.where(radial_index == 0, x[:, :, radial_cells - TILE :], x[:, :, :TILE])

    def interface(p, step):
        edge = jnp.where(radial_index == 0, p[1, :, 0, :], p[0, :, radial_cells - 1, :])
        offset = rot_offset[0] * step % (cells * size)
        return ghost_window(edge, offset, radial_index)

    def exchange(last, first, cut, cut_last, cut_first):
        left = lax.ppermute(last, "az", ring(size, 1))
        right = lax.ppermute(first, "az", ring(size, -1))
        facing = lax.ppermute(cut, "rad", [(0, 1), (1, 0)])
        corner_left = lax.ppermute(cut_last, ("az", "rad"), diagonal_pairs(size, 1))
        corner_right = lax.ppermute(cut_first, ("az", "rad"), diagonal_pairs(size, -1))
        return left, right, facing, corner_left, corner_right

    def ends(p, s, d):
        last = jnp.concatenate([p[:, cells - h :], s[:, cells - n :], d[:, cells - n :]], axis=1)
        first = jnp.concatenate([p[:, :h], s[:, :n], d[:, :n]], axis=1)
        return last, first

    cuts = [cut_tile(x) for x in (pressure, source, diagonal)]
    moved = exchange(*ends(pressure, source, diagonal), jnp.stack(cuts), *ends(*cuts))
    ghost = interface(pressure, 1)
    pressure, weight, shift = pl.pallas_call(
        first_kernel,
        out_shape=(own, extended, extended),
        in_specs=[smem] + [vmem] * 9,
        out_specs=[vmem] * 3,
        scratch_shapes=[pltpu.VMEM(extended.shape, jnp.float32)],
        compiler_params=params,
        name="first_step",
    )(rad, ghost, pressure, source, diagonal, *moved)
    for step in range(2, STEPS + 1):
        cut = cut_tile(pressure)
        moved = exchange(
            pressure[:, cells - h :], pressure[:, :h], cut, cut[:, cells - h :], cut[:, :h]
        )
        ghost = interface(pressure, step)
        pressure = pl.pallas_call(
            later_kernel,
            out_shape=own,
            in_specs=[smem] + [vmem] * 9,
            out_specs=vmem,
            scratch_shapes=[pltpu.VMEM(extended.shape, jnp.float32)],
            compiler_params=params,
            name="later_step",
        )(rad, ghost, pressure, weight, shift, *moved)
    return pressure


def solution(mesh):
    placed = (
        P(None, "az", "rad", None),
        P(None, "az", "rad", None),
        P(None, "az", "rad", None),
        P(),
    )
    return jax.shard_map(
        per_device,
        mesh=mesh,
        in_specs=placed,
        out_specs=P(None, "az", "rad", None),
        check_vma=False,
    )
```

time: 168 us -> 134 us (0.80); the launches traced: 168 us -> 136 us
  waiting for transfers between devices: 63.5 us -> 17.6 us
  blocking collectives: 36.7 us -> 0 us
  Pallas kernels: 0 us -> 35.4 us
  starting transfers between devices: 28.7 us -> 53.1 us
  other arithmetic: 28.9 us -> 8.78 us
  local copies, waits for them, and re-layouts: 8.85 us -> 20 us
    ppermute x34 -> x16, waiting for transfers between devices: 63.5 us -> 17.6 us  [the longest x6 8.27 us: branch(): lax.ppermute(e, ('az', 'rad'), facing_pairs(size, t, k))]
    all_gather x2 -> x0, blocking collectives: 36.7 us -> none  [per_device(): whole_cycle = lax.all_gather(facing, 'az', axis=0, tiled=True)]
    pallas_call x0 -> x2, Pallas kernels: none -> 35.4 us  [the longest x1 18.3 us: per_device(): pl.pallas_call(first_kernel, out_shape=(own, extended, extended), in_spec...]
    ppermute x34 -> x16, starting transfers between devices: 28.7 us -> 53.1 us  [the longest x6 26.2 us: branch(): lax.ppermute(e, ('az', 'rad'), facing_pairs(size, t, k))]
    add x8 -> x0, other arithmetic: 23.7 us -> none  [relax_once(): return center_cells + OMEGA * misfit / center]
    unnamed x7 -> x32, local copies, waits for them, and re-layouts: 4.03 us -> 13.3 us
    another operation x2 -> x1, local copies, waits for them, and re-layouts: 0.01 us -> 2.37 us  [relax_once(): low_value = jnp.stack([padded[0, :, margin, :], ghost_cycle])]
    select_n x2 -> x5, other arithmetic: 0.01 us -> 2.28 us  [the longest x3 2.26 us: cut_tile(): jnp.where(radial_index == 0, x[:, :, radial_cells - TILE:], x[:, :, :TILE])]
  transfers between devices with their start and end apart: 34 -> 16, of which waited for: 29 -> 7; matrix products, arithmetic and copies ran while one was open for 1% -> 9% of each run, Pallas kernels for 0% -> 0%
where the time goes in v1:
time: 134 us; the launch traced here: 136 us
  starting transfers between devices  53.1 us (40%)
  Pallas kernels  35.4 us (26%)
  local copies, waits for them, and re-layouts  20 us (15%)
  waiting for transfers between devices  17.6 us (13%)
  other arithmetic  8.78 us (7%)
    ppermute x6, starting transfers between devices, branch(): lax.ppermute(e, ('az', 'rad'), facing_pairs(size, t, k))  26.2 us
    pallas_call x1, Pallas kernels, per_device(): pl.pallas_call(first_kernel, out_shape=(own, extended, extended), in_spec...  18.3 us
    pallas_call x1, Pallas kernels, per_device(): pl.pallas_call(later_kernel, out_shape=own, in_specs=[smem] + [vmem] * 9,...  17.1 us
    unnamed x32, local copies, waits for them, and re-layouts  13.3 us
    ppermute x2, starting transfers between devices, exchange(): right = lax.ppermute(first, 'az', ring(size, -1))  9.91 us
    ppermute x2, starting transfers between devices, exchange(): facing = lax.ppermute(cut, 'rad', [(0, 1), (1, 0)])  9.02 us
    ppermute x6, waiting for transfers between devices, branch(): lax.ppermute(e, ('az', 'rad'), facing_pairs(size, t, k))  8.27 us
    ppermute x2, waiting for transfers between devices, exchange(): corner_left = lax.ppermute(cut_last, ('az', 'rad'), diagonal_pairs(size, 1))  5.45 us
  transfers between devices with their start and end apart: 16, of which 7 were waited for; matrix products, arithmetic and copies ran while one was open for 9% of the time, Pallas kernels for 0%

profile of v1, /device:TPU:0, one launch (start us, length us, event | category | flops | bytes accessed | tf_op | source)
XLA Modules:
  0.0 135.8 jit_solution(11554295580944318165)
XLA Ops:
  3.2 7.1 %collective-permute-start.98 = (f32[3,2,16,8,128]{4,3,2,1,0:T(8,128)}, f32[3,2,16,8,128]{4,3,2,1,0:T(8,128)S(1)}, u32[]{:S(2)}, u32[]{:S(2)}) collective-permute-start(f32[3,2,16,8,128]{4,3,2,1,0:T(8,128)} %pad_maximum_fusion.2), channel_id=1, source_target_pairs={{0,1},{1,0},{2,3},{3,2},{4,5},{5,4},{6,7},{7,6},{8,9},{9,8},{10,11... | collective-permute-start | bytes 1179656 | tf_op jit(solution)/shard_map/ppermute | solution.py:225
  11.1 2.0 %fusion.22 = (f32[2,3,96,128]{3,2,1,0:T(8,128)}, f32[2,3,96,128]{3,2,1,0:T(8,128)S(1)}, f32[2,3,96,128]{3,2,1,0:T(8,128)S(1)}, f32[2,3,96,128]{3,2,1,0:T(8,128)}) fusion(f32[2,16,96,128]{3,2,1,0:T(8,128)S(1)} %copy-done, f32[2,16,96,128]{3,2,1,0:T(8,128)} %d_ref.1), kind=kLoop, calls=%fused_computation.54 | loop fusion | bytes 2359296 | tf_op jit(solution)/shard_map/slice | solution.py:232
  15.2 26.0 %conditional.2 = (f32[16,128]{1,0:T(8,128)}, f32[16,128]{1,0:T(8,128)}, f32[16,128]{1,0:T(8,128)}) conditional(s32[]{:T(128)} %clamp.7, (pred[]{:T(512)}, f32[2,16,96,128]{3,2,1,0:T(8,128)}) %tuple.149, (pred[]{:T(512)}, f32[2,16,96,128]{3,2,1,0:T(8,128)}) %tuple.149, (pred[]{:T(512)}, ...), branch_computations={%region_0.1_spmd, %region_1.2_spmd, %region_2.3_spmd, %region_3.4_... | conditional | flops 2048 | bytes 3268753 | solution.py:194
  15.2 2.4 %copy.11 = f32[2,16,96,128]{3,1,2,0:T(8,128)S(1)} copy(f32[2,16,96,128]{3,2,1,0:T(8,128)} %get-tuple-element.204) | data formatting | bytes 3145728 | tf_op jit(solution)/shard_map
  17.6 5.7 %collective-permute-start.59 = (f32[16,128]{1,0:T(8,128)S(1)}, f32[16,128]{1,0:T(8,128)}, u32[]{:S(2)}, u32[]{:S(2)}) collective-permute-start(f32[16,128]{1,0:T(8,128)S(1)} %fusion.3), channel_id=1, source_target_pairs={{29,0},{8,1},{31,2},{10,3},{1,4},{12,5},{3,6},{14,7},{5,8},{16,9},... | collective-permute-start | bytes 24584 | tf_op jit(solution)/shard_map/cond/branch_3_fun/ppermute | solution.py:189
  23.3 5.7 %collective-permute-start.58 = (f32[16,128]{1,0:T(8,128)S(1)}, f32[16,128]{1,0:T(8,128)}, u32[]{:S(2)}, u32[]{:S(2)}) collective-permute-start(f32[16,128]{1,0:T(8,128)S(1)} %fusion.3), channel_id=1, source_target_pairs={{27,0},{6,1},{29,2},{8,3},{31,4},{10,5},{1,6},{12,7},{3,8},{14,9},... | collective-permute-start | bytes 24584 | tf_op jit(solution)/shard_map/cond/branch_3_fun/ppermute | solution.py:189
  29.0 5.7 %collective-permute-start.57 = (f32[16,128]{1,0:T(8,128)S(1)}, f32[16,128]{1,0:T(8,128)}, u32[]{:S(2)}, u32[]{:S(2)}) collective-permute-start(f32[16,128]{1,0:T(8,128)S(1)} %fusion.3), channel_id=1, source_target_pairs={{25,0},{4,1},{27,2},{6,3},{29,4},{8,5},{31,6},{10,7},{1,8},{12,9},... | collective-permute-start | bytes 24584 | tf_op jit(solution)/shard_map/cond/branch_3_fun/ppermute | solution.py:189
  34.9 6.3 %collective-permute-done.57 = f32[16,128]{1,0:T(8,128)} collective-permute-done((f32[16,128]{1,0:T(8,128)S(1)}, f32[16,128]{1,0:T(8,128)}, u32[]{:S(2)}, u32[]{:S(2)}) %collective-permute-start.57) | collective-permute-done | bytes 8224 | tf_op jit(solution)/shard_map/cond/branch_3_fun/ppermute | solution.py:189
  41.2 2.1 %pad_maximum_fusion.1 = f32[2,10,96,128]{3,2,1,0:T(8,128)} fusion(f32[2,3,96,128]{3,2,1,0:T(8,128)} %get-tuple-element.266, f32[2,3,96,128]{3,2,1,0:T(8,128)} %get-tuple-element.251, f32[2,4,96,128]{3,2,1,0:T(8,128)S(1)} %copy-done.13), kind=kLoop, calls=%fused_computation.33 | loop fusion | flops 491520 | bytes 1966080 | tf_op jit(solution)/shard_map/concatenate | solution.py:232
  49.1 3.8 %collective-permute-start.100 = (f32[2,10,8,128]{3,2,1,0:T(8,128)S(1)}, f32[2,10,8,128]{3,2,1,0:T(8,128)S(1)}, u32[]{:S(2)}, u32[]{:S(2)}) collective-permute-start(f32[2,10,8,128]{3,2,1,0:T(8,128)S(1)} %pad_maximum_fusion.4), channel_id=1, source_target_pairs={{0,31},{1,30},{2,1},{3,0},{4,3},{5,2},{6,5},{7,4},{8,7},{9,6},{10,... | collective-permute-start | bytes 245768 | tf_op jit(solution)/shard_map/ppermute | solution.py:227
  55.7 1.9 %collective-permute-done.100.cut_right_ref = f32[2,10,8,128]{3,2,1,0:T(8,128)S(1)} collective-permute-done((f32[2,10,8,128]{3,2,1,0:T(8,128)S(1)}, f32[2,10,8,128]{3,2,1,0:T(8,128)S(1)}, u32[]{:S(2)}, u32[]{:S(2)}) %collective-permute-start.100) | collective-permute-done | bytes 81952 | tf_op jit(solution)/shard_map/ppermute | solution.py:227
  63.5 18.3 %first_step.1 = (f32[2,16,96,128]{3,2,1,0:T(8,128)S(1)}, f32[2,24,112,128]{3,2,1,0:T(8,128)S(1)}, f32[2,24,112,128]{3,2,1,0:T(8,128)S(1)}) custom-call(s32[1]{0:T(128)} %bitcast.16.rad_ref, f32[24,128]{1,0:T(8,128)S(1)} %fusion.19.ghost_ref, f32[2,16,96,128]{3,2,1,0:T(8,128)} %p_ref.1, f32[2,16,96,128]{3,2,1,0:T(8,128)S(1)} %copy-done, ...), custom_call_target="tpu_custom_call" | custom-call | tf_op jit(solution)/shard_map/first_step/pallas_call | solution.py:238
  85.0 8.3 %collective-permute-start.102 = (f32[2,4,96,128]{3,2,1,0:T(8,128)S(1)}, f32[2,4,96,128]{3,2,1,0:T(8,128)S(1)}, u32[]{:S(2)}, u32[]{:S(2)}) collective-permute-start(f32[2,4,96,128]{3,2,1,0:T(8,128)S(1)} %get-tuple-element.247), channel_id=1, source_target_pairs={{0,30},{2,0},{4,2},{6,4},{8,6},{10,8},{12,10},{14,12},{16,14},{18,... | collective-permute-start | bytes 1179656 | tf_op jit(solution)/shard_map/ppermute | solution.py:224
  93.7 10.9 %conditional.3 = (f32[16,128]{1,0:T(8,128)}, f32[16,128]{1,0:T(8,128)}, f32[16,128]{1,0:T(8,128)}) conditional(s32[]{:T(128)} %clamp.6, f32[16,128]{1,0:T(8,128)S(1)} %bitcast.45, f32[16,128]{1,0:T(8,128)S(1)} %bitcast.46, f32[16,128]{1,0:T(8,128)S(1)} %bitcast.47, f32[16,128]{1,0:T(8,128)S(1)} %bitcast.48, ...), branch_computations={%region_16.17_spmd, %region_17.18_spmd, %region_18.19_spmd, %regio... | conditional | bytes 98448 | solution.py:194
  93.8 3.5 %collective-permute-start.23 = (f32[16,128]{1,0:T(8,128)S(1)}, f32[16,128]{1,0:T(8,128)}, u32[]{:S(2)}, u32[]{:S(2)}) collective-permute-start(f32[16,128]{1,0:T(8,128)S(1)} %param.23), channel_id=1, source_target_pairs={{21,0},{16,1},{23,2},{18,3},{25,4},{20,5},{27,6},{22,7},{29,8},{24... | collective-permute-start | bytes 24584 | tf_op jit(solution)/shard_map/cond/branch_7_fun/ppermute | solution.py:189
  97.3 1.8 %collective-permute-start.22 = (f32[16,128]{1,0:T(8,128)S(1)}, f32[16,128]{1,0:T(8,128)}, u32[]{:S(2)}, u32[]{:S(2)}) collective-permute-start(f32[16,128]{1,0:T(8,128)S(1)} %param.23), channel_id=1, source_target_pairs={{19,0},{14,1},{21,2},{16,3},{23,4},{18,5},{25,6},{20,7},{27,8},{22... | collective-permute-start | bytes 24584 | tf_op jit(solution)/shard_map/cond/branch_7_fun/ppermute | solution.py:189
  99.1 3.7 %collective-permute-start.21 = (f32[16,128]{1,0:T(8,128)S(1)}, f32[16,128]{1,0:T(8,128)}, u32[]{:S(2)}, u32[]{:S(2)}) collective-permute-start(f32[16,128]{1,0:T(8,128)S(1)} %param.23), channel_id=1, source_target_pairs={{17,0},{12,1},{19,2},{14,3},{21,4},{16,5},{23,6},{18,7},{25,8},{20... | collective-permute-start | bytes 24584 | tf_op jit(solution)/shard_map/cond/branch_7_fun/ppermute | solution.py:189
  102.8 1.9 %collective-permute-done.21 = f32[16,128]{1,0:T(8,128)} collective-permute-done((f32[16,128]{1,0:T(8,128)S(1)}, f32[16,128]{1,0:T(8,128)}, u32[]{:S(2)}, u32[]{:S(2)}) %collective-permute-start.21) | collective-permute-done | bytes 8224 | tf_op jit(solution)/shard_map/cond/branch_7_fun/ppermute | solution.py:189
  104.7 2.0 %collective-permute-start.103 = (f32[2,16,8,128]{3,2,1,0:T(8,128)S(1)}, f32[2,16,8,128]{3,2,1,0:T(8,128)S(1)}, u32[]{:S(2)}, u32[]{:S(2)}) collective-permute-start(f32[2,16,8,128]{3,2,1,0:T(8,128)S(1)} %slice_select_fusion.16), channel_id=1, source_target_pairs={{0,1},{1,0},{2,3},{3,2},{4,5},{5,4},{6,7},{7,6},{8,9},{9,8},{10,11... | collective-permute-start | bytes 393224 | tf_op jit(solution)/shard_map/ppermute | solution.py:225
  109.1 2.0 %collective-permute-done.105.cut_right_ref = f32[2,4,8,128]{3,2,1,0:T(8,128)S(1)} collective-permute-done((f32[2,4,8,128]{3,2,1,0:T(8,128)S(1)}, f32[2,4,8,128]{3,2,1,0:T(8,128)S(1)}, u32[]{:S(2)}, u32[]{:S(2)}) %collective-permute-start.105) | collective-permute-done | bytes 32800 | tf_op jit(solution)/shard_map/ppermute | solution.py:227
  111.1 4.0 %collective-permute-done.104.cut_left_ref = f32[2,4,8,128]{3,2,1,0:T(8,128)S(1)} collective-permute-done((f32[2,4,8,128]{3,2,1,0:T(8,128)S(1)}, f32[2,4,8,128]{3,2,1,0:T(8,128)S(1)}, u32[]{:S(2)}, u32[]{:S(2)}) %collective-permute-start.104) | collective-permute-done | bytes 32800 | tf_op jit(solution)/shard_map/ppermute | solution.py:226
  115.2 1.8 %copy-done.3 = f32[2,24,112,128]{3,2,1,0:T(8,128)S(1)} copy-done((f32[2,24,112,128]{3,2,1,0:T(8,128)S(1)}, f32[2,24,112,128]{3,2,1,0:T(8,128)}, u32[]{:S(2)}) %copy-start.3) | copy-done | bytes 2752536
  116.9 1.8 %copy-done.5 = f32[2,24,112,128]{3,2,1,0:T(8,128)S(1)} copy-done((f32[2,24,112,128]{3,2,1,0:T(8,128)S(1)}, f32[2,24,112,128]{3,2,1,0:T(8,128)}, u32[]{:S(2)}) %copy-start.5) | copy-done | bytes 2752536
  118.7 17.1 %later_step.1 = f32[2,16,96,128]{3,2,1,0:T(8,128)} custom-call(s32[1]{0:T(128)} %bitcast.16.rad_ref, f32[24,128]{1,0:T(8,128)S(1)} %fusion.17.ghost_ref, f32[2,16,96,128]{3,2,1,0:T(8,128)S(1)} %get-tuple-element.241.p_ref, f32[2,24,112,128]{3,2,1,0:T(8,128)S(1)} %copy-done.3, f32[2,24,112,128]{3,2,1,0:T(8,128)S(1)} %copy-done.5, ...), custom_call_target="tpu_custom_call" | custom-call | tf_op jit(solution)/shard_map/later_step/pallas_call | solution.py:253
  (65 shorter events, 26.2 us)
Async XLA Ops:
  0.0 10.3 %copy-start.12 = (f32[2,16,96,128]{3,2,1,0:T(8,128)S(1)}, f32[2,16,96,128]{3,2,1,0:T(8,128)}, u32[]{:S(2)}) copy-start(f32[2,16,96,128]{3,2,1,0:T(8,128)} %p_ref.1) | copy-start | bytes 4718596
  1.1 10.0 %copy-start = (f32[2,16,96,128]{3,2,1,0:T(8,128)S(1)}, f32[2,16,96,128]{3,2,1,0:T(8,128)}, u32[]{:S(2)}) copy-start(f32[2,16,96,128]{3,2,1,0:T(8,128)} %s_ref.1) | copy-start | bytes 4718596
  3.2 55.0 %collective-permute-start.98 = (f32[3,2,16,8,128]{4,3,2,1,0:T(8,128)}, f32[3,2,16,8,128]{4,3,2,1,0:T(8,128)S(1)}, u32[]{:S(2)}, u32[]{:S(2)}) collective-permute-start(f32[3,2,16,8,128]{4,3,2,1,0:T(8,128)} %pad_maximum_fusion.2), channel_id=1, source_target_pairs={{0,1},{1,0},{2,3},{3,2},{4,5},{5,4},{6,7},{7,6},{8,9},{9,8},{10,11... | collective-permute-start | bytes 1179656 | tf_op jit(solution)/shard_map/ppermute | solution.py:225
  14.1 44.1 %collective-permute-start.96 = (f32[2,10,96,128]{3,2,1,0:T(8,128)}, f32[2,10,96,128]{3,2,1,0:T(8,128)S(1)}, u32[]{:S(2)}, u32[]{:S(2)}) collective-permute-start(f32[2,10,96,128]{3,2,1,0:T(8,128)} %pad_maximum_fusion), channel_id=1, source_target_pairs={{0,2},{2,4},{4,6},{6,8},{8,10},{10,12},{12,14},{14,16},{16,18},{18... | collective-permute-start | bytes 2949128 | tf_op jit(solution)/shard_map/ppermute | solution.py:223
  15.2 26.0 %copy-start.13 = (f32[2,4,96,128]{3,2,1,0:T(8,128)S(1)}, f32[2,4,96,128]{3,2,1,0:T(8,128)}, u32[]{:S(2)}) copy-start(f32[2,4,96,128]{3,2,1,0:T(8,128)} %get-tuple-element.249) | copy-start | bytes 1179652
  17.6 17.2 %collective-permute-start.59 = (f32[16,128]{1,0:T(8,128)S(1)}, f32[16,128]{1,0:T(8,128)}, u32[]{:S(2)}, u32[]{:S(2)}) collective-permute-start(f32[16,128]{1,0:T(8,128)S(1)} %fusion.3), channel_id=1, source_target_pairs={{29,0},{8,1},{31,2},{10,3},{1,4},{12,5},{3,6},{14,7},{5,8},{16,9},... | collective-permute-start | bytes 24584 | tf_op jit(solution)/shard_map/cond/branch_3_fun/ppermute | solution.py:189
  23.3 11.6 %collective-permute-start.58 = (f32[16,128]{1,0:T(8,128)S(1)}, f32[16,128]{1,0:T(8,128)}, u32[]{:S(2)}, u32[]{:S(2)}) collective-permute-start(f32[16,128]{1,0:T(8,128)S(1)} %fusion.3), channel_id=1, source_target_pairs={{27,0},{6,1},{29,2},{8,3},{31,4},{10,5},{1,6},{12,7},{3,8},{14,9},... | collective-permute-start | bytes 24584 | tf_op jit(solution)/shard_map/cond/branch_3_fun/ppermute | solution.py:189
  29.0 12.1 %collective-permute-start.57 = (f32[16,128]{1,0:T(8,128)S(1)}, f32[16,128]{1,0:T(8,128)}, u32[]{:S(2)}, u32[]{:S(2)}) collective-permute-start(f32[16,128]{1,0:T(8,128)S(1)} %fusion.3), channel_id=1, source_target_pairs={{25,0},{4,1},{27,2},{6,3},{29,4},{8,5},{31,6},{10,7},{1,8},{12,9},... | collective-permute-start | bytes 24584 | tf_op jit(solution)/shard_map/cond/branch_3_fun/ppermute | solution.py:189
  43.3 15.9 %collective-permute-start.97 = (f32[2,10,96,128]{3,2,1,0:T(8,128)}, f32[2,10,96,128]{3,2,1,0:T(8,128)}, u32[]{:S(2)}, u32[]{:S(2)}) collective-permute-start(f32[2,10,96,128]{3,2,1,0:T(8,128)} %pad_maximum_fusion.1), channel_id=1, source_target_pairs={{0,30},{2,0},{4,2},{6,4},{8,6},{10,8},{12,10},{14,12},{16,14},{18,... | collective-permute-start | bytes 2949128 | tf_op jit(solution)/shard_map/ppermute | solution.py:224
  47.4 7.6 %collective-permute-start.99 = (f32[2,10,8,128]{3,2,1,0:T(8,128)S(1)}, f32[2,10,8,128]{3,2,1,0:T(8,128)S(1)}, u32[]{:S(2)}, u32[]{:S(2)}) collective-permute-start(f32[2,10,8,128]{3,2,1,0:T(8,128)S(1)} %pad_maximum_fusion.3), channel_id=1, source_target_pairs={{0,3},{1,2},{2,5},{3,4},{4,7},{5,6},{6,9},{7,8},{8,11},{9,10},{10,... | collective-permute-start | bytes 245768 | tf_op jit(solution)/shard_map/ppermute | solution.py:226
  49.1 8.4 %collective-permute-start.100 = (f32[2,10,8,128]{3,2,1,0:T(8,128)S(1)}, f32[2,10,8,128]{3,2,1,0:T(8,128)S(1)}, u32[]{:S(2)}, u32[]{:S(2)}) collective-permute-start(f32[2,10,8,128]{3,2,1,0:T(8,128)S(1)} %pad_maximum_fusion.4), channel_id=1, source_target_pairs={{0,31},{1,30},{2,1},{3,0},{4,3},{5,2},{6,5},{7,4},{8,7},{9,6},{10,... | collective-permute-start | bytes 245768 | tf_op jit(solution)/shard_map/ppermute | solution.py:227
  59.1 1.4 %copy-start.1 = (f32[2,16,96,128]{3,2,1,0:T(8,128)S(1)}, f32[2,16,96,128]{3,2,1,0:T(8,128)}, u32[]{:S(2)}) copy-start(f32[2,16,96,128]{3,2,1,0:T(8,128)} %d_ref.1) | copy-start | bytes 4718596
  81.8 1.5 %copy-start.2 = (f32[2,24,112,128]{3,2,1,0:T(8,128)}, f32[2,24,112,128]{3,2,1,0:T(8,128)S(1)}, u32[]{:S(2)}) copy-start(f32[2,24,112,128]{3,2,1,0:T(8,128)S(1)} %get-tuple-element.245.weight) | copy-start | bytes 8257540
  83.4 1.6 %copy-start.4 = (f32[2,24,112,128]{3,2,1,0:T(8,128)}, f32[2,24,112,128]{3,2,1,0:T(8,128)S(1)}, u32[]{:S(2)}) copy-start(f32[2,24,112,128]{3,2,1,0:T(8,128)S(1)} %get-tuple-element.246.shift) | copy-start | bytes 8257540
  85.0 30.1 %collective-permute-start.102 = (f32[2,4,96,128]{3,2,1,0:T(8,128)S(1)}, f32[2,4,96,128]{3,2,1,0:T(8,128)S(1)}, u32[]{:S(2)}, u32[]{:S(2)}) collective-permute-start(f32[2,4,96,128]{3,2,1,0:T(8,128)S(1)} %get-tuple-element.247), channel_id=1, source_target_pairs={{0,30},{2,0},{4,2},{6,4},{8,6},{10,8},{12,10},{14,12},{16,14},{18,... | collective-permute-start | bytes 1179656 | tf_op jit(solution)/shard_map/ppermute | solution.py:224
  93.3 21.8 %collective-permute-start.101 = (f32[2,4,96,128]{3,2,1,0:T(8,128)S(1)}, f32[2,4,96,128]{3,2,1,0:T(8,128)S(1)}, u32[]{:S(2)}, u32[]{:S(2)}) collective-permute-start(f32[2,4,96,128]{3,2,1,0:T(8,128)S(1)} %get-tuple-element.248), channel_id=1, source_target_pairs={{0,2},{2,4},{4,6},{6,8},{8,10},{10,12},{12,14},{14,16},{16,18},{18... | collective-permute-start | bytes 1179656 | tf_op jit(solution)/shard_map/ppermute | solution.py:223
  93.8 9.0 %collective-permute-start.23 = (f32[16,128]{1,0:T(8,128)S(1)}, f32[16,128]{1,0:T(8,128)}, u32[]{:S(2)}, u32[]{:S(2)}) collective-permute-start(f32[16,128]{1,0:T(8,128)S(1)} %param.23), channel_id=1, source_target_pairs={{21,0},{16,1},{23,2},{18,3},{25,4},{20,5},{27,6},{22,7},{29,8},{24... | collective-permute-start | bytes 24584 | tf_op jit(solution)/shard_map/cond/branch_7_fun/ppermute | solution.py:189
  97.3 5.5 %collective-permute-start.22 = (f32[16,128]{1,0:T(8,128)S(1)}, f32[16,128]{1,0:T(8,128)}, u32[]{:S(2)}, u32[]{:S(2)}) collective-permute-start(f32[16,128]{1,0:T(8,128)S(1)} %param.23), channel_id=1, source_target_pairs={{19,0},{14,1},{21,2},{16,3},{23,4},{18,5},{25,6},{20,7},{27,8},{22... | collective-permute-start | bytes 24584 | tf_op jit(solution)/shard_map/cond/branch_7_fun/ppermute | solution.py:189
  99.1 5.6 %collective-permute-start.21 = (f32[16,128]{1,0:T(8,128)S(1)}, f32[16,128]{1,0:T(8,128)}, u32[]{:S(2)}, u32[]{:S(2)}) collective-permute-start(f32[16,128]{1,0:T(8,128)S(1)} %param.23), channel_id=1, source_target_pairs={{17,0},{12,1},{19,2},{14,3},{21,4},{16,5},{23,6},{18,7},{25,8},{20... | collective-permute-start | bytes 24584 | tf_op jit(solution)/shard_map/cond/branch_7_fun/ppermute | solution.py:189
  104.7 10.5 %collective-permute-start.103 = (f32[2,16,8,128]{3,2,1,0:T(8,128)S(1)}, f32[2,16,8,128]{3,2,1,0:T(8,128)S(1)}, u32[]{:S(2)}, u32[]{:S(2)}) collective-permute-start(f32[2,16,8,128]{3,2,1,0:T(8,128)S(1)} %slice_select_fusion.16), channel_id=1, source_target_pairs={{0,1},{1,0},{2,3},{3,2},{4,5},{5,4},{6,7},{7,6},{8,9},{9,8},{10,11... | collective-permute-start | bytes 393224 | tf_op jit(solution)/shard_map/ppermute | solution.py:225
  106.6 4.5 %collective-permute-start.105 = (f32[2,4,8,128]{3,2,1,0:T(8,128)S(1)}, f32[2,4,8,128]{3,2,1,0:T(8,128)S(1)}, u32[]{:S(2)}, u32[]{:S(2)}) collective-permute-start(f32[2,4,8,128]{3,2,1,0:T(8,128)S(1)} %get-tuple-element.255), channel_id=1, source_target_pairs={{0,31},{1,30},{2,1},{3,0},{4,3},{5,2},{6,5},{7,4},{8,7},{9,6},{10,... | collective-permute-start | bytes 98312 | tf_op jit(solution)/shard_map/ppermute | solution.py:227
  108.2 6.9 %collective-permute-start.104 = (f32[2,4,8,128]{3,2,1,0:T(8,128)S(1)}, f32[2,4,8,128]{3,2,1,0:T(8,128)S(1)}, u32[]{:S(2)}, u32[]{:S(2)}) collective-permute-start(f32[2,4,8,128]{3,2,1,0:T(8,128)S(1)} %get-tuple-element.256), channel_id=1, source_target_pairs={{0,3},{1,2},{2,5},{3,4},{4,7},{5,6},{6,9},{7,8},{8,11},{9,10},{10,... | collective-permute-start | bytes 98312 | tf_op jit(solution)/shard_map/ppermute | solution.py:226
  115.2 1.8 %copy-start.3 = (f32[2,24,112,128]{3,2,1,0:T(8,128)S(1)}, f32[2,24,112,128]{3,2,1,0:T(8,128)}, u32[]{:S(2)}) copy-start(f32[2,24,112,128]{3,2,1,0:T(8,128)} %copy-done.2) | copy-start | bytes 8257540
  116.9 1.8 %copy-start.5 = (f32[2,24,112,128]{3,2,1,0:T(8,128)S(1)}, f32[2,24,112,128]{3,2,1,0:T(8,128)}, u32[]{:S(2)}) copy-start(f32[2,24,112,128]{3,2,1,0:T(8,128)} %copy-done.4) | copy-start | bytes 8257540
  (8 other events, 6.9 us)

commit v2 on v0

v2 whole, which is shorter than its diff:
```python
import functools

import jax
import jax.numpy as jnp
from jax import lax
from jax.experimental import pallas as pl
from jax.experimental.pallas import tpu as pltpu
from jax.sharding import PartitionSpec as P

STEPS = 2
SWEEPS = 4
OMEGA = 0.8
TILE = 8
OWN = 2 * TILE
SLOTS = SWEEPS + 2


class Side:
    def __init__(self, low, radial_cells):
        end = OWN + radial_cells
        self.low = low
        self.own = slice(OWN, end)
        self.first = OWN if low else TILE
        self.count = radial_cells + TILE
        self.rows = slice(self.first, self.first + self.count)
        self.cut = slice(end, end + SWEEPS) if low else slice(OWN - SWEEPS, OWN)
        self.tile = slice(end, end + TILE) if low else slice(TILE, OWN)
        self.ghost = OWN - 1 if low else end
        self.edge = OWN if low else end - 1
        self.spare = self.count - 1 if low else 0
        self.facing = 1 if low else 0


def shifted(s, by):
    return slice(s.start + by, s.stop + by)


def axial_sum(x):
    lane = lax.broadcasted_iota(jnp.int32, x.shape, 1)
    last = x.shape[1] - 1
    return jnp.where(lane == 0, 0.0, pltpu.roll(x, 1, 1)) + jnp.where(
        lane == last, 0.0, pltpu.roll(x, last, 1)
    )


def relaxed(column, side, beside, weight, shift):
    here = column[side.rows]
    radial = column[shifted(side.rows, -1)] + column[shifted(side.rows, 1)]
    nbr = beside + radial + axial_sum(here)
    kept = (1.0 - OMEGA) * here
    if shift is not None:
        kept = kept + shift
    return kept + weight * nbr


def mirror(column, side):
    column[side.ghost : side.ghost + 1] = column[side.edge : side.edge + 1]


def on_each_side(rad_ref, radial_cells, body):
    @pl.when(rad_ref[0] == 0)
    def _():
        body(Side(True, radial_cells))

    @pl.when(rad_ref[0] != 0)
    def _():
        body(Side(False, radial_cells))


def copy_all(copies):
    for c in copies:
        c.start()
    for c in copies:
        c.wait()


def trajectories(side, field, other, weight, shift, messages):
    bufs = (field, other)
    for edge, message in enumerate(messages):

        def at(distance, n, edge=edge):
            return distance - 1 if edge == 0 else n - distance

        for k in range(2):
            facing = k == side.facing
            for sweep in range(SWEEPS):
                src, dst = bufs[sweep % 2], bufs[1 - sweep % 2]
                top = src.at[edge, k, at(1, SWEEPS)]
                message[k, sweep] = top[side.rows]
                for j in range(1, SWEEPS - sweep):
                    here = src.at[edge, k, at(j, SWEEPS)]
                    beside = src[edge, k, at(j + 1, SWEEPS), side.rows]
                    if j > 1:
                        beside = beside + src[edge, k, at(j - 1, SWEEPS), side.rows]
                    i = at(j, SWEEPS - 1)
                    new = relaxed(here, side, beside, weight[edge, k, i], shift[edge, k, i])
                    out = dst.at[edge, k, at(j, SWEEPS)]
                    out[side.rows] = new
                    if facing:
                        out[side.ghost : side.ghost + 1] = jnp.zeros((1, new.shape[1]), jnp.float32)
                    else:
                        mirror(out, side)
            if message.shape[1] == SWEEPS:
                continue
            message[k, SWEEPS] = weight[edge, k, at(1, SWEEPS - 1)]
            message[k, SWEEPS + 1] = weight[edge, k, at(2, SWEEPS - 1)]
            if facing:
                row = side.edge - side.first
                message[k, SWEEPS + 1, side.spare : side.spare + 1] = weight[
                    edge, k, at(3, SWEEPS - 1), row : row + 1
                ]


def level_ghosts(side, field):
    for edge in range(2):
        for k in range(2):
            for i in range(SWEEPS):
                column = field.at[edge, k, i]
                if k == side.facing:
                    column[side.ghost : side.ghost + 1] = jnp.zeros(
                        (1, column.shape[1]), jnp.float32
                    )
                else:
                    mirror(column, side)


def edges(known, rad_ref, p_ref, b_ref, w_ref, cut_ref, ghost_ref, last, first, *scratch):
    field, other, weight, shift, sems = scratch
    cells, radial_cells = p_ref.shape[1:3]
    n = SWEEPS - 1

    def body(side):
        inner = pl.ds(OWN, radial_cells)
        own = pl.ds(0, side.count) if known else pl.ds(OWN - side.first, radial_cells)
        copies = []
        for source, target, count, rows in (
            (p_ref, field, SWEEPS, inner),
            (b_ref, shift, n, own),
            (w_ref, weight, n, own),
        ):
            for edge in range(2):
                span = pl.ds(0 if edge == 0 else cells - count, count)
                copies.append(
                    pltpu.make_async_copy(
                        source.at[:, span], target.at[edge, :, :, rows, :], sems.at[len(copies)]
                    )
                )
        copy_all(copies)
        cut = shifted(side.cut, -side.first)
        for edge in range(2):
            for at, count, target, rows in (
                (0, SWEEPS, field, side.cut),
                (1, n, shift, cut),
                (2, n, weight, cut),
            )[: 1 if known else 3]:
                span = slice(0, count) if edge == 0 else slice(cells - count, cells)
                target[edge, :, :, rows, :] = cut_ref[at, :, span]
        if not known:
            for edge in range(2):
                for k in range(2):
                    for i in range(n):
                        w = OMEGA / (6.0 + weight[edge, k, i])
                        weight[edge, k, i] = w
                        shift[edge, k, i] = w * shift[edge, k, i]
        level_ghosts(side, field)
        trajectories(side, field, other, weight, shift, (first, last))
        for edge, message in enumerate((first, last)):
            for j in range(3):
                g = j if edge == 0 else cells - 1 - j
                message[side.facing, j, side.spare : side.spare + 1] = ghost_ref[g : g + 1]

    on_each_side(rad_ref, radial_cells, body)


def interior(known, rad_ref, p_ref, b_ref, w_ref, cut_ref, ghost_ref, *rest):
    if known:
        out_ref, stash, levels, last, weight, shift, sems = rest
    else:
        out_ref, stash, b_out, w_out, levels, last, weight, shift, sems = rest
    cells, radial_cells = p_ref.shape[1:3]

    def body(side):
        own = pl.ds(0, side.count) if known else pl.ds(OWN - side.first, radial_cells)
        copy_all(
            [
                pltpu.make_async_copy(
                    p_ref, levels.at[0, :, :, pl.ds(OWN, radial_cells), :], sems.at[0]
                ),
                pltpu.make_async_copy(b_ref, shift.at[:, :, own, :], sems.at[1]),
                pltpu.make_async_copy(w_ref, weight.at[:, :, own, :], sems.at[2]),
            ]
        )
        levels[0, :, :, side.cut, :] = cut_ref[0]
        pending = []
        if not known:
            cut = shifted(side.cut, -side.first)
            shift[:, :, cut, :] = cut_ref[1]
            weight[:, :, cut, :] = cut_ref[2]

            def invert(j, carry):
                for k in range(2):
                    w = OMEGA / (6.0 + weight[k, j])
                    weight[k, j] = w
                    shift[k, j] = w * shift[k, j]
                return carry

            lax.fori_loop(0, cells, invert, 0)
            pending += [
                pltpu.make_async_copy(shift, b_out, sems.at[1]),
                pltpu.make_async_copy(weight, w_out, sems.at[2]),
            ]
            for c in pending:
                c.start()
        for j in range(cells):
            mirror(levels.at[0, 1 - side.facing, j], side)
            for n in range(SWEEPS):
                levels[n, side.facing, j, side.ghost : side.ghost + 1] = ghost_ref[j : j + 1]
        for n in range(SWEEPS):
            final = n == SWEEPS - 1

            def step(j, carry, n=n, final=final):
                for k in range(2):
                    beside = levels[n, k, j - 1, side.rows] + levels[n, k, j + 1, side.rows]
                    new = relaxed(levels.at[n, k, j], side, beside, weight[k, j], shift[k, j])
                    if final:
                        at = OWN - side.first
                        last[k, j - SWEEPS] = new[at : at + radial_cells]
                    else:
                        levels[n + 1, k, j, side.rows] = new
                        if k != side.facing:
                            at = side.edge - side.first
                            levels[n + 1, k, j, side.ghost : side.ghost + 1] = new[at : at + 1]
                return carry

            lax.fori_loop(n + 1, cells - 1 - n, step, 0, unroll=2)
            if not final:
                for e, at in enumerate((n + 1, cells - 3 - n)):
                    pending.append(
                        pltpu.make_async_copy(
                            levels.at[n + 1, :, pl.ds(at, 2)],
                            stash.at[e, n],
                            sems.at[3 + 2 * n + e],
                        )
                    )
                    pending[-1].start()
        inner = pltpu.make_async_copy(
            last, out_ref.at[:, pl.ds(SWEEPS, cells - 2 * SWEEPS)], sems.at[0]
        )
        inner.start()
        pending.append(inner)
        for c in pending:
            c.wait()

    on_each_side(rad_ref, radial_cells, body)


def finish(known, rad_ref, p_ref, b_ref, w_ref, stash, cut_ref, ghost_ref, left_ref, right_ref, *rest):
    if known:
        left_w, right_w, _, out_ref, *rest = rest
    else:
        _, out_ref, *rest = rest
    levels, last, near, near2, weight, shift, moved, moved_w, sems = rest
    cells, radial_cells = p_ref.shape[1:3]
    width = SWEEPS + 2

    def at(e, distance):
        return distance if e == 0 else width - 1 - distance

    def body(side):
        facing = side.facing
        copies = []

        def fetch(source, target):
            copies.append(pltpu.make_async_copy(source, target, sems.at[len(copies)]))

        for e, message in enumerate((left_ref, right_ref)):
            fetch(message, moved.at[e])
            if known:
                fetch((left_w, right_w)[e].at[:, pl.ds(SWEEPS, 2)], moved_w.at[e])
            ends = pl.ds(0 if e == 0 else cells - SWEEPS, SWEEPS)
            fetch(b_ref.at[:, ends], shift.at[e])
            fetch(w_ref.at[:, ends], weight.at[e])
            fetch(
                p_ref.at[:, pl.ds(0 if e == 0 else cells - 2, 2)],
                levels.at[0, e, :, pl.ds(min(at(e, 1), at(e, 2)), 2), pl.ds(OWN, radial_cells), :],
            )
            for n in range(1, SWEEPS):
                fetch(
                    stash.at[e, n - 1],
                    levels.at[n, e, :, pl.ds(min(at(e, n + 1), at(e, n + 2)), 2)],
                )
        copy_all(copies)

        def weights(e, k, i):
            return moved_w[e, k, i] if known else moved[e, k, SWEEPS + i]

        lanes = levels.shape[-1]
        for e in range(2):
            for d in range(1, 3):
                column = d - 1 if e == 0 else cells - d
                for k in range(2):
                    target = levels.at[0, e, k, at(e, d)]
                    target[side.cut, :] = cut_ref[0, k, column]
                    if k != facing:
                        mirror(target, side)
            for d in range(1, SWEEPS):
                column = d - 1 if e == 0 else cells - d
                for n in range(SWEEPS):
                    if n >= d or (n == 0 and d < 3):
                        levels[n, e, facing, at(e, d), side.ghost : side.ghost + 1] = ghost_ref[
                            column : column + 1
                        ]
            beyond = [moved[e, facing, j, side.spare : side.spare + 1] for j in range(3)]
            for k in range(2):
                levels[0, e, k, at(e, 0), side.rows] = moved[e, k, 0]
                for buf in (near, near2):
                    for i in range(3):
                        buf[e, k, i] = jnp.zeros(buf.shape[3:], jnp.float32)
                        if k == facing and i < 2:
                            buf[e, k, i, side.ghost : side.ghost + 1] = beyond[i]
            w3 = (moved_w if known else moved)[
                e, facing, 1 if known else SWEEPS + 1, side.spare : side.spare + 1
            ]
            near2[e, facing, 2, side.edge : side.edge + 1] = w3 * beyond[2]
        nears = (near, near2)
        for n in range(SWEEPS):
            final = n == SWEEPS - 1
            src, dst = nears[n % 2], nears[1 - n % 2]
            for e in range(2):
                for k in range(2):
                    for d in range(1, n + 2):
                        i = d - 1 if e == 0 else SWEEPS - d
                        beside = (
                            levels[n, e, k, at(e, d - 1), side.rows]
                            + levels[n, e, k, at(e, d + 1), side.rows]
                        )
                        new = relaxed(
                            levels.at[n, e, k, at(e, d)],
                            side,
                            beside,
                            weight[e, k, i],
                            shift[e, k, i],
                        )
                        if final:
                            first = OWN - side.first
                            last[e, k, i] = new[first : first + radial_cells]
                        else:
                            levels[n + 1, e, k, at(e, d), side.rows] = new
                            if k != facing:
                                mirror(levels.at[n + 1, e, k, at(e, d)], side)
                    if final:
                        continue
                    beside = levels[n, e, k, at(e, 1), side.rows] + src[e, k, 1, side.rows]
                    new = relaxed(src.at[e, k, 0], side, beside, weights(e, k, 0), None)
                    dst[e, k, 0, side.rows] = new
                    levels[n + 1, e, k, at(e, 0), side.rows] = moved[e, k, n + 1] + new
                    if k != facing:
                        mirror(dst.at[e, k, 0], side)
                    if n < SWEEPS - 2:
                        beside = src[e, k, 0, side.rows] + src[e, k, 2, side.rows]
                        new = relaxed(src.at[e, k, 1], side, beside, weights(e, k, 1), None)
                        dst[e, k, 1, side.rows] = new
                        if k != facing:
                            mirror(dst.at[e, k, 1], side)
        copy_all(
            [
                pltpu.make_async_copy(
                    last.at[e],
                    out_ref.at[:, pl.ds(0 if e == 0 else cells - SWEEPS, SWEEPS)],
                    sems.at[e],
                )
                for e in range(2)
            ]
        )

    on_each_side(rad_ref, radial_cells, body)


def ring(size, step):
    return [(i, (i + step) % size) for i in range(size)]


def facing_pairs(size, turn, k):
    pairs = []
    for i in range(size):
        pairs.append((2 * ((i - turn - 1 + k) % size) + 1, 2 * i))
        pairs.append((2 * ((i + turn + k) % size), 2 * i + 1))
    return pairs


def far_pairs(size, turn):
    return [(2 * i + r, 2 * ((i + (2 * r - 1) * turn) % size) + r) for i in range(size) for r in range(2)]


def facing_cells(edge, offset, radial_index):
    size = lax.axis_size("az")
    cells = edge.shape[0]
    turn, rest = offset // cells, offset % cells
    near = min(size, 16)

    def far(t):
        return lambda e: lax.ppermute(e, ("az", "rad"), far_pairs(size, t * near))

    def branch(t):
        return lambda e: tuple(
            lax.ppermute(e, ("az", "rad"), facing_pairs(size, t, k)) for k in range(2)
        )

    if size > near:
        edge = lax.switch(turn // near, [far(t) for t in range(-(-size // near))], edge)
    blocks = lax.switch(turn % near, [branch(t) for t in range(near)], edge)
    start = jnp.where(radial_index == 0, cells - rest, rest)
    return lax.dynamic_slice_in_dim(jnp.concatenate(blocks, axis=0), start, cells, 0)


def per_device(pressure, source, diagonal, rot_offset):
    _, cells, radial_cells, lanes = pressure.shape
    size = lax.axis_size("az")
    radial_index = lax.axis_index("rad")
    rad = radial_index.astype(jnp.int32).reshape(1)
    rows, span = radial_cells + 4 * TILE, radial_cells + TILE

    def array(*shape):
        return jax.ShapeDtypeStruct(shape, jnp.float32)

    def scratch(*shape):
        return pltpu.VMEM(shape, jnp.float32)

    own = array(*pressure.shape)
    kept = array(2, cells, span, lanes)
    stash = array(2, SWEEPS - 1, 2, 2, rows, lanes)
    vmem = pl.BlockSpec(memory_space=pltpu.VMEM)
    smem = pl.BlockSpec(memory_space=pltpu.SMEM)
    hbm = pl.BlockSpec(memory_space=pltpu.HBM)

    def call(kernel, known, out_shape, in_specs, out_specs, scratch_shapes, operands, cells_done, **more):
        work = 2 * cells_done * span * lanes
        return pl.pallas_call(
            functools.partial(kernel, known),
            out_shape=out_shape,
            in_specs=in_specs,
            out_specs=out_specs,
            scratch_shapes=scratch_shapes,
            compiler_params=pltpu.CompilerParams(vmem_limit_bytes=40 << 20),
            cost_estimate=pl.CostEstimate(
                flops=12 * work, bytes_accessed=8 * work, transcendentals=0
            ),
            name=kernel.__name__,
            **more,
        )(*operands)

    def swap_cut(arrays):
        cuts = [
            jnp.where(radial_index == 0, x[:, :, radial_cells - SWEEPS :], x[:, :, :SWEEPS])
            for x in arrays
        ]
        return jnp.stack(cuts)

    fields = (pressure, source, diagonal)
    for step in range(1, STEPS + 1):
        known = step > 1
        p = fields[0]
        edge = jnp.where(radial_index == 0, p[1, :, 0, :], p[0, :, radial_cells - 1, :])
        cut = swap_cut(fields[:1] if known else fields)
        edge, cut = lax.optimization_barrier((edge, cut))
        cut = lax.ppermute(cut, "rad", [(0, 1), (1, 0)])
        offset = rot_offset[0] * step % (cells * size)
        ghost = facing_cells(edge, offset, radial_index)
        operands = (rad, *fields, cut, ghost)
        specs = [smem] + [hbm] * 3 + [vmem] * 2
        message = array(2, SWEEPS if known else SLOTS, span, lanes)
        last, first = call(
            edges,
            known,
            (message, message),
            specs,
            [vmem] * 2,
            [
                scratch(2, 2, SWEEPS, rows, lanes),
                scratch(2, 2, SWEEPS, rows, lanes),
                scratch(2, 2, SWEEPS - 1, span, lanes),
                scratch(2, 2, SWEEPS - 1, span, lanes),
                pltpu.SemaphoreType.DMA((6,)),
            ],
            operands,
            12,
        )
        left = lax.ppermute(last, "az", ring(size, 1))
        right = lax.ppermute(first, "az", ring(size, -1))
        inner, saved, *made = call(
            interior,
            known,
            (own, stash) if known else (own, stash, kept, kept),
            specs,
            [hbm] * (2 if known else 4),
            [
                scratch(SWEEPS, 2, cells, rows, lanes),
                scratch(2, cells - 2 * SWEEPS, radial_cells, lanes),
                scratch(*kept.shape),
                scratch(*kept.shape),
                pltpu.SemaphoreType.DMA((9,)),
            ],
            operands,
            44,
        )
        if not known:
            shift, weight = made
            beyond = (left, right)
        operands = (rad, p, shift, weight, saved, cut, ghost, left, right)
        specs = [smem] + [hbm] * 4 + [vmem] * 2 + [hbm] * 2
        if known:
            operands += beyond
            specs += [hbm] * 2
        pressure = call(
            finish,
            known,
            own,
            specs + [hbm],
            hbm,
            [
                scratch(SWEEPS, 2, 2, SWEEPS + 2, rows, lanes),
                scratch(2, 2, SWEEPS, radial_cells, lanes),
                scratch(2, 2, 3, rows, lanes),
                scratch(2, 2, 3, rows, lanes),
                scratch(2, 2, SWEEPS, span, lanes),
                scratch(2, 2, SWEEPS, span, lanes),
                scratch(2, *message.shape),
                scratch(2, 2, 2, span, lanes),
                pltpu.SemaphoreType.DMA((16,)),
            ],
            (*operands, inner),
            26,
            input_output_aliases={len(operands): 0},
        )
        fields = (pressure, shift, weight)
    return pressure


def solution(mesh):
    placed = (
        P(None, "az", "rad", None),
        P(None, "az", "rad", None),
        P(None, "az", "rad", None),
        P(),
    )
    return jax.shard_map(
        per_device,
        mesh=mesh,
        in_specs=placed,
        out_specs=P(None, "az", "rad", None),
        check_vma=False,
    )
```

time: 168 us -> 73.6 us (0.44)
  the two profiles are of different devices: /device:TPU:0 before, /device:TPU:1 now
where the time goes in v2:
time: 73.6 us
  Pallas kernels  23.6 us (32%)
  waiting for transfers between devices  19 us (26%)
  starting transfers between devices  13.4 us (18%)
  local copies, waits for them, and re-layouts  12 us (16%)
  other arithmetic  4.52 us (6%)
  between operations  1.05 us (1%)
    pallas_call x6, Pallas kernels, call(): pl.pallas_call(functools.partial(kernel, known), out_shape=out_shape, in_...  23.6 us
    unnamed x22, local copies, waits for them, and re-layouts  12 us
    ppermute x4, starting transfers between devices, branch(): lax.ppermute(e, ('az', 'rad'), facing_pairs(size, t, k))  7.77 us
    ppermute x4, waiting for transfers between devices, branch(): lax.ppermute(e, ('az', 'rad'), facing_pairs(size, t, k))  7.26 us
    ppermute x2, waiting for transfers between devices, per_device(): left = lax.ppermute(last, 'az', ring(size, 1))  7.16 us
    ppermute x2, waiting for transfers between devices, per_device(): right = lax.ppermute(first, 'az', ring(size, -1))  4.6 us
    ppermute x2, starting transfers between devices, per_device(): left = lax.ppermute(last, 'az', ring(size, 1))  3.47 us
    another operation x4, other arithmetic, swap_cut(): return jnp.stack(cuts)  2.2 us
  transfers between devices with their start and end apart: 10, of which 7 were waited for; matrix products, arithmetic and copies ran while one was open for 2% of the time, Pallas kernels for 16%

profile of v2, /device:TPU:1, one launch (start us, length us, event | category | flops | bytes accessed | tf_op | source)
XLA Modules:
  0.0 73.6 jit_solution(5266957889628621342)
XLA Ops:
  3.1 2.1 %collective-permute-start.64 = (f32[3,2,16,4,128]{4,3,2,1,0:T(4,128)S(1)}, f32[3,2,16,4,128]{4,3,2,1,0:T(4,128)S(1)}, u32[]{:S(2)}, u32[]{:S(2)}) collective-permute-start(f32[3,2,16,4,128]{4,3,2,1,0:T(4,128)S(1)} %pad_maximum_fusion), channel_id=1, source_target_pairs={{0,1},{1,0},{2,3},{3,2},{4,5},{5,4},{6,7},{7,6},{8,9},{9,8},{10,11... | collective-permute-start | bytes 589832 | tf_op jit(solution)/shard_map/ppermute | solution.py:466
  5.9 10.1 %conditional.2 = (f32[16,128]{1,0:T(8,128)}, f32[16,128]{1,0:T(8,128)}) conditional(s32[]{:T(128)} %clamp.6, f32[16,128]{1,0:T(8,128)S(1)} %bitcast.16, f32[16,128]{1,0:T(8,128)S(1)} %bitcast.17, f32[16,128]{1,0:T(8,128)S(1)} %bitcast.18, f32[16,128]{1,0:T(8,128)S(1)} %bitcast.19, ...), branch_computations={%region_0.1_spmd, %region_1.2_spmd, %region_2.3_spmd, %region_3.4_... | conditional | bytes 65632 | solution.py:411
  6.0 4.2 %collective-permute-start.9 = (f32[16,128]{1,0:T(8,128)S(1)}, f32[16,128]{1,0:T(8,128)}, u32[]{:S(2)}, u32[]{:S(2)}) collective-permute-start(f32[16,128]{1,0:T(8,128)S(1)} %param.4), channel_id=1, source_target_pairs={{25,0},{10,1},{27,2},{12,3},{29,4},{14,5},{31,6},{16,7},{1,8},{18,... | collective-permute-start | bytes 24584 | tf_op jit(solution)/shard_map/cond/branch_4_fun/ppermute | solution.py:406
  11.3 4.7 %collective-permute-done.8 = f32[16,128]{1,0:T(8,128)} collective-permute-done((f32[16,128]{1,0:T(8,128)S(1)}, f32[16,128]{1,0:T(8,128)}, u32[]{:S(2)}, u32[]{:S(2)}) %collective-permute-start.8) | collective-permute-done | bytes 8224 | tf_op jit(solution)/shard_map/cond/branch_4_fun/ppermute | solution.py:406
  16.7 1.5 %copy-done.2 = f32[2,16,96,128]{3,2,1,0:T(8,128)S(1)} copy-done((f32[2,16,96,128]{3,2,1,0:T(8,128)S(1)}, f32[2,16,96,128]{3,2,1,0:T(8,128)}, u32[]{:S(2)}) %copy-start.2) | copy-done | bytes 1572888
  18.2 1.4 %copy-done.4 = f32[2,16,96,128]{3,2,1,0:T(8,128)S(1)} copy-done((f32[2,16,96,128]{3,2,1,0:T(8,128)S(1)}, f32[2,16,96,128]{3,2,1,0:T(8,128)}, u32[]{:S(2)}) %copy-start.4) | copy-done | bytes 1572888
  19.6 1.4 %copy-done.6 = f32[2,16,96,128]{3,2,1,0:T(8,128)S(1)} copy-done((f32[2,16,96,128]{3,2,1,0:T(8,128)S(1)}, f32[2,16,96,128]{3,2,1,0:T(8,128)}, u32[]{:S(2)}) %copy-start.6) | copy-done | bytes 1572888
  21.0 2.2 %edges.2 = (f32[2,6,104,128]{3,2,1,0:T(8,128)}, f32[2,6,104,128]{3,2,1,0:T(8,128)}) custom-call(s32[1]{0:T(128)} %bitcast.rad_ref, f32[2,16,96,128]{3,2,1,0:T(8,128)S(1)} %copy-done.2, f32[2,16,96,128]{3,2,1,0:T(8,128)S(1)} %copy-done.4, f32[2,16,96,128]{3,2,1,0:T(8,128)S(1)} %copy-done.6, f32[3,2,16,4,128]{4,3,2,1,0:T(4,128)S(1)} %collective-permute-done.64.cut_ref, ...), custom_call_target="tpu_custom_call" | custom-call | flops 3833856 | bytes 2555904 | tf_op jit(solution)/shard_map/edges/pallas_call | solution.py:438
  23.2 1.6 %collective-permute-start.65 = (f32[2,6,104,128]{3,2,1,0:T(8,128)}, f32[2,6,104,128]{3,2,1,0:T(8,128)}, u32[]{:S(2)}, u32[]{:S(2)}) collective-permute-start(f32[2,6,104,128]{3,2,1,0:T(8,128)} %get-tuple-element.62), channel_id=1, source_target_pairs={{0,2},{2,4},{4,6},{6,8},{8,10},{10,12},{12,14},{14,16},{16,18},{18... | collective-permute-start | bytes 1916936 | tf_op jit(solution)/shard_map/ppermute | solution.py:488
  24.8 1.4 %copy-done.3 = f32[2,16,96,128]{3,2,1,0:T(8,128)S(1)} copy-done((f32[2,16,96,128]{3,2,1,0:T(8,128)S(1)}, f32[2,16,96,128]{3,2,1,0:T(8,128)}, u32[]{:S(2)}) %copy-start.3) | copy-done | bytes 1572888
  26.2 1.4 %copy-done.5 = f32[2,16,96,128]{3,2,1,0:T(8,128)S(1)} copy-done((f32[2,16,96,128]{3,2,1,0:T(8,128)S(1)}, f32[2,16,96,128]{3,2,1,0:T(8,128)}, u32[]{:S(2)}) %copy-start.5) | copy-done | bytes 1572888
  27.6 1.4 %copy-done.7 = f32[2,16,96,128]{3,2,1,0:T(8,128)S(1)} copy-done((f32[2,16,96,128]{3,2,1,0:T(8,128)S(1)}, f32[2,16,96,128]{3,2,1,0:T(8,128)}, u32[]{:S(2)}) %copy-start.7) | copy-done | bytes 1572888
  30.0 5.8 %interior.2 = (f32[2,16,96,128]{3,2,1,0:T(8,128)S(1)}, f32[2,3,2,2,128,128]{5,4,3,2,1,0:T(8,128)S(1)}, f32[2,16,104,128]{3,2,1,0:T(8,128)S(1)}, f32[2,16,104,128]{3,2,1,0:T(8,128)S(1)}) custom-call(s32[1]{0:T(128)} %bitcast.rad_ref, f32[2,16,96,128]{3,2,1,0:T(8,128)S(1)} %copy-done.3, f32[2,16,96,128]{3,2,1,0:T(8,128)S(1)} %copy-done.5, ...), custom_call_target="tpu_custom_call" | custom-call | flops 14057472 | bytes 9371648 | tf_op jit(solution)/shard_map/interior/pallas_call | solution.py:438
  35.8 3.5 %collective-permute-done.65.left_ref.rest_0_ = f32[2,6,104,128]{3,2,1,0:T(8,128)} collective-permute-done((f32[2,6,104,128]{3,2,1,0:T(8,128)}, f32[2,6,104,128]{3,2,1,0:T(8,128)}, u32[]{:S(2)}, u32[]{:S(2)}) %collective-permute-start.65) | collective-permute-done | bytes 639008 | tf_op jit(solution)/shard_map/ppermute | solution.py:488
  39.3 2.4 %collective-permute-done.66.right_ref.rest_1_ = f32[2,6,104,128]{3,2,1,0:T(8,128)} collective-permute-done((f32[2,6,104,128]{3,2,1,0:T(8,128)}, f32[2,6,104,128]{3,2,1,0:T(8,128)}, u32[]{:S(2)}, u32[]{:S(2)}) %collective-permute-start.66) | collective-permute-done | bytes 639008 | tf_op jit(solution)/shard_map/ppermute | solution.py:489
  41.8 3.8 %finish.2.p_ref = f32[2,16,96,128]{3,2,1,0:T(8,128)S(1)} custom-call(s32[1]{0:T(128)} %bitcast.rad_ref, f32[2,16,96,128]{3,2,1,0:T(8,128)S(1)} %copy-done.3, f32[2,16,104,128]{3,2,1,0:T(8,128)S(1)} %get-tuple-element.59.b_ref, f32[2,16,104,128]{3,2,1,0:T(8,128)S(1)} %get-tuple-element.60.w_ref, ...), custom_call_target="tpu_custom_call", output_to_operand_aliasing={{}: (9, {})} | custom-call | flops 8306688 | bytes 5537792 | tf_op jit(solution)/shard_map/finish/pallas_call | solution.py:438
  46.8 5.0 %conditional.3 = (f32[16,128]{1,0:T(8,128)}, f32[16,128]{1,0:T(8,128)}) conditional(s32[]{:T(128)} %clamp.7, f32[16,128]{1,0:T(8,128)S(1)} %bitcast.32, f32[16,128]{1,0:T(8,128)S(1)} %bitcast.33, f32[16,128]{1,0:T(8,128)S(1)} %bitcast.34, f32[16,128]{1,0:T(8,128)S(1)} %bitcast.35, ...), branch_computations={%region_16.17_spmd, %region_17.18_spmd, %region_18.19_spmd, %regio... | conditional | bytes 65632 | solution.py:411
  46.8 3.5 %collective-permute-start.50 = (f32[16,128]{1,0:T(8,128)S(1)}, f32[16,128]{1,0:T(8,128)}, u32[]{:S(2)}, u32[]{:S(2)}) collective-permute-start(f32[16,128]{1,0:T(8,128)S(1)} %param.25), channel_id=1, source_target_pairs={{13,0},{18,1},{15,2},{20,3},{17,4},{22,5},{19,6},{24,7},{21,8},{26... | collective-permute-start | bytes 24584 | tf_op jit(solution)/shard_map/cond/branch_9_fun/ppermute | solution.py:406
  50.3 1.4 %collective-permute-done.51 = f32[16,128]{1,0:T(8,128)} collective-permute-done((f32[16,128]{1,0:T(8,128)S(1)}, f32[16,128]{1,0:T(8,128)}, u32[]{:S(2)}, u32[]{:S(2)}) %collective-permute-start.51) | collective-permute-done | bytes 8224 | tf_op jit(solution)/shard_map/cond/branch_9_fun/ppermute | solution.py:406
  55.1 1.9 %collective-permute-start.68 = (f32[2,4,104,128]{3,2,1,0:T(8,128)S(1)}, f32[2,4,104,128]{3,2,1,0:T(8,128)S(1)}, u32[]{:S(2)}, u32[]{:S(2)}) collective-permute-start(f32[2,4,104,128]{3,2,1,0:T(8,128)S(1)} %get-tuple-element.70), channel_id=1, source_target_pairs={{0,2},{2,4},{4,6},{6,8},{8,10},{10,12},{12,14},{14,16},{16,18},{18... | collective-permute-start | bytes 1277960 | tf_op jit(solution)/shard_map/ppermute | solution.py:488
  57.0 6.0 %interior.3 = (f32[2,16,96,128]{3,2,1,0:T(8,128)}, f32[2,3,2,2,128,128]{5,4,3,2,1,0:T(8,128)S(1)}) custom-call(s32[1]{0:T(128)} %bitcast.rad_ref, f32[2,16,96,128]{3,2,1,0:T(8,128)S(1)} %copy-done.1, f32[2,16,104,128]{3,2,1,0:T(8,128)S(1)} %get-tuple-element.59.b_ref, f32[2,16,104,128]{3,2,1,0:T(8,128)S(1)} %get-tuple-element.60.w_ref, ...), custom_call_target="tpu_custom_call" | custom-call | flops 14057472 | bytes 9371648 | tf_op jit(solution)/shard_map/interior/pallas_call | solution.py:438
  63.0 3.6 %collective-permute-done.68.left_ref = f32[2,4,104,128]{3,2,1,0:T(8,128)S(1)} collective-permute-done((f32[2,4,104,128]{3,2,1,0:T(8,128)S(1)}, f32[2,4,104,128]{3,2,1,0:T(8,128)S(1)}, u32[]{:S(2)}, u32[]{:S(2)}) %collective-permute-start.68) | collective-permute-done | bytes 426016 | tf_op jit(solution)/shard_map/ppermute | solution.py:488
  66.7 2.2 %collective-permute-done.69.right_ref = f32[2,4,104,128]{3,2,1,0:T(8,128)S(1)} collective-permute-done((f32[2,4,104,128]{3,2,1,0:T(8,128)S(1)}, f32[2,4,104,128]{3,2,1,0:T(8,128)S(1)}, u32[]{:S(2)}, u32[]{:S(2)}) %collective-permute-start.69) | collective-permute-done | bytes 426016 | tf_op jit(solution)/shard_map/ppermute | solution.py:489
  68.8 4.6 %finish.3 = f32[2,16,96,128]{3,2,1,0:T(8,128)} custom-call(s32[1]{0:T(128)} %bitcast.rad_ref, f32[2,16,96,128]{3,2,1,0:T(8,128)S(1)} %copy-done.1, f32[2,16,104,128]{3,2,1,0:T(8,128)S(1)} %get-tuple-element.59.b_ref, f32[2,16,104,128]{3,2,1,0:T(8,128)S(1)} %get-tuple-element.60.w_ref, ...), custom_call_target="tpu_custom_call", output_to_operand_aliasing={{}: (11, {})} | custom-call | flops 8306688 | bytes 5537792 | tf_op jit(solution)/shard_map/finish/pallas_call | solution.py:438
  (34 shorter events, 10.5 us)
Async XLA Ops:
  3.1 13.6 %collective-permute-start.64 = (f32[3,2,16,4,128]{4,3,2,1,0:T(4,128)S(1)}, f32[3,2,16,4,128]{4,3,2,1,0:T(4,128)S(1)}, u32[]{:S(2)}, u32[]{:S(2)}) collective-permute-start(f32[3,2,16,4,128]{4,3,2,1,0:T(4,128)S(1)} %pad_maximum_fusion), channel_id=1, source_target_pairs={{0,1},{1,0},{2,3},{3,2},{4,5},{5,4},{6,7},{7,6},{8,9},{9,8},{10,11... | collective-permute-start | bytes 589832 | tf_op jit(solution)/shard_map/ppermute | solution.py:466
  6.0 5.4 %collective-permute-start.9 = (f32[16,128]{1,0:T(8,128)S(1)}, f32[16,128]{1,0:T(8,128)}, u32[]{:S(2)}, u32[]{:S(2)}) collective-permute-start(f32[16,128]{1,0:T(8,128)S(1)} %param.4), channel_id=1, source_target_pairs={{25,0},{10,1},{27,2},{12,3},{29,4},{14,5},{31,6},{16,7},{1,8},{18,... | collective-permute-start | bytes 24584 | tf_op jit(solution)/shard_map/cond/branch_4_fun/ppermute | solution.py:406
  10.1 5.9 %collective-permute-start.8 = (f32[16,128]{1,0:T(8,128)S(1)}, f32[16,128]{1,0:T(8,128)}, u32[]{:S(2)}, u32[]{:S(2)}) collective-permute-start(f32[16,128]{1,0:T(8,128)S(1)} %param.4), channel_id=1, source_target_pairs={{23,0},{8,1},{25,2},{10,3},{27,4},{12,5},{29,6},{14,7},{31,8},{16,... | collective-permute-start | bytes 24584 | tf_op jit(solution)/shard_map/cond/branch_4_fun/ppermute | solution.py:406
  16.7 6.5 %copy-start.8 = (f32[3,2,16,4,128]{4,3,2,1,0:T(4,128)}, f32[3,2,16,4,128]{4,3,2,1,0:T(4,128)S(1)}, u32[]{:S(2)}) copy-start(f32[3,2,16,4,128]{4,3,2,1,0:T(4,128)S(1)} %collective-permute-done.64.cut_ref) | copy-start | bytes 589828
  16.7 1.5 %copy-start.2 = (f32[2,16,96,128]{3,2,1,0:T(8,128)S(1)}, f32[2,16,96,128]{3,2,1,0:T(8,128)}, u32[]{:S(2)}) copy-start(f32[2,16,96,128]{3,2,1,0:T(8,128)} %p_ref.5) | copy-start | bytes 4718596
  18.2 1.4 %copy-start.4 = (f32[2,16,96,128]{3,2,1,0:T(8,128)S(1)}, f32[2,16,96,128]{3,2,1,0:T(8,128)}, u32[]{:S(2)}) copy-start(f32[2,16,96,128]{3,2,1,0:T(8,128)} %b_ref.3) | copy-start | bytes 4718596
  19.6 1.4 %copy-start.6 = (f32[2,16,96,128]{3,2,1,0:T(8,128)S(1)}, f32[2,16,96,128]{3,2,1,0:T(8,128)}, u32[]{:S(2)}) copy-start(f32[2,16,96,128]{3,2,1,0:T(8,128)} %w_ref.3) | copy-start | bytes 4718596
  23.2 16.1 %collective-permute-start.65 = (f32[2,6,104,128]{3,2,1,0:T(8,128)}, f32[2,6,104,128]{3,2,1,0:T(8,128)}, u32[]{:S(2)}, u32[]{:S(2)}) collective-permute-start(f32[2,6,104,128]{3,2,1,0:T(8,128)} %get-tuple-element.62), channel_id=1, source_target_pairs={{0,2},{2,4},{4,6},{6,8},{8,10},{10,12},{12,14},{14,16},{16,18},{18... | collective-permute-start | bytes 1916936 | tf_op jit(solution)/shard_map/ppermute | solution.py:488
  24.8 17.0 %collective-permute-start.66 = (f32[2,6,104,128]{3,2,1,0:T(8,128)}, f32[2,6,104,128]{3,2,1,0:T(8,128)}, u32[]{:S(2)}, u32[]{:S(2)}) collective-permute-start(f32[2,6,104,128]{3,2,1,0:T(8,128)} %get-tuple-element.63), channel_id=1, source_target_pairs={{0,30},{2,0},{4,2},{6,4},{8,6},{10,8},{12,10},{14,12},{16,14},{18,... | collective-permute-start | bytes 1916936 | tf_op jit(solution)/shard_map/ppermute | solution.py:489
  24.8 1.4 %copy-start.3 = (f32[2,16,96,128]{3,2,1,0:T(8,128)S(1)}, f32[2,16,96,128]{3,2,1,0:T(8,128)}, u32[]{:S(2)}) copy-start(f32[2,16,96,128]{3,2,1,0:T(8,128)} %p_ref.5) | copy-start | bytes 4718596
  26.2 1.4 %copy-start.5 = (f32[2,16,96,128]{3,2,1,0:T(8,128)S(1)}, f32[2,16,96,128]{3,2,1,0:T(8,128)}, u32[]{:S(2)}) copy-start(f32[2,16,96,128]{3,2,1,0:T(8,128)} %b_ref.3) | copy-start | bytes 4718596
  27.6 1.4 %copy-start.7 = (f32[2,16,96,128]{3,2,1,0:T(8,128)S(1)}, f32[2,16,96,128]{3,2,1,0:T(8,128)}, u32[]{:S(2)}) copy-start(f32[2,16,96,128]{3,2,1,0:T(8,128)} %w_ref.3) | copy-start | bytes 4718596
  29.1 0.9 %copy-start.9 = (f32[3,2,16,4,128]{4,3,2,1,0:T(4,128)S(1)}, f32[3,2,16,4,128]{4,3,2,1,0:T(4,128)}, u32[]{:S(2)}) copy-start(f32[3,2,16,4,128]{4,3,2,1,0:T(4,128)} %copy-done.8) | copy-start | bytes 589828
  30.0 11.8 %copy-start.10 = (f32[3,2,16,4,128]{4,3,2,1,0:T(4,128)S(1)}, f32[3,2,16,4,128]{4,3,2,1,0:T(4,128)}, u32[]{:S(2)}) copy-start(f32[3,2,16,4,128]{4,3,2,1,0:T(4,128)} %copy-done.8) | copy-start | bytes 589828
  45.6 1.1 %copy-start = (f32[2,16,96,128]{3,2,1,0:T(8,128)}, f32[2,16,96,128]{3,2,1,0:T(8,128)S(1)}, u32[]{:S(2)}) copy-start(f32[2,16,96,128]{3,2,1,0:T(8,128)S(1)} %finish.2.p_ref) | copy-start | bytes 4718596
  46.8 5.7 %collective-permute-start.67 = (f32[1,2,16,4,128]{4,3,2,1,0:T(4,128)S(1)}, f32[1,2,16,4,128]{4,3,2,1,0:T(4,128)S(1)}, u32[]{:S(2)}, u32[]{:S(2)}) collective-permute-start(f32[1,2,16,4,128]{4,3,2,1,0:T(4,128)S(1)} %fusion), channel_id=1, source_target_pairs={{0,1},{1,0},{2,3},{3,2},{4,5},{5,4},{6,7},{7,6},{8,9},{9,8},{10,11... | collective-permute-start | bytes 196616 | tf_op jit(solution)/shard_map/ppermute | solution.py:466
  46.8 5.0 %collective-permute-start.51 = (f32[16,128]{1,0:T(8,128)S(1)}, f32[16,128]{1,0:T(8,128)}, u32[]{:S(2)}, u32[]{:S(2)}) collective-permute-start(f32[16,128]{1,0:T(8,128)S(1)} %param.25), channel_id=1, source_target_pairs={{15,0},{20,1},{17,2},{22,3},{19,4},{24,5},{21,6},{26,7},{23,8},{28... | collective-permute-start | bytes 24584 | tf_op jit(solution)/shard_map/cond/branch_9_fun/ppermute | solution.py:406
  46.8 5.0 %collective-permute-start.50 = (f32[16,128]{1,0:T(8,128)S(1)}, f32[16,128]{1,0:T(8,128)}, u32[]{:S(2)}, u32[]{:S(2)}) collective-permute-start(f32[16,128]{1,0:T(8,128)S(1)} %param.25), channel_id=1, source_target_pairs={{13,0},{18,1},{15,2},{20,3},{17,4},{22,5},{19,6},{24,7},{21,8},{26... | collective-permute-start | bytes 24584 | tf_op jit(solution)/shard_map/cond/branch_9_fun/ppermute | solution.py:406
  52.5 1.4 %copy-start.1 = (f32[2,16,96,128]{3,2,1,0:T(8,128)S(1)}, f32[2,16,96,128]{3,2,1,0:T(8,128)}, u32[]{:S(2)}) copy-start(f32[2,16,96,128]{3,2,1,0:T(8,128)} %copy-done) | copy-start | bytes 4718596
  55.1 11.5 %collective-permute-start.68 = (f32[2,4,104,128]{3,2,1,0:T(8,128)S(1)}, f32[2,4,104,128]{3,2,1,0:T(8,128)S(1)}, u32[]{:S(2)}, u32[]{:S(2)}) collective-permute-start(f32[2,4,104,128]{3,2,1,0:T(8,128)S(1)} %get-tuple-element.70), channel_id=1, source_target_pairs={{0,2},{2,4},{4,6},{6,8},{8,10},{10,12},{12,14},{14,16},{16,18},{18... | collective-permute-start | bytes 1277960 | tf_op jit(solution)/shard_map/ppermute | solution.py:488
  57.0 11.8 %collective-permute-start.69 = (f32[2,4,104,128]{3,2,1,0:T(8,128)S(1)}, f32[2,4,104,128]{3,2,1,0:T(8,128)S(1)}, u32[]{:S(2)}, u32[]{:S(2)}) collective-permute-start(f32[2,4,104,128]{3,2,1,0:T(8,128)S(1)} %get-tuple-element.71), channel_id=1, source_target_pairs={{0,30},{2,0},{4,2},{6,4},{8,6},{10,8},{12,10},{14,12},{16,14},{18,... | collective-permute-start | bytes 1277960 | tf_op jit(solution)/shard_map/ppermute | solution.py:489

commit v3 on v2

--- a/solution.py
+++ b/solution.py
@@ -29,6 +29,9 @@
         self.edge = OWN if low else end - 1
         self.spare = self.count - 1 if low else 0
         self.facing = 1 if low else 0
+        self.sent = slice(radial_cells - SWEEPS, radial_cells) if low else slice(0, SWEEPS)
+        self.sent_tile = radial_cells - TILE if low else 0
+        self.edge_tile = 0 if low else radial_cells - TILE
 
 
 def shifted(s, by):
@@ -124,8 +127,30 @@
                     mirror(column, side)
 
 
-def edges(known, rad_ref, p_ref, b_ref, w_ref, cut_ref, ghost_ref, last, first, *scratch):
-    field, other, weight, shift, sems = scratch
+def pack(rad_ref, p_ref, s_ref, d_ref, cut_ref, edge_ref, tiles, edge_tiles, sems):
+    radial_cells = p_ref.shape[2]
+
+    def body(side):
+        rows = pl.ds(side.sent_tile, TILE)
+        copies = [
+            pltpu.make_async_copy(x.at[:, :, rows, :], tiles.at[i], sems.at[i])
+            for i, x in enumerate((p_ref, s_ref, d_ref))
+        ]
+        rows = pl.ds(side.edge_tile, TILE)
+        copies.append(
+            pltpu.make_async_copy(p_ref.at[side.facing, :, rows, :], edge_tiles, sems.at[3])
+        )
+        copy_all(copies)
+        cut_ref[...] = tiles[:, :, :, shifted(side.sent, -side.sent_tile), :]
+        at = side.edge - OWN - side.edge_tile
+        for j in range(edge_ref.shape[0]):
+            edge_ref[j : j + 1] = edge_tiles[j, at : at + 1]
+
+    on_each_side(rad_ref, radial_cells, body)
+
+
+def edges(known, rad_ref, p_ref, b_ref, w_ref, cut_ref, near_ref, far_ref, last, first, ghost_ref, *scratch):
+    field, other, weight, shift, wide, sems = scratch
     cells, radial_cells = p_ref.shape[1:3]
     n = SWEEPS - 1
 
@@ -164,6 +189,9 @@
                         shift[edge, k, i] = w * shift[edge, k, i]
         level_ghosts(side, field)
         trajectories(side, field, other, weight, shift, (first, last))
+        wide[:cells] = near_ref[...]
+        wide[cells:] = far_ref[...]
+        ghost_ref[...] = wide[pl.ds(rad_ref[1], cells), :]
         for edge, message in enumerate((first, last)):
             for j in range(3):
                 g = j if edge == 0 else cells - 1 - j
@@ -176,7 +204,8 @@
     if known:
         out_ref, stash, levels, last, weight, shift, sems = rest
     else:
-        out_ref, stash, b_out, w_out, levels, last, weight, shift, sems = rest
+        out_ref, stash, cut_out, edge_out, b_out, w_out, *rest = rest
+        levels, last, weight, shift, sems = rest
     cells, radial_cells = p_ref.shape[1:3]
 
     def body(side):
@@ -248,6 +277,11 @@
         )
         inner.start()
         pending.append(inner)
+        if not known:
+            cut_out[...] = last[:, :, side.sent, :]
+            at = side.edge - OWN
+            for j in range(cells - 2 * SWEEPS):
+                edge_out[j : j + 1] = last[side.facing, j, at : at + 1]
         for c in pending:
             c.wait()
 
@@ -258,7 +292,7 @@
     if known:
         left_w, right_w, _, out_ref, *rest = rest
     else:
-        _, out_ref, *rest = rest
+        cut_in, edge_in, _, out_ref, cut_out, edge_out, *rest = rest
     levels, last, near, near2, weight, shift, moved, moved_w, sems = rest
     cells, radial_cells = p_ref.shape[1:3]
     width = SWEEPS + 2
@@ -362,16 +396,26 @@
                         dst[e, k, 1, side.rows] = new
                         if k != facing:
                             mirror(dst.at[e, k, 1], side)
-        copy_all(
-            [
-                pltpu.make_async_copy(
-                    last.at[e],
-                    out_ref.at[:, pl.ds(0 if e == 0 else cells - SWEEPS, SWEEPS)],
-                    sems.at[e],
-                )
-                for e in range(2)
-            ]
-        )
+        copies = [
+            pltpu.make_async_copy(
+                last.at[e],
+                out_ref.at[:, pl.ds(0 if e == 0 else cells - SWEEPS, SWEEPS)],
+                sems.at[e],
+            )
+            for e in range(2)
+        ]
+        for c in copies:
+            c.start()
+        if not known:
+            row = side.edge - OWN
+            cut_out[0, :, SWEEPS : cells - SWEEPS] = cut_in[...]
+            edge_out[SWEEPS : cells - SWEEPS] = edge_in[...]
+            for e, first in enumerate((0, cells - SWEEPS)):
+                cut_out[0, :, first : first + SWEEPS] = last[e, :, :, side.sent, :]
+                for i in range(SWEEPS):
+                    edge_out[first + i : first + i + 1] = last[e, facing, i, row : row + 1]
+        for c in copies:
+            c.wait()
 
     on_each_side(rad_ref, radial_cells, body)
 
@@ -409,8 +453,7 @@
     if size > near:
         edge = lax.switch(turn // near, [far(t) for t in range(-(-size // near))], edge)
     blocks = lax.switch(turn % near, [branch(t) for t in range(near)], edge)
-    start = jnp.where(radial_index == 0, cells - rest, rest)
-    return lax.dynamic_slice_in_dim(jnp.concatenate(blocks, axis=0), start, cells, 0)
+    return blocks, jnp.where(radial_index == 0, cells - rest, rest)
 
 
 def per_device(pressure, source, diagonal, rot_offset):
@@ -426,97 +469,116 @@
     def scratch(*shape):
         return pltpu.VMEM(shape, jnp.float32)
 
-    own = array(*pressure.shape)
+    def pinned(x):
+        return pltpu.with_memory_space_constraint(x, pltpu.HBM)
+
+    own = pltpu.HBM(pressure.shape, jnp.float32)
     kept = array(2, cells, span, lanes)
     stash = array(2, SWEEPS - 1, 2, 2, rows, lanes)
+    cells_in = cells - 2 * SWEEPS
     vmem = pl.BlockSpec(memory_space=pltpu.VMEM)
     smem = pl.BlockSpec(memory_space=pltpu.SMEM)
     hbm = pl.BlockSpec(memory_space=pltpu.HBM)
-
-    def call(kernel, known, out_shape, in_specs, out_specs, scratch_shapes, operands, cells_done, **more):
-        work = 2 * cells_done * span * lanes
+    anywhere = pl.BlockSpec(memory_space=pl.ANY)
+
+    def call(kernel, out_shape, in_specs, out_specs, scratch_shapes, operands, columns, mib, **more):
+        work = 2 * columns * span * lanes
         return pl.pallas_call(
-            functools.partial(kernel, known),
+            kernel,
             out_shape=out_shape,
             in_specs=in_specs,
             out_specs=out_specs,
             scratch_shapes=scratch_shapes,
-            compiler_params=pltpu.CompilerParams(vmem_limit_bytes=40 << 20),
+            compiler_params=pltpu.CompilerParams(vmem_limit_bytes=mib << 20),
             cost_estimate=pl.CostEstimate(
                 flops=12 * work, bytes_accessed=8 * work, transcendentals=0
             ),
-            name=kernel.__name__,
             **more,
         )(*operands)
 
-    def swap_cut(arrays):
-        cuts = [
-            jnp.where(radial_index == 0, x[:, :, radial_cells - SWEEPS :], x[:, :, :SWEEPS])
-            for x in arrays
-        ]
-        return jnp.stack(cuts)
-
-    fields = (pressure, source, diagonal)
+    fields = tuple(pinned(x) for x in (pressure, source, diagonal))
+    cut, edge = call(
+        pack,
+        (array(3, 2, cells, SWEEPS, lanes), array(cells, lanes)),
+        [smem] + [hbm] * 3,
+        [vmem] * 2,
+        [
+            scratch(3, 2, cells, TILE, lanes),
+            scratch(cells, TILE, lanes),
+            pltpu.SemaphoreType.DMA((4,)),
+        ],
+        (rad, *fields),
+        1,
+        4,
+        name="pack",
+    )
     for step in range(1, STEPS + 1):
         known = step > 1
-        p = fields[0]
-        edge = jnp.where(radial_index == 0, p[1, :, 0, :], p[0, :, radial_cells - 1, :])
-        cut = swap_cut(fields[:1] if known else fields)
-        edge, cut = lax.optimization_barrier((edge, cut))
         cut = lax.ppermute(cut, "rad", [(0, 1), (1, 0)])
         offset = rot_offset[0] * step % (cells * size)
-        ghost = facing_cells(edge, offset, radial_index)
-        operands = (rad, *fields, cut, ghost)
-        specs = [smem] + [hbm] * 3 + [vmem] * 2
+        blocks, start = facing_cells(edge, offset, radial_index)
+        place = jnp.stack([radial_index, start]).astype(jnp.int32)
+        big = [hbm] + [anywhere if known else hbm] * 2
         message = array(2, SWEEPS if known else SLOTS, span, lanes)
-        last, first = call(
-            edges,
-            known,
-            (message, message),
-            specs,
-            [vmem] * 2,
+        last, first, ghost = call(
+            functools.partial(edges, known),
+            (message, message, array(cells, lanes)),
+            [smem, *big, vmem, vmem, vmem],
+            [vmem] * 3,
             [
                 scratch(2, 2, SWEEPS, rows, lanes),
                 scratch(2, 2, SWEEPS, rows, lanes),
                 scratch(2, 2, SWEEPS - 1, span, lanes),
                 scratch(2, 2, SWEEPS - 1, span, lanes),
+                scratch(2 * cells, lanes),
                 pltpu.SemaphoreType.DMA((6,)),
             ],
-            operands,
+            (place, *fields, cut, *blocks),
             12,
+            8,
+            name="edges",
         )
         left = lax.ppermute(last, "az", ring(size, 1))
         right = lax.ppermute(first, "az", ring(size, -1))
+        outs = (own, stash)
+        if not known:
+            outs += (array(2, cells_in, SWEEPS, lanes), array(cells_in, lanes), kept, kept)
         inner, saved, *made = call(
-            interior,
-            known,
-            (own, stash) if known else (own, stash, kept, kept),
-            specs,
-            [hbm] * (2 if known else 4),
+            functools.partial(interior, known),
+            outs,
+            [smem, *big, vmem, vmem],
+            [hbm, anywhere] + ([] if known else [vmem, vmem, anywhere, anywhere]),
             [
                 scratch(SWEEPS, 2, cells, rows, lanes),
-                scratch(2, cells - 2 * SWEEPS, radial_cells, lanes),
+                scratch(2, cells_in, radial_cells, lanes),
                 scratch(*kept.shape),
                 scratch(*kept.shape),
                 pltpu.SemaphoreType.DMA((9,)),
             ],
-            operands,
+            (rad, *fields, cut, ghost),
             44,
+            16,
+            name="interior",
         )
         if not known:
-            shift, weight = made
+            *inner_ends, shift, weight = made
             beyond = (left, right)
-        operands = (rad, p, shift, weight, saved, cut, ghost, left, right)
-        specs = [smem] + [hbm] * 4 + [vmem] * 2 + [hbm] * 2
+        operands = (rad, fields[0], shift, weight, saved, cut, ghost, left, right)
+        specs = [smem, hbm] + [anywhere] * 3 + [vmem] * 2 + [anywhere] * 2
         if known:
             operands += beyond
-            specs += [hbm] * 2
+            specs += [anywhere] * 2
+            outs, out_specs = own, hbm
+        else:
+            operands += tuple(inner_ends)
+            specs += [vmem] * 2
+            outs = (own, array(1, 2, cells, SWEEPS, lanes), array(cells, lanes))
+            out_specs = [hbm, vmem, vmem]
         pressure = call(
-            finish,
-            known,
-            own,
+            functools.partial(finish, known),
+            outs,
             specs + [hbm],
-            hbm,
+            out_specs,
             [
                 scratch(SWEEPS, 2, 2, SWEEPS + 2, rows, lanes),
                 scratch(2, 2, SWEEPS, radial_cells, lanes),
@@ -530,9 +592,13 @@
             ],
             (*operands, inner),
             26,
+            16,
             input_output_aliases={len(operands): 0},
+            name="finish",
         )
-        fields = (pressure, shift, weight)
+        if not known:
+            pressure, cut, edge = pressure
+            fields = (pinned(pressure), shift, weight)
     return pressure
 
 

time: 73.6 us -> 69.8 us (0.948)
  local copies, waits for them, and re-layouts: 12 us -> 0.93 us
  Pallas kernels: 23.6 us -> 32.8 us
  other arithmetic: 4.52 us -> 0.15 us
  starting transfers between devices: 13.4 us -> 15.9 us
    unnamed x22 -> x4, local copies, waits for them, and re-layouts: 12 us -> 0.93 us
    pallas_call x6 -> x7, Pallas kernels: 23.6 us -> 32.8 us  [call(): pl.pallas_call(kernel, out_shape=out_shape, in_specs=in_specs, out_specs=...]
    another operation x4 -> x2, other arithmetic: 2.2 us -> 0.15 us  [per_device(): place = jnp.stack([radial_index, start]).astype(jnp.int32)]
    concatenate x2 -> x0, other arithmetic: 1.42 us -> none  [facing_cells(): jnp.concatenate(blocks, axis=0)]
    ppermute x2, starting transfers between devices: 3.47 us -> 4.55 us  [per_device(): left = lax.ppermute(last, 'az', ring(size, 1))]
    ppermute x4, starting transfers between devices: 7.77 us -> 8.69 us  [branch(): lax.ppermute(e, ('az', 'rad'), facing_pairs(size, t, k))]
    select_n x2 -> x0, other arithmetic: 0.9 us -> none  [per_device(): jnp.where(radial_index == 0, p[1, :, 0, :], p[0, :, radial_cells - 1, :])]
  transfers between devices with their start and end apart: 10 -> 10, of which waited for: 7 -> 8; matrix products, arithmetic and copies ran while one was open for 2% -> 0% of each run, Pallas kernels for 16% -> 22%
where the time goes in v3:
time: 69.8 us; the launch traced here: 70.1 us
  Pallas kernels  32.8 us (47%)
  waiting for transfers between devices  19.3 us (28%)
  starting transfers between devices  15.9 us (23%)
  between operations  0.96 us (1%)
  local copies, waits for them, and re-layouts  0.93 us (1%)
    pallas_call x7, Pallas kernels, call(): pl.pallas_call(kernel, out_shape=out_shape, in_specs=in_specs, out_specs=...  32.8 us
    ppermute x4, starting transfers between devices, branch(): lax.ppermute(e, ('az', 'rad'), facing_pairs(size, t, k))  8.69 us
    ppermute x2, waiting for transfers between devices, per_device(): left = lax.ppermute(last, 'az', ring(size, 1))  7.34 us
    ppermute x4, waiting for transfers between devices, branch(): lax.ppermute(e, ('az', 'rad'), facing_pairs(size, t, k))  7.01 us
    ppermute x2, waiting for transfers between devices, per_device(): right = lax.ppermute(first, 'az', ring(size, -1))  4.98 us
    ppermute x2, starting transfers between devices, per_device(): left = lax.ppermute(last, 'az', ring(size, 1))  4.55 us
    ppermute x2, starting transfers between devices, per_device(): cut = lax.ppermute(cut, 'rad', [(0, 1), (1, 0)])  2.2 us
  transfers between devices with their start and end apart: 10, of which 8 were waited for; matrix products, arithmetic and copies ran while one was open for 0% of the time, Pallas kernels for 22%

profile of v3, /device:TPU:1, one launch (start us, length us, event | category | flops | bytes accessed | tf_op | source)
XLA Modules:
  0.0 70.1 jit_solution(8075558108212495286)
XLA Ops:
  0.0 1.1 %pack.1 = (f32[3,2,16,4,128]{4,3,2,1,0:T(4,128)S(1)}, f32[16,128]{1,0:T(8,128)S(1)}) custom-call(s32[1]{0:T(128)} %bitcast.rad_ref, f32[2,16,96,128]{3,2,1,0:T(8,128)} %p_ref.7, f32[2,16,96,128]{3,2,1,0:T(8,128)} %b_ref.3, f32[2,16,96,128]{3,2,1,0:T(8,128)} %w_ref.3), custom_call_target="tpu_custom_call" | custom-call | flops 319488 | bytes 212992 | tf_op jit(solution)/shard_map/pack/pallas_call | solution.py:486
  1.1 2.1 %collective-permute-start.64 = (f32[3,2,16,4,128]{4,3,2,1,0:T(4,128)S(1)}, f32[3,2,16,4,128]{4,3,2,1,0:T(4,128)S(1)}, u32[]{:S(2)}, u32[]{:S(2)}) collective-permute-start(f32[3,2,16,4,128]{4,3,2,1,0:T(4,128)S(1)} %get-tuple-element.60), channel_id=1, source_target_pairs={{0,1},{1,0},{2,3},{3,2},{4,5},{5,4},{6,7},{7,6},{8,9},{9,8},{10,11... | collective-permute-start | bytes 589832 | tf_op jit(solution)/shard_map/ppermute | solution.py:517
  4.0 6.7 %conditional.2 = (f32[16,128]{1,0:T(8,128)}, f32[16,128]{1,0:T(8,128)}) conditional(s32[]{:T(128)} %clamp.6, f32[16,128]{1,0:T(8,128)S(1)} %get-tuple-element.61, f32[16,128]{1,0:T(8,128)S(1)} %get-tuple-element.61, f32[16,128]{1,0:T(8,128)S(1)} %get-tuple-element.61, f32[16,128]{1,0:T(8,128)S(1)} %get-tuple-element.61, ...), branch_computations={%region_0.1_spmd, %region_1.2_spmd, %region_2.3_spmd, %region_3.4_... | conditional | bytes 65632 | solution.py:455
  4.0 2.2 %collective-permute-start.19 = (f32[16,128]{1,0:T(8,128)S(1)}, f32[16,128]{1,0:T(8,128)}, u32[]{:S(2)}, u32[]{:S(2)}) collective-permute-start(f32[16,128]{1,0:T(8,128)S(1)} %param.9), channel_id=1, source_target_pairs={{15,0},{20,1},{17,2},{22,3},{19,4},{24,5},{21,6},{26,7},{23,8},{28... | collective-permute-start | bytes 24584 | tf_op jit(solution)/shard_map/cond/branch_9_fun/ppermute | solution.py:450
  6.2 1.4 %collective-permute-start.18 = (f32[16,128]{1,0:T(8,128)S(1)}, f32[16,128]{1,0:T(8,128)}, u32[]{:S(2)}, u32[]{:S(2)}) collective-permute-start(f32[16,128]{1,0:T(8,128)S(1)} %param.9), channel_id=1, source_target_pairs={{13,0},{18,1},{15,2},{20,3},{17,4},{22,5},{19,6},{24,7},{21,8},{26... | collective-permute-start | bytes 24584 | tf_op jit(solution)/shard_map/cond/branch_9_fun/ppermute | solution.py:450
  7.6 1.4 %collective-permute-done.19 = f32[16,128]{1,0:T(8,128)} collective-permute-done((f32[16,128]{1,0:T(8,128)S(1)}, f32[16,128]{1,0:T(8,128)}, u32[]{:S(2)}, u32[]{:S(2)}) %collective-permute-start.19) | collective-permute-done | bytes 8224 | tf_op jit(solution)/shard_map/cond/branch_9_fun/ppermute | solution.py:450
  9.0 1.6 %collective-permute-done.18 = f32[16,128]{1,0:T(8,128)} collective-permute-done((f32[16,128]{1,0:T(8,128)S(1)}, f32[16,128]{1,0:T(8,128)}, u32[]{:S(2)}, u32[]{:S(2)}) %collective-permute-start.18) | collective-permute-done | bytes 8224 | tf_op jit(solution)/shard_map/cond/branch_9_fun/ppermute | solution.py:450
  10.7 4.3 %edges.2 = (f32[2,6,104,128]{3,2,1,0:T(8,128)}, f32[2,6,104,128]{3,2,1,0:T(8,128)}, f32[16,128]{1,0:T(8,128)S(1)}) custom-call(s32[2]{0:T(128)S(1)} %pad_add_fusion.rad_ref, f32[2,16,96,128]{3,2,1,0:T(8,128)} %p_ref.7, f32[2,16,96,128]{3,2,1,0:T(8,128)} %b_ref.3, f32[2,16,96,128]{3,2,1,0:T(8,128)} %w_ref.3, ...), custom_call_target="tpu_custom_call" | custom-call | flops 3833856 | bytes 2555904 | tf_op jit(solution)/shard_map/edges/pallas_call | solution.py:486
  15.0 4.5 %collective-permute-start.65 = (f32[2,6,104,128]{3,2,1,0:T(8,128)}, f32[2,6,104,128]{3,2,1,0:T(8,128)}, u32[]{:S(2)}, u32[]{:S(2)}) collective-permute-start(f32[2,6,104,128]{3,2,1,0:T(8,128)} %get-tuple-element.68), channel_id=1, source_target_pairs={{0,2},{2,4},{4,6},{6,8},{8,10},{10,12},{12,14},{14,16},{16,18},{18... | collective-permute-start | bytes 1916936 | tf_op jit(solution)/shard_map/ppermute | solution.py:541
  19.5 0.9 %copy-done.1 = f32[3,2,16,4,128]{4,3,2,1,0:T(4,128)S(1)} copy-done((f32[3,2,16,4,128]{4,3,2,1,0:T(4,128)S(1)}, f32[3,2,16,4,128]{4,3,2,1,0:T(4,128)}, u32[]{:S(2)}) %copy-start.1) | copy-done | bytes 196632
  20.4 8.7 %interior.2 = (f32[2,16,96,128]{3,2,1,0:T(8,128)}, f32[2,3,2,2,128,128]{5,4,3,2,1,0:T(8,128)S(1)}, f32[2,8,4,128]{3,2,1,0:T(4,128)S(1)}, f32[8,128]{1,0:T(8,128)...) custom-call(s32[1]{0:T(128)} %bitcast.rad_ref, f32[2,16,96,128]{3,2,1,0:T(8,128)} %p_ref.7, ...), custom_call_target="tpu_custom_call" | custom-call | flops 14057472 | bytes 9371648 | tf_op jit(solution)/shard_map/interior/pallas_call | solution.py:486
  29.1 4.9 %collective-permute-done.65.left_ref.rest_0_ = f32[2,6,104,128]{3,2,1,0:T(8,128)} collective-permute-done((f32[2,6,104,128]{3,2,1,0:T(8,128)}, f32[2,6,104,128]{3,2,1,0:T(8,128)}, u32[]{:S(2)}, u32[]{:S(2)}) %collective-permute-start.65) | collective-permute-done | bytes 639008 | tf_op jit(solution)/shard_map/ppermute | solution.py:541
  34.0 2.4 %collective-permute-done.66.right_ref.rest_1_ = f32[2,6,104,128]{3,2,1,0:T(8,128)} collective-permute-done((f32[2,6,104,128]{3,2,1,0:T(8,128)}, f32[2,6,104,128]{3,2,1,0:T(8,128)}, u32[]{:S(2)}, u32[]{:S(2)}) %collective-permute-start.66) | collective-permute-done | bytes 639008 | tf_op jit(solution)/shard_map/ppermute | solution.py:542
  36.5 4.4 %finish.2 = (f32[2,16,96,128]{3,2,1,0:T(8,128)}, f32[1,2,16,4,128]{4,3,2,1,0:T(4,128)S(1)}, f32[16,128]{1,0:T(8,128)S(1)}) custom-call(s32[1]{0:T(128)} %bitcast.rad_ref, f32[2,16,96,128]{3,2,1,0:T(8,128)} %p_ref.7, f32[2,16,104,128]{3,2,1,0:T(8,128)S(1)} %get-tuple-element.65.b_ref, ...), custom_call_target="tpu_custom_call", output_to_operand_aliasing={{0}: (11, {})} | custom-call | flops 8306688 | bytes 5537792 | tf_op jit(solution)/shard_map/finish/pallas_call | solution.py:486
  41.0 9.1 %conditional.3 = (f32[16,128]{1,0:T(8,128)}, f32[16,128]{1,0:T(8,128)}) conditional(s32[]{:T(128)} %clamp.7, f32[16,128]{1,0:T(8,128)S(1)} %get-tuple-element.75, f32[16,128]{1,0:T(8,128)S(1)} %get-tuple-element.75, f32[16,128]{1,0:T(8,128)S(1)} %get-tuple-element.75, f32[16,128]{1,0:T(8,128)S(1)} %get-tuple-element.75, ...), branch_computations={%region_16.17_spmd, %region_17.18_spmd, %region_18.19_spmd, %regio... | conditional | bytes 65632 | solution.py:455
  41.0 2.3 %collective-permute-start.37 = (f32[16,128]{1,0:T(8,128)S(1)}, f32[16,128]{1,0:T(8,128)}, u32[]{:S(2)}, u32[]{:S(2)}) collective-permute-start(f32[16,128]{1,0:T(8,128)S(1)} %param.18), channel_id=1, source_target_pairs={{29,0},{6,1},{31,2},{8,3},{1,4},{10,5},{3,6},{12,7},{5,8},{14,9},{... | collective-permute-start | bytes 24584 | tf_op jit(solution)/shard_map/cond/branch_2_fun/ppermute | solution.py:450
  43.3 2.8 %collective-permute-start.36 = (f32[16,128]{1,0:T(8,128)S(1)}, f32[16,128]{1,0:T(8,128)}, u32[]{:S(2)}, u32[]{:S(2)}) collective-permute-start(f32[16,128]{1,0:T(8,128)S(1)} %param.18), channel_id=1, source_target_pairs={{27,0},{4,1},{29,2},{6,3},{31,4},{8,5},{1,6},{10,7},{3,8},{12,9},{... | collective-permute-start | bytes 24584 | tf_op jit(solution)/shard_map/cond/branch_2_fun/ppermute | solution.py:450
  46.1 1.1 %collective-permute-done.37 = f32[16,128]{1,0:T(8,128)} collective-permute-done((f32[16,128]{1,0:T(8,128)S(1)}, f32[16,128]{1,0:T(8,128)}, u32[]{:S(2)}, u32[]{:S(2)}) %collective-permute-start.37) | collective-permute-done | bytes 8224 | tf_op jit(solution)/shard_map/cond/branch_2_fun/ppermute | solution.py:450
  47.3 2.8 %collective-permute-done.36 = f32[16,128]{1,0:T(8,128)} collective-permute-done((f32[16,128]{1,0:T(8,128)S(1)}, f32[16,128]{1,0:T(8,128)}, u32[]{:S(2)}, u32[]{:S(2)}) %collective-permute-start.36) | collective-permute-done | bytes 8224 | tf_op jit(solution)/shard_map/cond/branch_2_fun/ppermute | solution.py:450
  50.1 2.8 %edges.3 = (f32[2,4,104,128]{3,2,1,0:T(8,128)S(1)}, f32[2,4,104,128]{3,2,1,0:T(8,128)S(1)}, f32[16,128]{1,0:T(8,128)S(1)}) custom-call(s32[2]{0:T(128)S(1)} %pad_add_fusion.1.rad_ref, f32[2,16,96,128]{3,2,1,0:T(8,128)} %get-tuple-element.73.p_ref, f32[2,16,104,128]{3,2,1,0:T(8,128)S(1)} %get-tuple-element.65.b_ref, ...), custom_call_target="tpu_custom_call" | custom-call | flops 3833856 | bytes 2555904 | tf_op jit(solution)/shard_map/edges/pallas_call | solution.py:486
  53.5 6.7 %interior.3 = (f32[2,16,96,128]{3,2,1,0:T(8,128)}, f32[2,3,2,2,128,128]{5,4,3,2,1,0:T(8,128)S(1)}) custom-call(s32[1]{0:T(128)} %bitcast.rad_ref, f32[2,16,96,128]{3,2,1,0:T(8,128)} %get-tuple-element.73.p_ref, f32[2,16,104,128]{3,2,1,0:T(8,128)S(1)} %get-tuple-element.65.b_ref, f32[2,16,104,128]{3,2,1,0:T(8,128)S(1)} %get-tuple-element.66.w_ref, ...), custom_call_target="tpu_custom_call" | custom-call | flops 14057472 | bytes 9371648 | tf_op jit(solution)/shard_map/interior/pallas_call | solution.py:486
  60.2 2.4 %collective-permute-done.68.left_ref = f32[2,4,104,128]{3,2,1,0:T(8,128)S(1)} collective-permute-done((f32[2,4,104,128]{3,2,1,0:T(8,128)S(1)}, f32[2,4,104,128]{3,2,1,0:T(8,128)S(1)}, u32[]{:S(2)}, u32[]{:S(2)}) %collective-permute-start.68) | collective-permute-done | bytes 426016 | tf_op jit(solution)/shard_map/ppermute | solution.py:541
  62.6 2.5 %collective-permute-done.69.right_ref = f32[2,4,104,128]{3,2,1,0:T(8,128)S(1)} collective-permute-done((f32[2,4,104,128]{3,2,1,0:T(8,128)S(1)}, f32[2,4,104,128]{3,2,1,0:T(8,128)S(1)}, u32[]{:S(2)}, u32[]{:S(2)}) %collective-permute-start.69) | collective-permute-done | bytes 426016 | tf_op jit(solution)/shard_map/ppermute | solution.py:542
  65.2 4.8 %finish.3 = f32[2,16,96,128]{3,2,1,0:T(8,128)} custom-call(s32[1]{0:T(128)} %bitcast.rad_ref, f32[2,16,96,128]{3,2,1,0:T(8,128)} %get-tuple-element.73.p_ref, f32[2,16,104,128]{3,2,1,0:T(8,128)S(1)} %get-tuple-element.65.b_ref, f32[2,16,104,128]{3,2,1,0:T(8,128)S(1)} %get-tuple-element.66.w_ref, ...), custom_call_target="tpu_custom_call", output_to_operand_aliasing={{}: (11, {})} | custom-call | flops 8306688 | bytes 5537792 | tf_op jit(solution)/shard_map/finish/pallas_call | solution.py:486
  (11 shorter events, 0.8 us)
Async XLA Ops:
  1.1 9.6 %collective-permute-start.64 = (f32[3,2,16,4,128]{4,3,2,1,0:T(4,128)S(1)}, f32[3,2,16,4,128]{4,3,2,1,0:T(4,128)S(1)}, u32[]{:S(2)}, u32[]{:S(2)}) collective-permute-start(f32[3,2,16,4,128]{4,3,2,1,0:T(4,128)S(1)} %get-tuple-element.60), channel_id=1, source_target_pairs={{0,1},{1,0},{2,3},{3,2},{4,5},{5,4},{6,7},{7,6},{8,9},{9,8},{10,11... | collective-permute-start | bytes 589832 | tf_op jit(solution)/shard_map/ppermute | solution.py:517
  4.0 5.0 %collective-permute-start.19 = (f32[16,128]{1,0:T(8,128)S(1)}, f32[16,128]{1,0:T(8,128)}, u32[]{:S(2)}, u32[]{:S(2)}) collective-permute-start(f32[16,128]{1,0:T(8,128)S(1)} %param.9), channel_id=1, source_target_pairs={{15,0},{20,1},{17,2},{22,3},{19,4},{24,5},{21,6},{26,7},{23,8},{28... | collective-permute-start | bytes 24584 | tf_op jit(solution)/shard_map/cond/branch_9_fun/ppermute | solution.py:450
  6.2 4.4 %collective-permute-start.18 = (f32[16,128]{1,0:T(8,128)S(1)}, f32[16,128]{1,0:T(8,128)}, u32[]{:S(2)}, u32[]{:S(2)}) collective-permute-start(f32[16,128]{1,0:T(8,128)S(1)} %param.9), channel_id=1, source_target_pairs={{13,0},{18,1},{15,2},{20,3},{17,4},{22,5},{19,6},{24,7},{21,8},{26... | collective-permute-start | bytes 24584 | tf_op jit(solution)/shard_map/cond/branch_9_fun/ppermute | solution.py:450
  10.7 4.3 %copy-start = (f32[3,2,16,4,128]{4,3,2,1,0:T(4,128)}, f32[3,2,16,4,128]{4,3,2,1,0:T(4,128)S(1)}, u32[]{:S(2)}) copy-start(f32[3,2,16,4,128]{4,3,2,1,0:T(4,128)S(1)} %collective-permute-done.64.cut_ref) | copy-start | bytes 589828
  15.0 19.0 %collective-permute-start.65 = (f32[2,6,104,128]{3,2,1,0:T(8,128)}, f32[2,6,104,128]{3,2,1,0:T(8,128)}, u32[]{:S(2)}, u32[]{:S(2)}) collective-permute-start(f32[2,6,104,128]{3,2,1,0:T(8,128)} %get-tuple-element.68), channel_id=1, source_target_pairs={{0,2},{2,4},{4,6},{6,8},{8,10},{10,12},{12,14},{14,16},{16,18},{18... | collective-permute-start | bytes 1916936 | tf_op jit(solution)/shard_map/ppermute | solution.py:541
  19.5 17.0 %collective-permute-start.66 = (f32[2,6,104,128]{3,2,1,0:T(8,128)}, f32[2,6,104,128]{3,2,1,0:T(8,128)}, u32[]{:S(2)}, u32[]{:S(2)}) collective-permute-start(f32[2,6,104,128]{3,2,1,0:T(8,128)} %get-tuple-element.69), channel_id=1, source_target_pairs={{0,30},{2,0},{4,2},{6,4},{8,6},{10,8},{12,10},{14,12},{16,14},{18,... | collective-permute-start | bytes 1916936 | tf_op jit(solution)/shard_map/ppermute | solution.py:542
  19.5 0.9 %copy-start.1 = (f32[3,2,16,4,128]{4,3,2,1,0:T(4,128)S(1)}, f32[3,2,16,4,128]{4,3,2,1,0:T(4,128)}, u32[]{:S(2)}) copy-start(f32[3,2,16,4,128]{4,3,2,1,0:T(4,128)} %copy-done) | copy-start | bytes 589828
  40.9 9.2 %collective-permute-start.67 = (f32[1,2,16,4,128]{4,3,2,1,0:T(4,128)S(1)}, f32[1,2,16,4,128]{4,3,2,1,0:T(4,128)S(1)}, u32[]{:S(2)}, u32[]{:S(2)}) collective-permute-start(f32[1,2,16,4,128]{4,3,2,1,0:T(4,128)S(1)} %get-tuple-element.74), channel_id=1, source_target_pairs={{0,1},{1,0},{2,3},{3,2},{4,5},{5,4},{6,7},{7,6},{8,9},{9,8},{10,11... | collective-permute-start | bytes 196616 | tf_op jit(solution)/shard_map/ppermute | solution.py:517
  41.0 6.2 %collective-permute-start.37 = (f32[16,128]{1,0:T(8,128)S(1)}, f32[16,128]{1,0:T(8,128)}, u32[]{:S(2)}, u32[]{:S(2)}) collective-permute-start(f32[16,128]{1,0:T(8,128)S(1)} %param.18), channel_id=1, source_target_pairs={{29,0},{6,1},{31,2},{8,3},{1,4},{10,5},{3,6},{12,7},{5,8},{14,9},{... | collective-permute-start | bytes 24584 | tf_op jit(solution)/shard_map/cond/branch_2_fun/ppermute | solution.py:450
  43.3 6.8 %collective-permute-start.36 = (f32[16,128]{1,0:T(8,128)S(1)}, f32[16,128]{1,0:T(8,128)}, u32[]{:S(2)}, u32[]{:S(2)}) collective-permute-start(f32[16,128]{1,0:T(8,128)S(1)} %param.18), channel_id=1, source_target_pairs={{27,0},{4,1},{29,2},{6,3},{31,4},{8,5},{1,6},{10,7},{3,8},{12,9},{... | collective-permute-start | bytes 24584 | tf_op jit(solution)/shard_map/cond/branch_2_fun/ppermute | solution.py:450
  52.9 9.7 %collective-permute-start.68 = (f32[2,4,104,128]{3,2,1,0:T(8,128)S(1)}, f32[2,4,104,128]{3,2,1,0:T(8,128)S(1)}, u32[]{:S(2)}, u32[]{:S(2)}) collective-permute-start(f32[2,4,104,128]{3,2,1,0:T(8,128)S(1)} %get-tuple-element.80), channel_id=1, source_target_pairs={{0,2},{2,4},{4,6},{6,8},{8,10},{10,12},{12,14},{14,16},{16,18},{18... | collective-permute-start | bytes 1277960 | tf_op jit(solution)/shard_map/ppermute | solution.py:541
  53.0 12.2 %collective-permute-start.69 = (f32[2,4,104,128]{3,2,1,0:T(8,128)S(1)}, f32[2,4,104,128]{3,2,1,0:T(8,128)S(1)}, u32[]{:S(2)}, u32[]{:S(2)}) collective-permute-start(f32[2,4,104,128]{3,2,1,0:T(8,128)S(1)} %get-tuple-element.81), channel_id=1, source_target_pairs={{0,30},{2,0},{4,2},{6,4},{8,6},{10,8},{12,10},{14,12},{16,14},{18,... | collective-permute-start | bytes 1277960 | tf_op jit(solution)/shard_map/ppermute | solution.py:542

commit v4 on v0

v4 whole, which is shorter than its diff:
```python
import functools

import jax
import jax.numpy as jnp
from jax import lax
from jax.experimental import pallas as pl
from jax.experimental.pallas import tpu as pltpu
from jax.sharding import PartitionSpec as P

STEPS = 2
SWEEPS = 4
OMEGA = 0.8
TILE = 8
OWN = 2 * TILE
SLOTS = SWEEPS + 2


class Side:
    def __init__(self, low, radial_cells):
        end = OWN + radial_cells
        self.low = low
        self.own = slice(OWN, end)
        self.first = OWN if low else TILE
        self.count = radial_cells + TILE
        self.rows = slice(self.first, self.first + self.count)
        self.cut = slice(end, end + SWEEPS) if low else slice(OWN - SWEEPS, OWN)
        self.tile = slice(end, end + TILE) if low else slice(TILE, OWN)
        self.ghost = OWN - 1 if low else end
        self.edge = OWN if low else end - 1
        self.spare = self.count - TILE + SWEEPS if low else 0
        self.facing = 1 if low else 0
        self.sent = slice(radial_cells - SWEEPS, radial_cells) if low else slice(0, SWEEPS)
        self.sent_tile = radial_cells - TILE if low else 0
        self.edge_tile = 0 if low else radial_cells - TILE


def shifted(s, by):
    return slice(s.start + by, s.stop + by)


def axial_sum(x):
    lane = lax.broadcasted_iota(jnp.int32, x.shape, 1)
    last = x.shape[1] - 1
    return jnp.where(lane == 0, 0.0, pltpu.roll(x, 1, 1)) + jnp.where(
        lane == last, 0.0, pltpu.roll(x, last, 1)
    )


def relaxed(column, side, beside, weight, shift):
    here = column[side.rows]
    radial = column[shifted(side.rows, -1)] + column[shifted(side.rows, 1)]
    nbr = beside + radial + axial_sum(here)
    kept = (1.0 - OMEGA) * here
    if shift is not None:
        kept = kept + shift
    return kept + weight * nbr


def mirror(column, side):
    column[side.ghost : side.ghost + 1] = column[side.edge : side.edge + 1]


def on_each_side(rad_ref, radial_cells, body):
    @pl.when(rad_ref[0] == 0)
    def _():
        body(Side(True, radial_cells))

    @pl.when(rad_ref[0] != 0)
    def _():
        body(Side(False, radial_cells))


def copy_all(copies):
    for c in copies:
        c.start()
    for c in copies:
        c.wait()


def end_columns(edge, cells, count):
    return slice(0, count) if edge == 0 else slice(cells - count, cells)


def spare_rows(side):
    return [(slot, side.spare + i) for slot in range(SWEEPS) for i in range(TILE - SWEEPS)]


def close(column, side, facing):
    row = slice(side.ghost, side.ghost + 1)
    if facing:
        column[row] = jnp.zeros((1, column.shape[1]), jnp.float32)
    else:
        column[row] = column[side.edge : side.edge + 1]


def trajectories(side, field, other, weight, shift, messages):
    bufs = (field, other)
    for edge, message in enumerate(messages):

        def at(distance, n, edge=edge):
            return distance - 1 if edge == 0 else n - distance

        for k in range(2):
            facing = k == side.facing
            for i in range(SWEEPS):
                close(field.at[edge, k, i], side, facing)
            for sweep in range(SWEEPS):
                src, dst = bufs[sweep % 2], bufs[1 - sweep % 2]
                top = src.at[edge, k, at(1, SWEEPS)]
                message[k, sweep] = top[side.rows]
                for j in range(1, SWEEPS - sweep):
                    here = src.at[edge, k, at(j, SWEEPS)]
                    beside = src[edge, k, at(j + 1, SWEEPS), side.rows]
                    if j > 1:
                        beside = beside + src[edge, k, at(j - 1, SWEEPS), side.rows]
                    i = at(j, SWEEPS - 1)
                    out = dst.at[edge, k, at(j, SWEEPS)]
                    out[side.rows] = relaxed(here, side, beside, weight(edge, k, i), shift(edge, k, i))
                    close(out, side, facing)
            if message.shape[1] == SWEEPS:
                continue
            for i in range(2):
                message[k, SWEEPS + i] = weight(edge, k, at(1 + i, SWEEPS - 1))
            if facing:
                row = side.edge - side.first
                message[k, SWEEPS + 1, side.spare : side.spare + 1] = weight(
                    edge, k, at(3, SWEEPS - 1)
                )[row : row + 1]


def pack(rad_ref, p_ref, s_ref, d_ref, cut_ref, edge_ref, p_ends, s_ends, d_ends, tiles, edge_tiles, sems):
    cells, radial_cells = p_ref.shape[1:3]

    def body(side):
        copies = []

        def fetch(source, target):
            copies.append(pltpu.make_async_copy(source, target, sems.at[len(copies)]))

        rows = pl.ds(side.sent_tile, TILE)
        for i, x in enumerate((p_ref, s_ref, d_ref)):
            fetch(x.at[:, :, rows, :], tiles.at[i])
        fetch(p_ref.at[side.facing, :, pl.ds(side.edge_tile, TILE), :], edge_tiles)
        for source, target in ((p_ref, p_ends), (s_ref, s_ends), (d_ref, d_ends)):
            count = target.shape[2]
            for edge in range(2):
                span = pl.ds(end_columns(edge, cells, count).start, count)
                fetch(source.at[:, span], target.at[edge])
        copy_all(copies)
        cut_ref[...] = tiles[:, :, :, shifted(side.sent, -side.sent_tile), :]
        at = side.edge - OWN - side.edge_tile
        for j in range(cells):
            edge_ref[j : j + 1] = edge_tiles[j, at : at + 1]

    on_each_side(rad_ref, radial_cells, body)


def fill_ends(field, side, p_column, cut_ref, cells, radial_cells):
    for edge in range(2):
        columns = end_columns(edge, cells, SWEEPS)
        for k in range(2):
            for i in range(SWEEPS):
                field[edge, k, i, side.own] = p_column(edge, k, i)
                field[edge, k, i, side.cut] = cut_ref[0, k, columns.start + i]


def send_block(side, block_ref, messages):
    for message in messages:
        for i, (slot, row) in enumerate(spare_rows(side)):
            message[side.facing, slot, row : row + 1] = block_ref[i : i + 1]


def first_edges(
    rad_ref, p_ends, s_ends, d_ends, cut_ref, block_ref, last, first, field, other, weight, shift
):
    radial_cells = p_ends.shape[3]
    cells = cut_ref.shape[2]
    n = SWEEPS - 1

    def body(side):
        own = shifted(side.own, -side.first)
        cut = shifted(side.cut, -side.first)
        fill_ends(field, side, lambda e, k, i: p_ends[e, k, i], cut_ref, cells, radial_cells)
        for edge in range(2):
            columns = end_columns(edge, cells, n)
            for k in range(2):
                for i in range(n):
                    for rows, s, d in (
                        (own, s_ends[edge, k, i], d_ends[edge, k, i]),
                        (cut, cut_ref[1, k, columns.start + i], cut_ref[2, k, columns.start + i]),
                    ):
                        w = OMEGA / (6.0 + d)
                        weight[edge, k, i, rows] = w
                        shift[edge, k, i, rows] = w * s
        trajectories(
            side,
            field,
            other,
            lambda e, k, i: weight[e, k, i],
            lambda e, k, i: shift[e, k, i],
            (first, last),
        )
        send_block(side, block_ref, (first, last))

    on_each_side(rad_ref, radial_cells, body)


def later_edges(rad_ref, p_ref, b_ref, w_ref, cut_ref, block_ref, last, first, field, other):
    cells, radial_cells = p_ref.shape[1:3]

    def body(side):
        fill_ends(
            field,
            side,
            lambda e, k, i: p_ref[k, end_columns(e, cells, SWEEPS).start + i],
            cut_ref,
            cells,
            radial_cells,
        )
        trajectories(
            side,
            field,
            other,
            lambda e, k, i: w_ref[k, end_columns(e, cells, SWEEPS - 1).start + i],
            lambda e, k, i: b_ref[k, end_columns(e, cells, SWEEPS - 1).start + i],
            (first, last),
        )
        send_block(side, block_ref, (first, last))

    on_each_side(rad_ref, radial_cells, body)


def inner_sweeps(side, levels, weight, shift, last, out_ref, stash, tile_out, sems):
    cells = levels.shape[2]
    radial_cells = side.own.stop - side.own.start
    for j in range(cells):
        for k in range(2):
            close(levels.at[0, k, j], side, k == side.facing)
        for n in range(1, SWEEPS):
            close(levels.at[n, side.facing, j], side, True)
    at = side.edge - side.first
    for n in range(SWEEPS):
        final = n == SWEEPS - 1

        def step(j, carry, n=n, final=final):
            for k in range(2):
                beside = levels[n, k, j - 1, side.rows] + levels[n, k, j + 1, side.rows]
                new = relaxed(levels.at[n, k, j], side, beside, weight[k, j], shift[k, j])
                if final:
                    last[k, j - SWEEPS] = new[shifted(side.own, -side.first)]
                else:
                    levels[n + 1, k, j, side.rows] = new
                    if k != side.facing:
                        levels[n + 1, k, j, side.ghost : side.ghost + 1] = new[at : at + 1]
            return carry

        lax.fori_loop(n + 1, cells - 1 - n, step, 0, unroll=2)
        if not final:
            for e, first in enumerate((n + 1, cells - 3 - n)):
                for k in range(2):
                    for i in range(2):
                        stash[e, n, k, i] = levels[n + 1, k, first + i]
    inner = pltpu.make_async_copy(
        last, out_ref.at[:, pl.ds(SWEEPS, cells - 2 * SWEEPS)], sems.at[0]
    )
    inner.start()
    tile_out[...] = last[side.facing, :, side.edge_tile : side.edge_tile + TILE, :]
    return inner


def first_interior(
    rad_ref, p_ref, s_ref, d_ref, cut_ref, out_ref, stash, tile_out, cut_out, b_out, w_out, levels, last, sems
):
    cells, radial_cells = p_ref.shape[1:3]

    def body(side):
        own = pl.ds(OWN - side.first, radial_cells)
        copy_all(
            [
                pltpu.make_async_copy(
                    p_ref, levels.at[0, :, :, pl.ds(OWN, radial_cells), :], sems.at[0]
                ),
                pltpu.make_async_copy(s_ref, b_out.at[:, :, own, :], sems.at[1]),
                pltpu.make_async_copy(d_ref, w_out.at[:, :, own, :], sems.at[2]),
            ]
        )
        cut = shifted(side.cut, -side.first)
        levels[0, :, :, side.cut, :] = cut_ref[0]
        b_out[:, :, cut, :] = cut_ref[1]
        w_out[:, :, cut, :] = cut_ref[2]

        def invert(j, carry):
            for k in range(2):
                w = OMEGA / (6.0 + w_out[k, j])
                w_out[k, j] = w
                b_out[k, j] = w * b_out[k, j]
            return carry

        lax.fori_loop(0, cells, invert, 0)
        inner = inner_sweeps(side, levels, w_out, b_out, last, out_ref, stash, tile_out, sems)
        cut_out[...] = last[:, :, side.sent, :]
        inner.wait()

    on_each_side(rad_ref, radial_cells, body)


def later_interior(
    rad_ref, p_ref, b_ref, w_ref, cut_ref, out_ref, stash, tile_out, levels, last, sems
):
    cells, radial_cells = p_ref.shape[1:3]

    def body(side):
        levels[0, :, :, side.own, :] = p_ref[...]
        levels[0, :, :, side.cut, :] = cut_ref[0]
        inner_sweeps(side, levels, w_ref, b_ref, last, out_ref, stash, tile_out, sems).wait()

    on_each_side(rad_ref, radial_cells, body)


def ghost_response(side, rad_ref, w_ref, block_ref, messages, weights, wide, source):
    facing = side.facing
    cells = w_ref.shape[1]
    reach = SWEEPS - 1
    tile = slice(side.edge_tile + OWN - side.first, side.edge_tile + OWN - side.first + TILE)
    at = side.edge - OWN - side.edge_tile
    rows = spare_rows(side)
    for i, (slot, row) in enumerate(rows):
        wide[i : i + 1] = messages[0][facing, slot, row : row + 1]
        wide[2 * cells + i : 2 * cells + i + 1] = messages[1][facing, slot, row : row + 1]
    wide[cells : 2 * cells] = block_ref[...]
    source[...] = jnp.zeros(source.shape, jnp.float32)
    for c in range(cells + 2 * reach):
        source[c, at : at + 1] = wide[pl.ds(rad_ref[1] + c, 1), :]
    row = lax.broadcasted_iota(jnp.int32, source.shape[1:], 0)
    weight = [w_ref[facing, j, tile] for j in range(cells)]
    for e in range(2):
        far = weights[e][facing, SWEEPS + 1, side.spare : side.spare + 1]
        beyond = [
            weights[e][facing, SWEEPS, tile],
            weights[e][facing, SWEEPS + 1, tile],
            jnp.where(row == at, far, 0.0),
        ]
        weight = beyond[::-1] + weight if e == 0 else weight + beyond
    given = [source[c] for c in range(cells + 2 * reach)]
    response = [w * g for w, g in zip(weight, given)]
    for n in range(1, SWEEPS):
        old = response
        response = list(old)
        for c in range(n, len(old) - n):
            x = old[c]
            radial = jnp.where(row == 0, 0.0, pltpu.roll(x, 1, 0)) + jnp.where(
                row == TILE - 1, 0.0, pltpu.roll(x, TILE - 1, 0)
            )
            nbr = (old[c - 1] + old[c + 1]) + (radial + axial_sum(x)) + given[c]
            response[c] = (1.0 - OMEGA) * x + weight[c] * nbr
    return response[reach : reach + cells]


def finish(known, rad_ref, p_ref, b_ref, w_ref, stash, cut_ref, block_ref, tile_in, left_ref, right_ref, *rest):
    if known:
        left_w, right_w, _, out_ref, *rest = rest
        weights = (left_w, right_w)
    else:
        cut_in, _, out_ref, cut_out, edge_out, *rest = rest
        weights = (left_ref, right_ref)
    levels, last, inner_tiles, near, near2, wide, source, sems = rest
    messages = (left_ref, right_ref)
    cells, radial_cells = w_ref.shape[1], out_ref.shape[2]

    def column(e, d):
        return d - 1 if e == 0 else cells - d

    def body(side):
        facing = side.facing

        def at(n, e, k, d):
            if n == 0 or d <= n:
                return levels.at[n, e, k, d]
            return stash.at[e, n - 1, k, d - n - 1 if e == 0 else n + 2 - d]

        for e in range(2):
            for k in range(2):
                for d in range(1, 3):
                    target = levels.at[0, e, k, d]
                    if known:
                        target[side.own] = p_ref[k, column(e, d)]
                    else:
                        target[side.own] = p_ref[e, k, d - 1 if e == 0 else SWEEPS - d]
                    target[side.cut] = cut_ref[0, k, column(e, d)]
                    close(target, side, k == facing)
                levels[0, e, k, 0, side.rows] = messages[e][k, 0]
                for buf in (near, near2):
                    buf[e, k] = jnp.zeros(buf.shape[2:], jnp.float32)
        nears = (near, near2)
        for n in range(SWEEPS):
            final = n == SWEEPS - 1
            src, dst = nears[n % 2], nears[1 - n % 2]
            for e in range(2):
                for k in range(2):
                    for d in range(1, n + 2):
                        j = column(e, d)
                        beside = at(n, e, k, d - 1)[side.rows] + at(n, e, k, d + 1)[side.rows]
                        new = relaxed(at(n, e, k, d), side, beside, w_ref[k, j], b_ref[k, j])
                        if final:
                            i = d - 1 if e == 0 else SWEEPS - d
                            last[e, k, i] = new[shifted(side.own, -side.first)]
                        else:
                            levels[n + 1, e, k, d, side.rows] = new
                            close(levels.at[n + 1, e, k, d], side, k == facing)
                    if final:
                        continue
                    beside = at(n, e, k, 1)[side.rows]
                    if n > 0:
                        beside = beside + src[e, k, 1, side.rows]
                        new = relaxed(src.at[e, k, 0], side, beside, weights[e][k, SWEEPS], None)
                    else:
                        new = weights[e][k, SWEEPS] * beside
                    dst[e, k, 0, side.rows] = new
                    levels[n + 1, e, k, 0, side.rows] = messages[e][k, n + 1] + new
                    close(dst.at[e, k, 0], side, k == facing)
                    if n == 1:
                        dst[e, k, 1, side.rows] = (
                            weights[e][k, SWEEPS + 1] * src[e, k, 0, side.rows]
                        )
        response = ghost_response(
            side, rad_ref, w_ref, block_ref, messages, weights, wide, source
        )
        tile = slice(side.edge_tile, side.edge_tile + TILE)
        for e in range(2):
            for i in range(SWEEPS):
                j = end_columns(e, cells, SWEEPS).start + i
                last[e, facing, i, tile] += response[j]
        for i in range(cells - 2 * SWEEPS):
            inner_tiles[i] = tile_in[i] + response[SWEEPS + i]
        copies = [
            pltpu.make_async_copy(
                last.at[e],
                out_ref.at[:, pl.ds(end_columns(e, cells, SWEEPS).start, SWEEPS)],
                sems.at[e],
            )
            for e in range(2)
        ]
        copies.append(
            pltpu.make_async_copy(
                inner_tiles,
                out_ref.at[
                    facing, pl.ds(SWEEPS, cells - 2 * SWEEPS), pl.ds(side.edge_tile, TILE), :
                ],
                sems.at[2],
            )
        )
        for c in copies:
            c.start()
        if not known:
            row = side.edge - OWN
            cut_out[0, :, SWEEPS : cells - SWEEPS] = cut_in[...]
            for i in range(cells - 2 * SWEEPS):
                j = SWEEPS + i
                r = row - side.edge_tile
                edge_out[j : j + 1] = inner_tiles[i, r : r + 1]
            for e in range(2):
                first = end_columns(e, cells, SWEEPS).start
                cut_out[0, :, first : first + SWEEPS] = last[e, :, :, side.sent, :]
                for i in range(SWEEPS):
                    edge_out[first + i : first + i + 1] = last[e, facing, i, row : row + 1]
        for c in copies:
            c.wait()

    on_each_side(rad_ref, radial_cells, body)


def ring(size, step):
    return [(i, (i + step) % size) for i in range(size)]


def facing_pairs(size, turn):
    pairs = []
    for i in range(size):
        pairs.append((2 * ((i - turn) % size) + 1, 2 * i))
        pairs.append((2 * ((i + turn) % size), 2 * i + 1))
    return pairs


def far_pairs(size, turn):
    return [(2 * i + r, 2 * ((i + (2 * r - 1) * turn) % size) + r) for i in range(size) for r in range(2)]


def facing_block(edge, offset, radial_index):
    size = lax.axis_size("az")
    cells = edge.shape[0]
    turn = (offset + cells // 2) // cells
    rest = offset - turn * cells
    turn = turn % size
    near = min(size, 16)

    def far(t):
        return lambda e: lax.ppermute(e, ("az", "rad"), far_pairs(size, t * near))

    def branch(t):
        return lambda e: lax.ppermute(e, ("az", "rad"), facing_pairs(size, t))

    if size > near:
        edge = lax.switch(turn // near, [far(t) for t in range(-(-size // near))], edge)
    block = lax.switch(turn % near, [branch(t) for t in range(near)], edge)
    return block, cells - (SWEEPS - 1) + jnp.where(radial_index == 0, -rest, rest)


def per_device(pressure, source, diagonal, rot_offset):
    _, cells, radial_cells, lanes = pressure.shape
    size = lax.axis_size("az")
    radial_index = lax.axis_index("rad")
    rad = radial_index.astype(jnp.int32).reshape(1)
    rows, span = radial_cells + 4 * TILE, radial_cells + TILE

    def array(*shape):
        return jax.ShapeDtypeStruct(shape, jnp.float32)

    def scratch(*shape):
        return pltpu.VMEM(shape, jnp.float32)

    def pinned(x):
        return pltpu.with_memory_space_constraint(x, pltpu.HBM)

    own = array(*pressure.shape)
    kept = array(2, cells, span, lanes)
    stash = array(2, SWEEPS - 1, 2, 2, rows, lanes)
    cells_in = cells - 2 * SWEEPS
    tiles = array(cells_in, TILE, lanes)
    vmem = pl.BlockSpec(memory_space=pltpu.VMEM)
    smem = pl.BlockSpec(memory_space=pltpu.SMEM)
    hbm = pl.BlockSpec(memory_space=pltpu.HBM)
    anywhere = pl.BlockSpec(memory_space=pl.ANY)
    columns = scratch(2, 2, SWEEPS, rows, lanes)
    three = scratch(2, 2, SWEEPS - 1, span, lanes)

    def call(kernel, out_shape, in_specs, out_specs, scratch_shapes, operands, work_columns, **more):
        work = 2 * work_columns * span * lanes
        return pl.pallas_call(
            kernel,
            out_shape=out_shape,
            in_specs=in_specs,
            out_specs=out_specs,
            scratch_shapes=scratch_shapes,
            compiler_params=pltpu.CompilerParams(vmem_limit_bytes=28 << 20),
            cost_estimate=pl.CostEstimate(
                flops=12 * work, bytes_accessed=8 * work, transcendentals=0
            ),
            **more,
        )(*operands)

    fields = tuple(pinned(x) for x in (pressure, source, diagonal))
    cut, edge, *ends = call(
        pack,
        (
            array(3, 2, cells, SWEEPS, lanes),
            array(cells, lanes),
            array(2, 2, SWEEPS, radial_cells, lanes),
            array(2, 2, SWEEPS - 1, radial_cells, lanes),
            array(2, 2, SWEEPS - 1, radial_cells, lanes),
        ),
        [smem] + [hbm] * 3,
        [vmem] * 2 + [anywhere] * 3,
        [
            scratch(3, 2, cells, TILE, lanes),
            scratch(cells, TILE, lanes),
            pltpu.SemaphoreType.DMA((10,)),
        ],
        (rad, *fields),
        1,
        name="pack",
    )
    for step in range(1, STEPS + 1):
        known = step > 1
        cut = lax.ppermute(cut, "rad", [(0, 1), (1, 0)])
        offset = rot_offset[0] * step % (cells * size)
        block, start = facing_block(edge, offset, radial_index)
        place = jnp.stack([radial_index, start]).astype(jnp.int32)
        message = array(2, SWEEPS if known else SLOTS, span, lanes)
        last, first = call(
            later_edges if known else first_edges,
            (message, message),
            [smem] + [vmem] * 5,
            [vmem] * 2,
            [columns] * 2 + ([] if known else [three] * 2),
            (rad, *(fields if known else ends), cut, block),
            12,
            name="edges",
        )
        left = lax.ppermute(last, "az", ring(size, 1))
        right = lax.ppermute(first, "az", ring(size, -1))
        outs = (own, stash, tiles)
        if not known:
            outs += (array(2, cells_in, SWEEPS, lanes), kept, kept)
        inner, saved, inner_tiles, *made = call(
            later_interior if known else first_interior,
            outs,
            [smem] + ([vmem] * 3 if known else [hbm] * 3) + [vmem],
            [anywhere] + [vmem] * (len(outs) - 1),
            [
                scratch(SWEEPS, 2, cells, rows, lanes),
                scratch(2, cells_in, radial_cells, lanes),
                pltpu.SemaphoreType.DMA((3,)),
            ],
            (rad, *fields, cut),
            44,
            name="interior",
        )
        if not known:
            inner_cut, shift, weight = made
            beyond = (left, right)
        operands = (
            place,
            fields[0] if known else ends[0],
            shift,
            weight,
            saved,
            cut,
            block,
            inner_tiles,
            left,
            right,
        )
        operands += beyond if known else (inner_cut,)
        outs = own if known else (own, array(1, 2, cells, SWEEPS, lanes), array(cells, lanes))
        pressure = call(
            functools.partial(finish, known),
            outs,
            [smem] + [vmem] * (len(operands) - 1) + [anywhere],
            anywhere if known else [anywhere, vmem, vmem],
            [
                scratch(SWEEPS, 2, 2, SWEEPS, rows, lanes),
                scratch(2, 2, SWEEPS, radial_cells, lanes),
                scratch(*tiles.shape),
                scratch(2, 2, 2, rows, lanes),
                scratch(2, 2, 2, rows, lanes),
                scratch(3 * cells, lanes),
                scratch(cells + 2 * (SWEEPS - 1), TILE, lanes),
                pltpu.SemaphoreType.DMA((3,)),
            ],
            (*operands, inner),
            26,
            input_output_aliases={len(operands): 0},
            name="finish",
        )
        if not known:
            pressure, cut, edge = pressure
            fields = (pressure, shift, weight)
    return pressure


def solution(mesh):
    placed = (
        P(None, "az", "rad", None),
        P(None, "az", "rad", None),
        P(None, "az", "rad", None),
        P(),
    )
    return jax.shard_map(
        per_device,
        mesh=mesh,
        in_specs=placed,
        out_specs=P(None, "az", "rad", None),
        check_vma=False,
    )
```

time: 168 us -> 62.2 us (0.37)
  the two profiles are of different devices: /device:TPU:0 before, /device:TPU:1 now
where the time goes in v4:
time: 62.2 us; the launch traced here: 62.7 us
  Pallas kernels  27 us (43%)
  waiting for transfers between devices  19.2 us (31%)
  starting transfers between devices  10.5 us (17%)
  local copies, waits for them, and re-layouts  4.9 us (8%)
  between operations  0.95 us (2%)
    pallas_call x7, Pallas kernels, call(): pl.pallas_call(kernel, out_shape=out_shape, in_specs=in_specs, out_specs=...  27 us
    ppermute x2, waiting for transfers between devices, per_device(): left = lax.ppermute(last, 'az', ring(size, 1))  8.84 us
    ppermute x2, waiting for transfers between devices, branch(): return lambda e: lax.ppermute(e, ('az', 'rad'), facing_pairs(size, t))  7.84 us
    unnamed x16, local copies, waits for them, and re-layouts  4.9 us
    ppermute x2, starting transfers between devices, per_device(): cut = lax.ppermute(cut, 'rad', [(0, 1), (1, 0)])  4.38 us
    ppermute x2, starting transfers between devices, branch(): return lambda e: lax.ppermute(e, ('az', 'rad'), facing_pairs(size, t))  3.08 us
    ppermute x2, starting transfers between devices, per_device(): left = lax.ppermute(last, 'az', ring(size, 1))  3.01 us
    ppermute x2, waiting for transfers between devices, per_device(): right = lax.ppermute(first, 'az', ring(size, -1))  2.48 us
  transfers between devices with their start and end apart: 8, of which 5 were waited for; matrix products, arithmetic and copies ran while one was open for 0% of the time, Pallas kernels for 20%

profile of v4, /device:TPU:1, one launch (start us, length us, event | category | flops | bytes accessed | tf_op | source)
XLA Modules:
  0.0 62.7 jit_solution(3010524651937375420)
XLA Ops:
  0.0 1.8 %pack.1 = (f32[3,2,16,4,128]{4,3,2,1,0:T(4,128)S(1)}, f32[16,128]{1,0:T(8,128)S(1)}, f32[2,2,4,96,128]{4,3,2,1,0:T(8,128)S(1)}, f32[2,2,3,96,128]{4,3,2,1,0:T(8,128)S(1)}, f32[2,2,3,96,128]{4,3,2,1,0:T(8,128)S(1)}) custom-call(s32[1]{0:T(128)} %bitcast.rad_ref, f32[2,16,96,128]{3,2,1,0:T(8,128)} %p_ref.3, f32[2,16,96,128]{3,2,1,0:T(8,128)} %s_ref.3, ...), custom_call_target="tpu_custom_call" | custom-call | flops 319488 | bytes 212992 | tf_op jit(solution)/shard_map/pack/pallas_call | solution.py:538
  1.9 2.1 %collective-permute-start.32 = (f32[3,2,16,4,128]{4,3,2,1,0:T(4,128)S(1)}, f32[3,2,16,4,128]{4,3,2,1,0:T(4,128)S(1)}, u32[]{:S(2)}, u32[]{:S(2)}) collective-permute-start(f32[3,2,16,4,128]{4,3,2,1,0:T(4,128)S(1)} %get-tuple-element.93), channel_id=1, source_target_pairs={{0,1},{1,0},{2,3},{3,2},{4,5},{5,4},{6,7},{7,6},{8,9},{9,8},{10,11... | collective-permute-start | bytes 589832 | tf_op jit(solution)/shard_map/ppermute | solution.py:574
  4.7 5.1 %conditional.2 = (f32[16,128]{1,0:T(8,128)}) conditional(s32[]{:T(128)} %clamp.6, f32[16,128]{1,0:T(8,128)S(1)} %get-tuple-element.97, f32[16,128]{1,0:T(8,128)S(1)} %get-tuple-element.97, f32[16,128]{1,0:T(8,128)S(1)} %get-tuple-element.97, f32[16,128]{1,0:T(8,128)S(1)} %get-tuple-element.97, ...), branch_computations={%region_0.1_spmd, %region_1.2_spmd, %region_2.3_spmd, %region_3.4_... | conditional | bytes 32816 | solution.py:504
  4.7 3.1 %collective-permute-start.11 = (f32[16,128]{1,0:T(8,128)S(1)}, f32[16,128]{1,0:T(8,128)}, u32[]{:S(2)}, u32[]{:S(2)}) collective-permute-start(f32[16,128]{1,0:T(8,128)S(1)} %param.11), channel_id=1, source_target_pairs={{11,0},{22,1},{13,2},{24,3},{15,4},{26,5},{17,6},{28,7},{19,8},{30... | collective-permute-start | bytes 24584 | tf_op jit(solution)/shard_map/cond/branch_11_fun/ppermute | solution.py:500
  7.8 2.0 %collective-permute-done.11 = f32[16,128]{1,0:T(8,128)} collective-permute-done((f32[16,128]{1,0:T(8,128)S(1)}, f32[16,128]{1,0:T(8,128)}, u32[]{:S(2)}, u32[]{:S(2)}) %collective-permute-start.11) | collective-permute-done | bytes 8224 | tf_op jit(solution)/shard_map/cond/branch_11_fun/ppermute | solution.py:500
  9.8 2.7 %edges.2 = (f32[2,6,104,128]{3,2,1,0:T(8,128)}, f32[2,6,104,128]{3,2,1,0:T(8,128)}) custom-call(s32[1]{0:T(128)} %bitcast.rad_ref, f32[2,2,4,96,128]{4,3,2,1,0:T(8,128)S(1)} %get-tuple-element.92.p_ends.p_ref, f32[2,2,3,96,128]{4,3,2,1,0:T(8,128)S(1)} %get-tuple-element.99.s_ends, f32[2,2,3,96,128]{4,3,2,1,0:T(8,128)S(1)} %get-tuple-element.100.d_ends, ...), custom_call_target="tpu_custom_call" | custom-call | flops 3833856 | bytes 2555904 | tf_op jit(solution)/shard_map/edges/pallas_call | solution.py:538
  12.5 1.5 %collective-permute-start.33 = (f32[2,6,104,128]{3,2,1,0:T(8,128)}, f32[2,6,104,128]{3,2,1,0:T(8,128)}, u32[]{:S(2)}, u32[]{:S(2)}) collective-permute-start(f32[2,6,104,128]{3,2,1,0:T(8,128)} %get-tuple-element.101), channel_id=1, source_target_pairs={{0,2},{2,4},{4,6},{6,8},{8,10},{10,12},{12,14},{14,16},{16,18},{18... | collective-permute-start | bytes 1916936 | tf_op jit(solution)/shard_map/ppermute | solution.py:589
  13.9 0.1 pad_add_fusion.1.rad_ref
  14.0 0.9 %copy-done.6 = f32[3,2,16,4,128]{4,3,2,1,0:T(4,128)S(1)} copy-done((f32[3,2,16,4,128]{4,3,2,1,0:T(4,128)S(1)}, f32[3,2,16,4,128]{4,3,2,1,0:T(4,128)}, u32[]{:S(2)}) %copy-start.6) | copy-done | bytes 196632
  14.9 7.3 %interior.2 = (f32[2,16,96,128]{3,2,1,0:T(8,128)S(1)}, f32[2,3,2,2,128,128]{5,4,3,2,1,0:T(8,128)S(1)}, f32[8,8,128]{2,1,0:T(8,128)S(1)}, f32[2,8,4,128]{3,2,1,0:...) custom-call(s32[1]{0:T(128)} %bitcast.rad_ref, f32[2,16,96,128]{3,2,1,0:T(8,128)} %p_ref.3, ...), custom_call_target="tpu_custom_call" | custom-call | flops 14057472 | bytes 9371648 | tf_op jit(solution)/shard_map/interior/pallas_call | solution.py:538
  22.2 6.2 %collective-permute-done.33.left_ref.rest_0_ = f32[2,6,104,128]{3,2,1,0:T(8,128)} collective-permute-done((f32[2,6,104,128]{3,2,1,0:T(8,128)}, f32[2,6,104,128]{3,2,1,0:T(8,128)}, u32[]{:S(2)}, u32[]{:S(2)}) %collective-permute-start.33) | collective-permute-done | bytes 639008 | tf_op jit(solution)/shard_map/ppermute | solution.py:589
  28.4 2.5 %collective-permute-done.34.right_ref.rest_1_ = f32[2,6,104,128]{3,2,1,0:T(8,128)} collective-permute-done((f32[2,6,104,128]{3,2,1,0:T(8,128)}, f32[2,6,104,128]{3,2,1,0:T(8,128)}, u32[]{:S(2)}, u32[]{:S(2)}) %collective-permute-start.34) | collective-permute-done | bytes 639008 | tf_op jit(solution)/shard_map/ppermute | solution.py:590
  30.9 3.1 %finish.2 = (f32[2,16,96,128]{3,2,1,0:T(8,128)S(1)}, f32[1,2,16,4,128]{4,3,2,1,0:T(4,128)S(1)}, f32[16,128]{1,0:T(8,128)S(1)}) custom-call(s32[2]{0:T(128)S(1)} %pad_add_fusion.1.rad_ref, f32[2,2,4,96,128]{4,3,2,1,0:T(8,128)S(1)} %copy-done.4, f32[2,16,104,128]{3,2,1,0:T(8,128)S(1)} %get-tuple-element.94.b_ref, ...), custom_call_target="tpu_custom_call", output_to_operand_aliasing={{0}: (11, {})} | custom-call | flops 8306688 | bytes 5537792 | tf_op jit(solution)/shard_map/finish/pallas_call | solution.py:538
  34.1 1.1 %copy-done = f32[2,16,96,128]{3,2,1,0:T(8,128)} copy-done((f32[2,16,96,128]{3,2,1,0:T(8,128)}, f32[2,16,96,128]{3,2,1,0:T(8,128)S(1)}, u32[]{:S(2)}) %copy-start) | copy-done | bytes 1572888
  35.2 2.2 %collective-permute-start.35 = (f32[1,2,16,4,128]{4,3,2,1,0:T(4,128)S(1)}, f32[1,2,16,4,128]{4,3,2,1,0:T(4,128)S(1)}, u32[]{:S(2)}, u32[]{:S(2)}) collective-permute-start(f32[1,2,16,4,128]{4,3,2,1,0:T(4,128)S(1)} %get-tuple-element.106), channel_id=1, source_target_pairs={{0,1},{1,0},{2,3},{3,2},{4,5},{5,4},{6,7},{7,6},{8,9},{9,8},{10,11... | collective-permute-start | bytes 196616 | tf_op jit(solution)/shard_map/ppermute | solution.py:574
  37.5 5.9 %conditional.3 = (f32[16,128]{1,0:T(8,128)}) conditional(s32[]{:T(128)} %clamp.7, f32[16,128]{1,0:T(8,128)S(1)} %get-tuple-element.108, f32[16,128]{1,0:T(8,128)S(1)} %get-tuple-element.108, f32[16,128]{1,0:T(8,128)S(1)} %get-tuple-element.108, f32[16,128]{1,0:T(8,128)S(1)} %get-tuple-element.108, ...), branch_computations={%region_16.17_spmd, %region_17.18_spmd, %region_18.19_spmd, %regio... | conditional | bytes 32816 | solution.py:504
  37.5 5.9 %collective-permute-done.21 = f32[16,128]{1,0:T(8,128)} collective-permute-done((f32[16,128]{1,0:T(8,128)S(1)}, f32[16,128]{1,0:T(8,128)}, u32[]{:S(2)}, u32[]{:S(2)}) %collective-permute-start.21) | collective-permute-done | bytes 8224 | tf_op jit(solution)/shard_map/cond/branch_5_fun/ppermute | solution.py:500
  43.3 1.4 %copy-done.1 = f32[2,16,96,128]{3,2,1,0:T(8,128)S(1)} copy-done((f32[2,16,96,128]{3,2,1,0:T(8,128)S(1)}, f32[2,16,96,128]{3,2,1,0:T(8,128)}, u32[]{:S(2)}) %copy-start.1) | copy-done | bytes 1572888
  44.7 2.6 %edges.3 = (f32[2,4,104,128]{3,2,1,0:T(8,128)}, f32[2,4,104,128]{3,2,1,0:T(8,128)}) custom-call(s32[1]{0:T(128)} %bitcast.rad_ref, f32[2,16,96,128]{3,2,1,0:T(8,128)S(1)} %copy-done.1, f32[2,16,104,128]{3,2,1,0:T(8,128)S(1)} %get-tuple-element.94.b_ref, f32[2,16,104,128]{3,2,1,0:T(8,128)S(1)} %get-tuple-element.95.w_ref, ...), custom_call_target="tpu_custom_call" | custom-call | flops 3833856 | bytes 2555904 | tf_op jit(solution)/shard_map/edges/pallas_call | solution.py:538
  47.3 1.6 %collective-permute-start.36 = (f32[2,4,104,128]{3,2,1,0:T(8,128)}, f32[2,4,104,128]{3,2,1,0:T(8,128)}, u32[]{:S(2)}, u32[]{:S(2)}) collective-permute-start(f32[2,4,104,128]{3,2,1,0:T(8,128)} %get-tuple-element.110), channel_id=1, source_target_pairs={{0,2},{2,4},{4,6},{6,8},{8,10},{10,12},{12,14},{14,16},{16,18},{18... | collective-permute-start | bytes 1277960 | tf_op jit(solution)/shard_map/ppermute | solution.py:589
  49.0 1.4 %copy-done.2 = f32[2,16,96,128]{3,2,1,0:T(8,128)S(1)} copy-done((f32[2,16,96,128]{3,2,1,0:T(8,128)S(1)}, f32[2,16,96,128]{3,2,1,0:T(8,128)}, u32[]{:S(2)}) %copy-start.2) | copy-done | bytes 1572888
  50.4 5.3 %interior.3 = (f32[2,16,96,128]{3,2,1,0:T(8,128)}, f32[2,3,2,2,128,128]{5,4,3,2,1,0:T(8,128)S(1)}, f32[8,8,128]{2,1,0:T(8,128)S(1)}) custom-call(s32[1]{0:T(128)} %bitcast.rad_ref, f32[2,16,96,128]{3,2,1,0:T(8,128)S(1)} %copy-done.2, f32[2,16,104,128]{3,2,1,0:T(8,128)S(1)} %get-tuple-element.94.b_ref, f32[2,16,104,128]{3,2,1,0:T(8,128)S(1)} %get-tuple-element.95.w_ref, ...), custom_call_target="tpu_custom_call" | custom-call | flops 14057472 | bytes 9371648 | tf_op jit(solution)/shard_map/interior/pallas_call | solution.py:538
  55.7 2.6 %collective-permute-done.36.left_ref = f32[2,4,104,128]{3,2,1,0:T(8,128)} collective-permute-done((f32[2,4,104,128]{3,2,1,0:T(8,128)}, f32[2,4,104,128]{3,2,1,0:T(8,128)}, u32[]{:S(2)}, u32[]{:S(2)}) %collective-permute-start.36) | collective-permute-done | bytes 426016 | tf_op jit(solution)/shard_map/ppermute | solution.py:589
  58.4 4.2 %finish.3 = f32[2,16,96,128]{3,2,1,0:T(8,128)} custom-call(s32[2]{0:T(128)S(1)} %pad_add_fusion.rad_ref, f32[2,16,96,128]{3,2,1,0:T(8,128)S(1)} %copy-done.2, f32[2,16,104,128]{3,2,1,0:T(8,128)S(1)} %get-tuple-element.94.b_ref, f32[2,16,104,128]{3,2,1,0:T(8,128)S(1)} %get-tuple-element.95.w_ref, ...), custom_call_target="tpu_custom_call", output_to_operand_aliasing={{}: (12, {})} | custom-call | flops 8306688 | bytes 5537792 | tf_op jit(solution)/shard_map/finish/pallas_call | solution.py:538
  (19 shorter events, 0.1 us)
Async XLA Ops:
  1.8 12.1 %copy-start.3 = (f32[2,2,4,96,128]{4,3,2,1,0:T(8,128)}, f32[2,2,4,96,128]{4,3,2,1,0:T(8,128)S(1)}, u32[]{:S(2)}) copy-start(f32[2,2,4,96,128]{4,3,2,1,0:T(8,128)S(1)} %get-tuple-element.92.p_ends.p_ref) | copy-start | bytes 2359300
  1.9 7.9 %collective-permute-start.32 = (f32[3,2,16,4,128]{4,3,2,1,0:T(4,128)S(1)}, f32[3,2,16,4,128]{4,3,2,1,0:T(4,128)S(1)}, u32[]{:S(2)}, u32[]{:S(2)}) collective-permute-start(f32[3,2,16,4,128]{4,3,2,1,0:T(4,128)S(1)} %get-tuple-element.93), channel_id=1, source_target_pairs={{0,1},{1,0},{2,3},{3,2},{4,5},{5,4},{6,7},{7,6},{8,9},{9,8},{10,11... | collective-permute-start | bytes 589832 | tf_op jit(solution)/shard_map/ppermute | solution.py:574
  4.7 5.0 %collective-permute-start.11 = (f32[16,128]{1,0:T(8,128)S(1)}, f32[16,128]{1,0:T(8,128)}, u32[]{:S(2)}, u32[]{:S(2)}) collective-permute-start(f32[16,128]{1,0:T(8,128)S(1)} %param.11), channel_id=1, source_target_pairs={{11,0},{22,1},{13,2},{24,3},{15,4},{26,5},{17,6},{28,7},{19,8},{30... | collective-permute-start | bytes 24584 | tf_op jit(solution)/shard_map/cond/branch_11_fun/ppermute | solution.py:500
  9.8 4.1 %copy-start.5 = (f32[3,2,16,4,128]{4,3,2,1,0:T(4,128)}, f32[3,2,16,4,128]{4,3,2,1,0:T(4,128)S(1)}, u32[]{:S(2)}) copy-start(f32[3,2,16,4,128]{4,3,2,1,0:T(4,128)S(1)} %collective-permute-done.32.cut_ref) | copy-start | bytes 589828
  12.5 16.0 %collective-permute-start.33 = (f32[2,6,104,128]{3,2,1,0:T(8,128)}, f32[2,6,104,128]{3,2,1,0:T(8,128)}, u32[]{:S(2)}, u32[]{:S(2)}) collective-permute-start(f32[2,6,104,128]{3,2,1,0:T(8,128)} %get-tuple-element.101), channel_id=1, source_target_pairs={{0,2},{2,4},{4,6},{6,8},{8,10},{10,12},{12,14},{14,16},{16,18},{18... | collective-permute-start | bytes 1916936 | tf_op jit(solution)/shard_map/ppermute | solution.py:589
  13.9 17.0 %collective-permute-start.34 = (f32[2,6,104,128]{3,2,1,0:T(8,128)}, f32[2,6,104,128]{3,2,1,0:T(8,128)}, u32[]{:S(2)}, u32[]{:S(2)}) collective-permute-start(f32[2,6,104,128]{3,2,1,0:T(8,128)} %get-tuple-element.102), channel_id=1, source_target_pairs={{0,30},{2,0},{4,2},{6,4},{8,6},{10,8},{12,10},{14,12},{16,14},{18,... | collective-permute-start | bytes 1916936 | tf_op jit(solution)/shard_map/ppermute | solution.py:590
  14.0 0.9 %copy-start.6 = (f32[3,2,16,4,128]{4,3,2,1,0:T(4,128)S(1)}, f32[3,2,16,4,128]{4,3,2,1,0:T(4,128)}, u32[]{:S(2)}) copy-start(f32[3,2,16,4,128]{4,3,2,1,0:T(4,128)} %copy-done.5) | copy-start | bytes 589828
  14.9 16.0 %copy-start.4 = (f32[2,2,4,96,128]{4,3,2,1,0:T(8,128)S(1)}, f32[2,2,4,96,128]{4,3,2,1,0:T(8,128)}, u32[]{:S(2)}) copy-start(f32[2,2,4,96,128]{4,3,2,1,0:T(8,128)} %copy-done.3) | copy-start | bytes 2359300
  14.9 16.0 %copy-start.7 = (f32[3,2,16,4,128]{4,3,2,1,0:T(4,128)S(1)}, f32[3,2,16,4,128]{4,3,2,1,0:T(4,128)}, u32[]{:S(2)}) copy-start(f32[3,2,16,4,128]{4,3,2,1,0:T(4,128)} %copy-done.5) | copy-start | bytes 589828
  34.1 1.1 %copy-start = (f32[2,16,96,128]{3,2,1,0:T(8,128)}, f32[2,16,96,128]{3,2,1,0:T(8,128)S(1)}, u32[]{:S(2)}) copy-start(f32[2,16,96,128]{3,2,1,0:T(8,128)S(1)} %get-tuple-element.105.p_ref) | copy-start | bytes 4718596
  35.2 8.1 %collective-permute-start.35 = (f32[1,2,16,4,128]{4,3,2,1,0:T(4,128)S(1)}, f32[1,2,16,4,128]{4,3,2,1,0:T(4,128)S(1)}, u32[]{:S(2)}, u32[]{:S(2)}) collective-permute-start(f32[1,2,16,4,128]{4,3,2,1,0:T(4,128)S(1)} %get-tuple-element.106), channel_id=1, source_target_pairs={{0,1},{1,0},{2,3},{3,2},{4,5},{5,4},{6,7},{7,6},{8,9},{9,8},{10,11... | collective-permute-start | bytes 196616 | tf_op jit(solution)/shard_map/ppermute | solution.py:574
  37.5 5.9 %collective-permute-start.21 = (f32[16,128]{1,0:T(8,128)S(1)}, f32[16,128]{1,0:T(8,128)}, u32[]{:S(2)}, u32[]{:S(2)}) collective-permute-start(f32[16,128]{1,0:T(8,128)S(1)} %param.21), channel_id=1, source_target_pairs={{23,0},{10,1},{25,2},{12,3},{27,4},{14,5},{29,6},{16,7},{31,8},{18... | collective-permute-start | bytes 24584 | tf_op jit(solution)/shard_map/cond/branch_5_fun/ppermute | solution.py:500
  43.3 1.4 %copy-start.1 = (f32[2,16,96,128]{3,2,1,0:T(8,128)S(1)}, f32[2,16,96,128]{3,2,1,0:T(8,128)}, u32[]{:S(2)}) copy-start(f32[2,16,96,128]{3,2,1,0:T(8,128)} %copy-done) | copy-start | bytes 4718596
  47.3 11.0 %collective-permute-start.36 = (f32[2,4,104,128]{3,2,1,0:T(8,128)}, f32[2,4,104,128]{3,2,1,0:T(8,128)}, u32[]{:S(2)}, u32[]{:S(2)}) collective-permute-start(f32[2,4,104,128]{3,2,1,0:T(8,128)} %get-tuple-element.110), channel_id=1, source_target_pairs={{0,2},{2,4},{4,6},{6,8},{8,10},{10,12},{12,14},{14,16},{16,18},{18... | collective-permute-start | bytes 1277960 | tf_op jit(solution)/shard_map/ppermute | solution.py:589
  48.9 9.5 %collective-permute-start.37 = (f32[2,4,104,128]{3,2,1,0:T(8,128)}, f32[2,4,104,128]{3,2,1,0:T(8,128)}, u32[]{:S(2)}, u32[]{:S(2)}) collective-permute-start(f32[2,4,104,128]{3,2,1,0:T(8,128)} %get-tuple-element.111), channel_id=1, source_target_pairs={{0,30},{2,0},{4,2},{6,4},{8,6},{10,8},{12,10},{14,12},{16,14},{18,... | collective-permute-start | bytes 1277960 | tf_op jit(solution)/shard_map/ppermute | solution.py:590
  49.0 1.4 %copy-start.2 = (f32[2,16,96,128]{3,2,1,0:T(8,128)S(1)}, f32[2,16,96,128]{3,2,1,0:T(8,128)}, u32[]{:S(2)}) copy-start(f32[2,16,96,128]{3,2,1,0:T(8,128)} %copy-done) | copy-start | bytes 4718596

commit v5 on v4

--- a/solution.py
+++ b/solution.py
@@ -60,12 +60,14 @@
     column[side.ghost : side.ghost + 1] = column[side.edge : side.edge + 1]
 
 
-def on_each_side(rad_ref, radial_cells, body):
-    @pl.when(rad_ref[0] == 0)
+def on_each_side(radial_cells, body):
+    low = lax.axis_index("rad") == 0
+
+    @pl.when(low)
     def _():
         body(Side(True, radial_cells))
 
-    @pl.when(rad_ref[0] != 0)
+    @pl.when(jnp.logical_not(low))
     def _():
         body(Side(False, radial_cells))
 
@@ -128,7 +130,7 @@
                 )[row : row + 1]
 
 
-def pack(rad_ref, p_ref, s_ref, d_ref, cut_ref, edge_ref, p_ends, s_ends, d_ends, tiles, edge_tiles, sems):
+def pack(p_ref, s_ref, d_ref, cut_ref, edge_ref, p_ends, s_ends, d_ends, tiles, edge_tiles, sems):
     cells, radial_cells = p_ref.shape[1:3]
 
     def body(side):
@@ -152,7 +154,7 @@
         for j in range(cells):
             edge_ref[j : j + 1] = edge_tiles[j, at : at + 1]
 
-    on_each_side(rad_ref, radial_cells, body)
+    on_each_side(radial_cells, body)
 
 
 def fill_ends(field, side, p_column, cut_ref, cells, radial_cells):
@@ -164,20 +166,23 @@
                 field[edge, k, i, side.cut] = cut_ref[0, k, columns.start + i]
 
 
-def send_block(side, block_ref, messages):
+def send_block(side, arriving, block_ref, messages):
+    arriving.wait()
     for message in messages:
         for i, (slot, row) in enumerate(spare_rows(side)):
             message[side.facing, slot, row : row + 1] = block_ref[i : i + 1]
 
 
 def first_edges(
-    rad_ref, p_ends, s_ends, d_ends, cut_ref, block_ref, last, first, field, other, weight, shift
+    p_ends, s_ends, d_ends, cut_ref, block_ref, last, first, block, sem, field, other, weight, shift
 ):
     radial_cells = p_ends.shape[3]
     cells = cut_ref.shape[2]
     n = SWEEPS - 1
 
     def body(side):
+        arriving = pltpu.make_async_copy(block_ref, block, sem)
+        arriving.start()
         own = shifted(side.own, -side.first)
         cut = shifted(side.cut, -side.first)
         fill_ends(field, side, lambda e, k, i: p_ends[e, k, i], cut_ref, cells, radial_cells)
@@ -200,15 +205,17 @@
             lambda e, k, i: shift[e, k, i],
             (first, last),
         )
-        send_block(side, block_ref, (first, last))
-
-    on_each_side(rad_ref, radial_cells, body)
-
-
-def later_edges(rad_ref, p_ref, b_ref, w_ref, cut_ref, block_ref, last, first, field, other):
+        send_block(side, arriving, block, (first, last))
+
+    on_each_side(radial_cells, body)
+
+
+def later_edges(p_ref, b_ref, w_ref, cut_ref, block_ref, last, first, block, sem, field, other):
     cells, radial_cells = p_ref.shape[1:3]
 
     def body(side):
+        arriving = pltpu.make_async_copy(block_ref, block, sem)
+        arriving.start()
         fill_ends(
             field,
             side,
@@ -225,9 +232,9 @@
             lambda e, k, i: b_ref[k, end_columns(e, cells, SWEEPS - 1).start + i],
             (first, last),
         )
-        send_block(side, block_ref, (first, last))
-
-    on_each_side(rad_ref, radial_cells, body)
+        send_block(side, arriving, block, (first, last))
+
+    on_each_side(radial_cells, body)
 
 
 def inner_sweeps(side, levels, weight, shift, last, out_ref, stash, tile_out, sems):
@@ -269,7 +276,7 @@
 
 
 def first_interior(
-    rad_ref, p_ref, s_ref, d_ref, cut_ref, out_ref, stash, tile_out, cut_out, b_out, w_out, levels, last, sems
+    p_ref, s_ref, d_ref, cut_ref, out_ref, stash, tile_out, cut_out, b_out, w_out, levels, last, sems
 ):
     cells, radial_cells = p_ref.shape[1:3]
 
@@ -301,11 +308,11 @@
         cut_out[...] = last[:, :, side.sent, :]
         inner.wait()
 
-    on_each_side(rad_ref, radial_cells, body)
+    on_each_side(radial_cells, body)
 
 
 def later_interior(
-    rad_ref, p_ref, b_ref, w_ref, cut_ref, out_ref, stash, tile_out, levels, last, sems
+    p_ref, b_ref, w_ref, cut_ref, out_ref, stash, tile_out, levels, last, sems
 ):
     cells, radial_cells = p_ref.shape[1:3]
 
@@ -314,10 +321,10 @@
         levels[0, :, :, side.cut, :] = cut_ref[0]
         inner_sweeps(side, levels, w_ref, b_ref, last, out_ref, stash, tile_out, sems).wait()
 
-    on_each_side(rad_ref, radial_cells, body)
-
-
-def ghost_response(side, rad_ref, w_ref, block_ref, messages, weights, wide, source):
+    on_each_side(radial_cells, body)
+
+
+def ghost_response(side, start_ref, w_ref, block_ref, messages, weights, wide, source):
     facing = side.facing
     cells = w_ref.shape[1]
     reach = SWEEPS - 1
@@ -330,7 +337,7 @@
     wide[cells : 2 * cells] = block_ref[...]
     source[...] = jnp.zeros(source.shape, jnp.float32)
     for c in range(cells + 2 * reach):
-        source[c, at : at + 1] = wide[pl.ds(rad_ref[1] + c, 1), :]
+        source[c, at : at + 1] = wide[pl.ds(start_ref[0] + c, 1), :]
     row = lax.broadcasted_iota(jnp.int32, source.shape[1:], 0)
     weight = [w_ref[facing, j, tile] for j in range(cells)]
     for e in range(2):
@@ -356,7 +363,7 @@
     return response[reach : reach + cells]
 
 
-def finish(known, rad_ref, p_ref, b_ref, w_ref, stash, cut_ref, block_ref, tile_in, left_ref, right_ref, *rest):
+def finish(known, start_ref, p_ref, b_ref, w_ref, stash, cut_ref, block_ref, tile_in, left_ref, right_ref, *rest):
     if known:
         left_w, right_w, _, out_ref, *rest = rest
         weights = (left_w, right_w)
@@ -423,7 +430,7 @@
                             weights[e][k, SWEEPS + 1] * src[e, k, 0, side.rows]
                         )
         response = ghost_response(
-            side, rad_ref, w_ref, block_ref, messages, weights, wide, source
+            side, start_ref, w_ref, block_ref, messages, weights, wide, source
         )
         tile = slice(side.edge_tile, side.edge_tile + TILE)
         for e in range(2):
@@ -466,7 +473,7 @@
         for c in copies:
             c.wait()
 
-    on_each_side(rad_ref, radial_cells, body)
+    on_each_side(radial_cells, body)
 
 
 def ring(size, step):
@@ -509,7 +516,6 @@
     _, cells, radial_cells, lanes = pressure.shape
     size = lax.axis_size("az")
     radial_index = lax.axis_index("rad")
-    rad = radial_index.astype(jnp.int32).reshape(1)
     rows, span = radial_cells + 4 * TILE, radial_cells + TILE
 
     def array(*shape):
@@ -521,7 +527,6 @@
     def pinned(x):
         return pltpu.with_memory_space_constraint(x, pltpu.HBM)
 
-    own = array(*pressure.shape)
     kept = array(2, cells, span, lanes)
     stash = array(2, SWEEPS - 1, 2, 2, rows, lanes)
     cells_in = cells - 2 * SWEEPS
@@ -558,14 +563,14 @@
             array(2, 2, SWEEPS - 1, radial_cells, lanes),
             array(2, 2, SWEEPS - 1, radial_cells, lanes),
         ),
-        [smem] + [hbm] * 3,
+        [hbm] * 3,
         [vmem] * 2 + [anywhere] * 3,
         [
             scratch(3, 2, cells, TILE, lanes),
             scratch(cells, TILE, lanes),
             pltpu.SemaphoreType.DMA((10,)),
         ],
-        (rad, *fields),
+        fields,
         1,
         name="pack",
     )
@@ -574,34 +579,36 @@
         cut = lax.ppermute(cut, "rad", [(0, 1), (1, 0)])
         offset = rot_offset[0] * step % (cells * size)
         block, start = facing_block(edge, offset, radial_index)
-        place = jnp.stack([radial_index, start]).astype(jnp.int32)
+        place = start.astype(jnp.int32).reshape(1)
         message = array(2, SWEEPS if known else SLOTS, span, lanes)
         last, first = call(
             later_edges if known else first_edges,
             (message, message),
-            [smem] + [vmem] * 5,
+            [vmem] * 4 + [anywhere],
             [vmem] * 2,
-            [columns] * 2 + ([] if known else [three] * 2),
-            (rad, *(fields if known else ends), cut, block),
+            [scratch(cells, lanes), pltpu.SemaphoreType.DMA, columns, columns]
+            + ([] if known else [three] * 2),
+            (*(fields if known else ends), cut, block),
             12,
             name="edges",
         )
         left = lax.ppermute(last, "az", ring(size, 1))
         right = lax.ppermute(first, "az", ring(size, -1))
-        outs = (own, stash, tiles)
+        result = array(*pressure.shape) if known else pltpu.VMEM(pressure.shape, jnp.float32)
+        outs = (result, stash, tiles)
         if not known:
             outs += (array(2, cells_in, SWEEPS, lanes), kept, kept)
         inner, saved, inner_tiles, *made = call(
             later_interior if known else first_interior,
             outs,
-            [smem] + ([vmem] * 3 if known else [hbm] * 3) + [vmem],
+            ([vmem] * 3 if known else [hbm] * 3) + [vmem],
             [anywhere] + [vmem] * (len(outs) - 1),
             [
                 scratch(SWEEPS, 2, cells, rows, lanes),
                 scratch(2, cells_in, radial_cells, lanes),
                 pltpu.SemaphoreType.DMA((3,)),
             ],
-            (rad, *fields, cut),
+            (*fields, cut),
             44,
             name="interior",
         )
@@ -621,7 +628,7 @@
             right,
         )
         operands += beyond if known else (inner_cut,)
-        outs = own if known else (own, array(1, 2, cells, SWEEPS, lanes), array(cells, lanes))
+        outs = result if known else (result, array(1, 2, cells, SWEEPS, lanes), array(cells, lanes))
         pressure = call(
             functools.partial(finish, known),
             outs,
@@ -644,7 +651,11 @@
         )
         if not known:
             pressure, cut, edge = pressure
-            fields = (pressure, shift, weight)
+            fields = (
+                pltpu.with_memory_space_constraint(pressure, pltpu.VMEM),
+                shift,
+                weight,
+            )
     return pressure
 
 

time: 62.2 us -> 60.8 us (0.977); the launches traced: 62.7 us -> 60.1 us
  waiting for transfers between devices: 19.2 us -> 17.8 us
  Pallas kernels: 27 us -> 26 us
    ppermute x2, waiting for transfers between devices: 7.84 us -> 6.19 us  [branch(): return lambda e: lax.ppermute(e, ('az', 'rad'), facing_pairs(size, t))]
    ppermute x2, starting transfers between devices: 3.01 us -> 4.36 us  [per_device(): left = lax.ppermute(last, 'az', ring(size, 1))]
    ppermute x2, starting transfers between devices: 3.08 us -> 1.9 us  [branch(): return lambda e: lax.ppermute(e, ('az', 'rad'), facing_pairs(size, t))]
    pallas_call x7, Pallas kernels: 27 us -> 26 us  [call(): pl.pallas_call(kernel, out_shape=out_shape, in_specs=in_specs, out_specs=...]
  transfers between devices with their start and end apart: 8 -> 8, of which waited for: 5 -> 6; matrix products, arithmetic and copies ran while one was open for 0% -> 0% of each run, Pallas kernels for 20% -> 21%
where the time goes in v5:
time: 60.8 us; the launch traced here: 60.1 us
  Pallas kernels  26 us (43%)
  waiting for transfers between devices  17.8 us (29%)
  starting transfers between devices  10.4 us (17%)
  local copies, waits for them, and re-layouts  4.89 us (8%)
  between operations  0.97 us (2%)
    pallas_call x7, Pallas kernels, call(): pl.pallas_call(kernel, out_shape=out_shape, in_specs=in_specs, out_specs=...  26 us
    ppermute x2, waiting for transfers between devices, per_device(): left = lax.ppermute(last, 'az', ring(size, 1))  8.86 us
    ppermute x2, waiting for transfers between devices, branch(): return lambda e: lax.ppermute(e, ('az', 'rad'), facing_pairs(size, t))  6.19 us
    unnamed x16, local copies, waits for them, and re-layouts  4.89 us
    ppermute x2, starting transfers between devices, per_device(): left = lax.ppermute(last, 'az', ring(size, 1))  4.36 us
    ppermute x2, starting transfers between devices, per_device(): cut = lax.ppermute(cut, 'rad', [(0, 1), (1, 0)])  4.15 us
    ppermute x2, waiting for transfers between devices, per_device(): right = lax.ppermute(first, 'az', ring(size, -1))  2.48 us
    ppermute x2, starting transfers between devices, branch(): return lambda e: lax.ppermute(e, ('az', 'rad'), facing_pairs(size, t))  1.9 us
  transfers between devices with their start and end apart: 8, of which 6 were waited for; matrix products, arithmetic and copies ran while one was open for 0% of the time, Pallas kernels for 21%

profile of v5, /device:TPU:1, one launch (start us, length us, event | category | flops | bytes accessed | tf_op | source)
XLA Modules:
  0.0 60.1 jit_solution(9081049043239778520)
XLA Ops:
  0.0 1.8 %pack.1 = (f32[3,2,16,4,128]{4,3,2,1,0:T(4,128)S(1)}, f32[16,128]{1,0:T(8,128)S(1)}, f32[2,2,4,96,128]{4,3,2,1,0:T(8,128)S(1)}, f32[2,2,3,96,128]{4,3,2,1,0:T(8,128)S(1)}, f32[2,2,3,96,128]{4,3,2,1,0:T(8,128)S(1)}) custom-call(f32[2,16,96,128]{3,2,1,0:T(8,128)} %p_ref.3, f32[2,16,96,128]{3,2,1,0:T(8,128)} %s_ref.3, f32[2,16,96,128]{3,2,1,0:T(8,128)} %d_ref.3), custom_call_target="tpu_custom_call" | custom-call | flops 319488 | bytes 212992 | tf_op jit(solution)/shard_map/pack/pallas_call | solution.py:543
  1.8 2.1 %collective-permute-start.32 = (f32[3,2,16,4,128]{4,3,2,1,0:T(4,128)S(1)}, f32[3,2,16,4,128]{4,3,2,1,0:T(4,128)S(1)}, u32[]{:S(2)}, u32[]{:S(2)}) collective-permute-start(f32[3,2,16,4,128]{4,3,2,1,0:T(4,128)S(1)} %get-tuple-element.93), channel_id=1, source_target_pairs={{0,1},{1,0},{2,3},{3,2},{4,5},{5,4},{6,7},{7,6},{8,9},{9,8},{10,11... | collective-permute-start | bytes 589832 | tf_op jit(solution)/shard_map/ppermute | solution.py:579
  4.7 3.7 %conditional.2 = (f32[16,128]{1,0:T(8,128)}) conditional(s32[]{:T(128)} %clamp.6, f32[16,128]{1,0:T(8,128)S(1)} %get-tuple-element.97, f32[16,128]{1,0:T(8,128)S(1)} %get-tuple-element.97, f32[16,128]{1,0:T(8,128)S(1)} %get-tuple-element.97, f32[16,128]{1,0:T(8,128)S(1)} %get-tuple-element.97, ...), branch_computations={%region_0.1_spmd, %region_1.2_spmd, %region_2.3_spmd, %region_3.4_... | conditional | bytes 32816 | solution.py:511
  4.7 1.3 %collective-permute-start.12 = (f32[16,128]{1,0:T(8,128)S(1)}, f32[16,128]{1,0:T(8,128)}, u32[]{:S(2)}, u32[]{:S(2)}) collective-permute-start(f32[16,128]{1,0:T(8,128)S(1)} %param.12), channel_id=1, source_target_pairs={{9,0},{24,1},{11,2},{26,3},{13,4},{28,5},{15,6},{30,7},{17,8},{0,9... | collective-permute-start | bytes 24584 | tf_op jit(solution)/shard_map/cond/branch_12_fun/ppermute | solution.py:507
  6.0 2.4 %collective-permute-done.12 = f32[16,128]{1,0:T(8,128)} collective-permute-done((f32[16,128]{1,0:T(8,128)S(1)}, f32[16,128]{1,0:T(8,128)}, u32[]{:S(2)}, u32[]{:S(2)}) %collective-permute-start.12) | collective-permute-done | bytes 8224 | tf_op jit(solution)/shard_map/cond/branch_12_fun/ppermute | solution.py:507
  8.7 2.6 %edges.2 = (f32[2,6,104,128]{3,2,1,0:T(8,128)}, f32[2,6,104,128]{3,2,1,0:T(8,128)}) custom-call(f32[2,2,4,96,128]{4,3,2,1,0:T(8,128)S(1)} %get-tuple-element.92.p_ends.p_ref, f32[2,2,3,96,128]{4,3,2,1,0:T(8,128)S(1)} %get-tuple-element.99.s_ends, f32[2,2,3,96,128]{4,3,2,1,0:T(8,128)S(1)} %get-tuple-element.100.d_ends, ...), custom_call_target="tpu_custom_call" | custom-call | flops 3833856 | bytes 2555904 | tf_op jit(solution)/shard_map/edges/pallas_call | solution.py:543
  11.3 2.9 %collective-permute-start.33 = (f32[2,6,104,128]{3,2,1,0:T(8,128)}, f32[2,6,104,128]{3,2,1,0:T(8,128)}, u32[]{:S(2)}, u32[]{:S(2)}) collective-permute-start(f32[2,6,104,128]{3,2,1,0:T(8,128)} %get-tuple-element.101), channel_id=1, source_target_pairs={{0,2},{2,4},{4,6},{6,8},{8,10},{10,12},{12,14},{14,16},{16,18},{18... | collective-permute-start | bytes 1916936 | tf_op jit(solution)/shard_map/ppermute | solution.py:595
  14.2 0.9 %copy-done.6 = f32[3,2,16,4,128]{4,3,2,1,0:T(4,128)S(1)} copy-done((f32[3,2,16,4,128]{4,3,2,1,0:T(4,128)S(1)}, f32[3,2,16,4,128]{4,3,2,1,0:T(4,128)}, u32[]{:S(2)}) %copy-start.6) | copy-done | bytes 196632
  15.1 7.3 %interior.2 = (f32[2,16,96,128]{3,2,1,0:T(8,128)S(1)}, f32[2,3,2,2,128,128]{5,4,3,2,1,0:T(8,128)S(1)}, f32[8,8,128]{2,1,0:T(8,128)S(1)}, f32[2,8,4,128]{3,2,1,0:...) custom-call(f32[2,16,96,128]{3,2,1,0:T(8,128)} %p_ref.3, f32[2,16,96,128]{3,2,1,0:T(8,128)} %s_ref.3, ...), custom_call_target="tpu_custom_call" | custom-call | flops 14057472 | bytes 9371648 | tf_op jit(solution)/shard_map/interior/pallas_call | solution.py:543
  22.4 6.3 %collective-permute-done.33.left_ref.rest_0_ = f32[2,6,104,128]{3,2,1,0:T(8,128)} collective-permute-done((f32[2,6,104,128]{3,2,1,0:T(8,128)}, f32[2,6,104,128]{3,2,1,0:T(8,128)}, u32[]{:S(2)}, u32[]{:S(2)}) %collective-permute-start.33) | collective-permute-done | bytes 639008 | tf_op jit(solution)/shard_map/ppermute | solution.py:595
  28.7 2.5 %collective-permute-done.34.right_ref.rest_1_ = f32[2,6,104,128]{3,2,1,0:T(8,128)} collective-permute-done((f32[2,6,104,128]{3,2,1,0:T(8,128)}, f32[2,6,104,128]{3,2,1,0:T(8,128)}, u32[]{:S(2)}, u32[]{:S(2)}) %collective-permute-start.34) | collective-permute-done | bytes 639008 | tf_op jit(solution)/shard_map/ppermute | solution.py:596
  31.2 3.1 %finish.2 = (f32[2,16,96,128]{3,2,1,0:T(8,128)S(1)}, f32[1,2,16,4,128]{4,3,2,1,0:T(4,128)S(1)}, f32[16,128]{1,0:T(8,128)S(1)}) custom-call(s32[1]{0:T(128)} %bitcast.2.start_ref, f32[2,2,4,96,128]{4,3,2,1,0:T(8,128)S(1)} %copy-done.4, f32[2,16,104,128]{3,2,1,0:T(8,128)S(1)} %get-tuple-element.94.b_ref, ...), custom_call_target="tpu_custom_call", output_to_operand_aliasing={{0}: (11, {})} | custom-call | flops 8306688 | bytes 5537792 | tf_op jit(solution)/shard_map/finish/pallas_call | solution.py:543
  34.3 1.1 %copy-done = f32[2,16,96,128]{3,2,1,0:T(8,128)} copy-done((f32[2,16,96,128]{3,2,1,0:T(8,128)}, f32[2,16,96,128]{3,2,1,0:T(8,128)S(1)}, u32[]{:S(2)}) %copy-start) | copy-done | bytes 1572888
  35.4 2.0 %collective-permute-start.35 = (f32[1,2,16,4,128]{4,3,2,1,0:T(4,128)S(1)}, f32[1,2,16,4,128]{4,3,2,1,0:T(4,128)S(1)}, u32[]{:S(2)}, u32[]{:S(2)}) collective-permute-start(f32[1,2,16,4,128]{4,3,2,1,0:T(4,128)S(1)} %get-tuple-element.106), channel_id=1, source_target_pairs={{0,1},{1,0},{2,3},{3,2},{4,5},{5,4},{6,7},{7,6},{8,9},{9,8},{10,11... | collective-permute-start | bytes 196616 | tf_op jit(solution)/shard_map/ppermute | solution.py:579
  37.4 4.4 %conditional.3 = (f32[16,128]{1,0:T(8,128)}) conditional(s32[]{:T(128)} %clamp.7, f32[16,128]{1,0:T(8,128)S(1)} %get-tuple-element.108, f32[16,128]{1,0:T(8,128)S(1)} %get-tuple-element.108, f32[16,128]{1,0:T(8,128)S(1)} %get-tuple-element.108, f32[16,128]{1,0:T(8,128)S(1)} %get-tuple-element.108, ...), branch_computations={%region_16.17_spmd, %region_17.18_spmd, %region_18.19_spmd, %regio... | conditional | bytes 32816 | solution.py:511
  37.4 0.6 collective-permute-start.24
  38.0 3.8 %collective-permute-done.24 = f32[16,128]{1,0:T(8,128)} collective-permute-done((f32[16,128]{1,0:T(8,128)S(1)}, f32[16,128]{1,0:T(8,128)}, u32[]{:S(2)}, u32[]{:S(2)}) %collective-permute-start.24) | collective-permute-done | bytes 8224 | tf_op jit(solution)/shard_map/cond/branch_8_fun/ppermute | solution.py:507
  41.9 1.4 %copy-done.1 = f32[2,16,96,128]{3,2,1,0:T(8,128)S(1)} copy-done((f32[2,16,96,128]{3,2,1,0:T(8,128)S(1)}, f32[2,16,96,128]{3,2,1,0:T(8,128)}, u32[]{:S(2)}) %copy-start.1) | copy-done | bytes 1572888
  43.3 1.8 %edges.3 = (f32[2,4,104,128]{3,2,1,0:T(8,128)}, f32[2,4,104,128]{3,2,1,0:T(8,128)}) custom-call(f32[2,16,96,128]{3,2,1,0:T(8,128)S(1)} %copy-done.1, f32[2,16,104,128]{3,2,1,0:T(8,128)S(1)} %get-tuple-element.94.b_ref, f32[2,16,104,128]{3,2,1,0:T(8,128)S(1)} %get-tuple-element.95.w_ref, f32[1,2,16,4,128]{4,3,2,1,0:T(4,128)S(1)} %collective-permute-done.35.cut_ref, ...), custom_call_target="tpu_custom_call" | custom-call | flops 3833856 | bytes 2555904 | tf_op jit(solution)/shard_map/edges/pallas_call | solution.py:543
  45.1 1.5 %collective-permute-start.36 = (f32[2,4,104,128]{3,2,1,0:T(8,128)}, f32[2,4,104,128]{3,2,1,0:T(8,128)}, u32[]{:S(2)}, u32[]{:S(2)}) collective-permute-start(f32[2,4,104,128]{3,2,1,0:T(8,128)} %get-tuple-element.110), channel_id=1, source_target_pairs={{0,2},{2,4},{4,6},{6,8},{8,10},{10,12},{12,14},{14,16},{16,18},{18... | collective-permute-start | bytes 1277960 | tf_op jit(solution)/shard_map/ppermute | solution.py:595
  46.6 1.4 %copy-done.2 = f32[2,16,96,128]{3,2,1,0:T(8,128)S(1)} copy-done((f32[2,16,96,128]{3,2,1,0:T(8,128)S(1)}, f32[2,16,96,128]{3,2,1,0:T(8,128)}, u32[]{:S(2)}) %copy-start.2) | copy-done | bytes 1572888
  48.0 5.3 %interior.3 = (f32[2,16,96,128]{3,2,1,0:T(8,128)}, f32[2,3,2,2,128,128]{5,4,3,2,1,0:T(8,128)S(1)}, f32[8,8,128]{2,1,0:T(8,128)S(1)}) custom-call(f32[2,16,96,128]{3,2,1,0:T(8,128)S(1)} %copy-done.2, f32[2,16,104,128]{3,2,1,0:T(8,128)S(1)} %get-tuple-element.94.b_ref, f32[2,16,104,128]{3,2,1,0:T(8,128)S(1)} %get-tuple-element.95.w_ref, ...), custom_call_target="tpu_custom_call" | custom-call | flops 14057472 | bytes 9371648 | tf_op jit(solution)/shard_map/interior/pallas_call | solution.py:543
  53.4 2.6 %collective-permute-done.36.left_ref = f32[2,4,104,128]{3,2,1,0:T(8,128)} collective-permute-done((f32[2,4,104,128]{3,2,1,0:T(8,128)}, f32[2,4,104,128]{3,2,1,0:T(8,128)}, u32[]{:S(2)}, u32[]{:S(2)}) %collective-permute-start.36) | collective-permute-done | bytes 426016 | tf_op jit(solution)/shard_map/ppermute | solution.py:595
  56.0 4.0 %finish.3 = f32[2,16,96,128]{3,2,1,0:T(8,128)} custom-call(s32[1]{0:T(128)} %bitcast.1.start_ref, f32[2,16,96,128]{3,2,1,0:T(8,128)S(1)} %copy-done.2, f32[2,16,104,128]{3,2,1,0:T(8,128)S(1)} %get-tuple-element.94.b_ref, f32[2,16,104,128]{3,2,1,0:T(8,128)S(1)} %get-tuple-element.95.w_ref, ...), custom_call_target="tpu_custom_call", output_to_operand_aliasing={{}: (12, {})} | custom-call | flops 8306688 | bytes 5537792 | tf_op jit(solution)/shard_map/finish/pallas_call | solution.py:543
  (17 shorter events, 0.3 us)
Async XLA Ops:
  1.8 12.3 %copy-start.3 = (f32[2,2,4,96,128]{4,3,2,1,0:T(8,128)}, f32[2,2,4,96,128]{4,3,2,1,0:T(8,128)S(1)}, u32[]{:S(2)}) copy-start(f32[2,2,4,96,128]{4,3,2,1,0:T(8,128)S(1)} %get-tuple-element.92.p_ends.p_ref) | copy-start | bytes 2359300
  1.8 6.8 %collective-permute-start.32 = (f32[3,2,16,4,128]{4,3,2,1,0:T(4,128)S(1)}, f32[3,2,16,4,128]{4,3,2,1,0:T(4,128)S(1)}, u32[]{:S(2)}, u32[]{:S(2)}) collective-permute-start(f32[3,2,16,4,128]{4,3,2,1,0:T(4,128)S(1)} %get-tuple-element.93), channel_id=1, source_target_pairs={{0,1},{1,0},{2,3},{3,2},{4,5},{5,4},{6,7},{7,6},{8,9},{9,8},{10,11... | collective-permute-start | bytes 589832 | tf_op jit(solution)/shard_map/ppermute | solution.py:579
  4.7 3.7 %collective-permute-start.12 = (f32[16,128]{1,0:T(8,128)S(1)}, f32[16,128]{1,0:T(8,128)}, u32[]{:S(2)}, u32[]{:S(2)}) collective-permute-start(f32[16,128]{1,0:T(8,128)S(1)} %param.12), channel_id=1, source_target_pairs={{9,0},{24,1},{11,2},{26,3},{13,4},{28,5},{15,6},{30,7},{17,8},{0,9... | collective-permute-start | bytes 24584 | tf_op jit(solution)/shard_map/cond/branch_12_fun/ppermute | solution.py:507
  8.7 5.5 %copy-start.5 = (f32[3,2,16,4,128]{4,3,2,1,0:T(4,128)}, f32[3,2,16,4,128]{4,3,2,1,0:T(4,128)S(1)}, u32[]{:S(2)}) copy-start(f32[3,2,16,4,128]{4,3,2,1,0:T(4,128)S(1)} %collective-permute-done.32.cut_ref) | copy-start | bytes 589828
  11.3 17.4 %collective-permute-start.33 = (f32[2,6,104,128]{3,2,1,0:T(8,128)}, f32[2,6,104,128]{3,2,1,0:T(8,128)}, u32[]{:S(2)}, u32[]{:S(2)}) collective-permute-start(f32[2,6,104,128]{3,2,1,0:T(8,128)} %get-tuple-element.101), channel_id=1, source_target_pairs={{0,2},{2,4},{4,6},{6,8},{8,10},{10,12},{12,14},{14,16},{16,18},{18... | collective-permute-start | bytes 1916936 | tf_op jit(solution)/shard_map/ppermute | solution.py:595
  14.2 17.0 %collective-permute-start.34 = (f32[2,6,104,128]{3,2,1,0:T(8,128)}, f32[2,6,104,128]{3,2,1,0:T(8,128)}, u32[]{:S(2)}, u32[]{:S(2)}) collective-permute-start(f32[2,6,104,128]{3,2,1,0:T(8,128)} %get-tuple-element.102), channel_id=1, source_target_pairs={{0,30},{2,0},{4,2},{6,4},{8,6},{10,8},{12,10},{14,12},{16,14},{18,... | collective-permute-start | bytes 1916936 | tf_op jit(solution)/shard_map/ppermute | solution.py:596
  14.2 0.9 %copy-start.6 = (f32[3,2,16,4,128]{4,3,2,1,0:T(4,128)S(1)}, f32[3,2,16,4,128]{4,3,2,1,0:T(4,128)}, u32[]{:S(2)}) copy-start(f32[3,2,16,4,128]{4,3,2,1,0:T(4,128)} %copy-done.5) | copy-start | bytes 589828
  15.1 16.1 %copy-start.4 = (f32[2,2,4,96,128]{4,3,2,1,0:T(8,128)S(1)}, f32[2,2,4,96,128]{4,3,2,1,0:T(8,128)}, u32[]{:S(2)}) copy-start(f32[2,2,4,96,128]{4,3,2,1,0:T(8,128)} %copy-done.3) | copy-start | bytes 2359300
  15.1 16.1 %copy-start.7 = (f32[3,2,16,4,128]{4,3,2,1,0:T(4,128)S(1)}, f32[3,2,16,4,128]{4,3,2,1,0:T(4,128)}, u32[]{:S(2)}) copy-start(f32[3,2,16,4,128]{4,3,2,1,0:T(4,128)} %copy-done.5) | copy-start | bytes 589828
  34.3 1.1 %copy-start = (f32[2,16,96,128]{3,2,1,0:T(8,128)}, f32[2,16,96,128]{3,2,1,0:T(8,128)S(1)}, u32[]{:S(2)}) copy-start(f32[2,16,96,128]{3,2,1,0:T(8,128)S(1)} %get-tuple-element.105.p_ref) | copy-start | bytes 4718596
  35.4 6.4 %collective-permute-start.35 = (f32[1,2,16,4,128]{4,3,2,1,0:T(4,128)S(1)}, f32[1,2,16,4,128]{4,3,2,1,0:T(4,128)S(1)}, u32[]{:S(2)}, u32[]{:S(2)}) collective-permute-start(f32[1,2,16,4,128]{4,3,2,1,0:T(4,128)S(1)} %get-tuple-element.106), channel_id=1, source_target_pairs={{0,1},{1,0},{2,3},{3,2},{4,5},{5,4},{6,7},{7,6},{8,9},{9,8},{10,11... | collective-permute-start | bytes 196616 | tf_op jit(solution)/shard_map/ppermute | solution.py:579
  37.4 4.4 %collective-permute-start.24 = (f32[16,128]{1,0:T(8,128)S(1)}, f32[16,128]{1,0:T(8,128)}, u32[]{:S(2)}, u32[]{:S(2)}) collective-permute-start(f32[16,128]{1,0:T(8,128)S(1)} %param.24), channel_id=1, source_target_pairs={{17,0},{16,1},{19,2},{18,3},{21,4},{20,5},{23,6},{22,7},{25,8},{24... | collective-permute-start | bytes 24584 | tf_op jit(solution)/shard_map/cond/branch_8_fun/ppermute | solution.py:507
  41.9 1.4 %copy-start.1 = (f32[2,16,96,128]{3,2,1,0:T(8,128)S(1)}, f32[2,16,96,128]{3,2,1,0:T(8,128)}, u32[]{:S(2)}) copy-start(f32[2,16,96,128]{3,2,1,0:T(8,128)} %copy-done) | copy-start | bytes 4718596
  45.1 10.8 %collective-permute-start.36 = (f32[2,4,104,128]{3,2,1,0:T(8,128)}, f32[2,4,104,128]{3,2,1,0:T(8,128)}, u32[]{:S(2)}, u32[]{:S(2)}) collective-permute-start(f32[2,4,104,128]{3,2,1,0:T(8,128)} %get-tuple-element.110), channel_id=1, source_target_pairs={{0,2},{2,4},{4,6},{6,8},{8,10},{10,12},{12,14},{14,16},{16,18},{18... | collective-permute-start | bytes 1277960 | tf_op jit(solution)/shard_map/ppermute | solution.py:595
  46.6 9.3 %collective-permute-start.37 = (f32[2,4,104,128]{3,2,1,0:T(8,128)}, f32[2,4,104,128]{3,2,1,0:T(8,128)}, u32[]{:S(2)}, u32[]{:S(2)}) collective-permute-start(f32[2,4,104,128]{3,2,1,0:T(8,128)} %get-tuple-element.111), channel_id=1, source_target_pairs={{0,30},{2,0},{4,2},{6,4},{8,6},{10,8},{12,10},{14,12},{16,14},{18,... | collective-permute-start | bytes 1277960 | tf_op jit(solution)/shard_map/ppermute | solution.py:596
  46.6 1.4 %copy-start.2 = (f32[2,16,96,128]{3,2,1,0:T(8,128)S(1)}, f32[2,16,96,128]{3,2,1,0:T(8,128)}, u32[]{:S(2)}) copy-start(f32[2,16,96,128]{3,2,1,0:T(8,128)} %copy-done) | copy-start | bytes 4718596
